TPU v7x, 128 devices: a whole 4x4x4 slice. The times are simulated.
128 devices in a mesh: elem: 128 (over x, y, z, core).
Axes of the slice: x: 4, y: 4, z: 4, core: 2. Of those that a mesh axis runs over, the one named last changes fastest.
Arguments:
- prognostic: float32 [524288, 128], P('elem'), may hold values from -6 to 6
- metric: float32 [2, 524288], P(None, 'elem'), may hold values from 0.5 to 1
- inv_mass: float32 [524288], P('elem'), may hold values from 1 to 12.6
- viscosity: float32 [128], replicated, may hold values from 8e-05 to 0.00024
- partner: int32 [3, 524288], P(None, 'elem'), may hold values from 0 to 4096, as said below
- send_rows: int32 [256, 768], P('elem'), may hold values from 0 to 4095, as said below
- recv_rows: int32 [512, 768], P('elem'), may hold values from 0 to 4096, as said below
Outputs:
- smoothed: float32 [524288, 128], P('elem')
Inputs may be any that keep to these rules, and one draw needn't show every extreme that they name: `partner`: for each local row, the other rows of the same block that hold the same grid point (up to three), the rest 4096. `send_rows`: directions in order: 1 ahead, 1 behind along the curve, cyclically. In direction k, entry m is a local row holding the m-th grid point along the element edge shared through that direction, already holding that point's local sum. `recv_rows`: rows 2 k and 2 k + 1 of a block: the one or two local rows holding grid point m of the edge shared through direction k, else 4096.
All inputs are finite; a program needn't handle non-finite values.
Results may differ from a plain program's by a relative error of at most 0.0001.
Values sent between devices are 32-bit elements; how exact they have to be, the bound alone decides.
No kernel may reach another device: no remote copies, remote signals or barrier semaphores. Data moves between devices by JAX's collectives and lax.ppermute only.
A program may use at most 64 MiB of HBM per device.

v0:
```python
import math

import jax
import jax.numpy as jnp
import numpy as np
from jax import lax
from jax.sharding import PartitionSpec as P

SUBCYCLES = 2


def from_behind(value, axis, by):
    count = lax.axis_size(axis)
    return lax.ppermute(value, axis, [(i, (i + by) % count) for i in range(count)])


def node_tables():
    root = 1.0 / math.sqrt(5.0)
    points = [-1.0, -root, root, 1.0]
    weights = np.array([1.0, 5.0, 5.0, 1.0]) / 6.0
    products = []
    for first in range(4):
        value = 1.0
        for other in range(4):
            if other != first:
                value = value * (points[first] - points[other])
        products.append(value)
    table = []
    for first in range(4):
        line = []
        for other in range(4):
            if other == first:
                total = 0.0
                for third in range(4):
                    if third != first:
                        total = total + 1.0 / (points[first] - points[third])
                line.append(total)
            else:
                line.append(products[first] / (products[other] * (points[first] - points[other])))
        table.append(line)
    return (np.array(table), weights)


def weak_laplacian(values, metric_x, metric_y):
    derivative, weights = node_tables()
    derivative = jnp.asarray(derivative, jnp.float32)
    weight_vec = jnp.asarray(weights, jnp.float32)
    along_i = weight_vec.reshape(1, 4, 1, 1)
    along_j = weight_vec.reshape(1, 1, 4, 1)
    element_grid = values.reshape(-1, 4, 4, values.shape[-1])
    highest = lax.Precision.HIGHEST
    grad_x = jnp.einsum("ik,ekjc->eijc", derivative, element_grid, precision=highest)
    grad_y = jnp.einsum("jk,eikc->eijc", derivative, element_grid, precision=highest)
    flux_x = metric_x * grad_x * along_i
    flux_y = metric_y * grad_y * along_j
    part_x = jnp.einsum("ki,ekjc->eijc", derivative, flux_x, precision=highest) * along_j
    part_y = jnp.einsum("kj,eikc->eijc", derivative, flux_y, precision=highest) * along_i
    return -(part_x + part_y).reshape(values.shape)


def place(accumulated, payload, targets):
    accumulated = accumulated.at[targets[0]].add(payload)
    return accumulated.at[targets[1]].add(payload)


def assemble(values, partner, send_rows, recv_rows, inv_mass):
    row_count, columns = values.shape
    zero_row = jnp.zeros((1, columns), jnp.float32)
    padded = jnp.concatenate([values, zero_row], axis=0)
    local_sum = values + padded[partner[0]] + padded[partner[1]] + padded[partner[2]]
    sendable = jnp.concatenate([local_sum, zero_row], axis=0)
    arrived = jnp.zeros((row_count + 1, columns), jnp.float32)
    ahead_edge = from_behind(sendable[send_rows[0]], "elem", 1)
    arrived = place(arrived, ahead_edge, recv_rows[0:2])
    behind_edge = from_behind(sendable[send_rows[1]], "elem", -1)
    arrived = place(arrived, behind_edge, recv_rows[2:4])
    return (local_sum + arrived[:row_count]) * inv_mass[:, None]


def shards(prognostic, metric, inv_mass, viscosity, partner, send_rows, recv_rows):
    metric_x = metric[0].reshape(-1, 4, 4, 1)
    metric_y = metric[1].reshape(-1, 4, 4, 1)
    fields = prognostic
    for subcycle in range(SUBCYCLES):
        first_pass = assemble(
            weak_laplacian(fields, metric_x, metric_y), partner, send_rows, recv_rows, inv_mass
        )
        second_pass = assemble(
            weak_laplacian(first_pass, metric_x, metric_y), partner, send_rows, recv_rows, inv_mass
        )
        fields = fields - viscosity[None, :] * second_pass
    return fields


def solution(mesh):
    placed = (
        P("elem", None),
        P(None, "elem"),
        P("elem"),
        P(),
        P(None, "elem"),
        P("elem", None),
        P("elem", None),
    )
    return jax.shard_map(
        shards, mesh=mesh, in_specs=placed, out_specs=P("elem", None), check_vma=False
    )
```

profile of v0, /device:TPU:0, one launch (start us, length us, event | category | flops | bytes accessed | tf_op | source)
XLA Modules:
  0.0 466.6 jit_solution(9138598840753866390)
XLA Ops:
  0.0 6.9 %fusion.78 = f32[4,256,4,128]{3,0,2,1:T(4,128)} fusion(f32[4,4,1,1]{1,0,3,2:T(4,128)} %constant.33, f32[256,4,4,128]{3,2,1,0:T(4,128)} %bitcast.137), kind=kOutput, calls=%fused_computation.150 | convolution fusion | flops 25165824 | bytes 4194368 | tf_op jit(solution)/shard_map/jk,eikc->eijc/dot_general | solution.py:53
  29.0 14.2 %gather_fusion.2 = f32[4096,128]{1,0:T(8,128)} fusion(f32[4097,128]{1,0:T(8,128)S(1)} %concatenate.24, s32[4096]{0:T(1024)S(1)} %broadcast_clamp_fusion), kind=kCustom, calls=%fused_computation.2 | custom fusion | bytes 4210688 | tf_op jit(solution)/shard_map/gather | solution.py:70
  43.2 14.1 %gather_fusion.1 = f32[4096,128]{1,0:T(8,128)} fusion(f32[4097,128]{1,0:T(8,128)S(1)} %concatenate.24, s32[4096]{0:T(1024)S(1)} %broadcast_clamp_fusion.1), kind=kCustom, calls=%fused_computation.1 | custom fusion | bytes 4210688 | tf_op jit(solution)/shard_map/gather | solution.py:70
  57.3 14.1 %gather_fusion = f32[4096,128]{1,0:T(8,128)} fusion(f32[4097,128]{1,0:T(8,128)S(1)} %concatenate.24, s32[4096]{0:T(1024)S(1)} %broadcast_clamp_fusion.2), kind=kCustom, calls=%fused_computation | custom fusion | bytes 4210688 | tf_op jit(solution)/shard_map/gather | solution.py:70
  81.2 8.6 %collective-permute-start.1 = (f32[768,128]{1,0:T(8,128)}, f32[768,128]{1,0:T(8,128)S(1)}, u32[]{:S(2)}, u32[]{:S(2)}) collective-permute-start(f32[768,128]{1,0:T(8,128)} %gather_fusion.4), channel_id=1, source_target_pairs={{0,127},{1,0},{2,1},{3,2},{4,3},{5,4},{6,5},{7,6},{8,7},{9,8},{10,... | collective-permute-start | bytes 1179656 | tf_op jit(solution)/shard_map/ppermute | solution.py:14
  92.9 6.9 %scatter_custom_fusion = f32[4097,128]{1,0:T(8,128)S(1)} fusion(s32[768]{0:T(1024)S(1)} %get-tuple-element.9, f32[768,128]{1,0:T(8,128)} %collective-permute-done, f32[]{:T(128)} %constant.5.clone.1), kind=kCustom, calls=%fused_computation.110 | custom fusion | flops 98304 | bytes 2098176 | tf_op jit(solution)/shard_map/scatter-add | solution.py:62
  99.8 7.1 %scatter_fusion = f32[4097,128]{1,0:T(8,128)S(1)} fusion(f32[4097,128]{1,0:T(8,128)S(1)} %scatter_custom_fusion, s32[768]{0:T(1024)S(1)} %get-tuple-element.8, f32[768,128]{1,0:T(8,128)} %collective-permute-done), kind=kCustom, calls=%fused_computation.21 | custom fusion | flops 98304 | bytes 1182720 | tf_op jit(solution)/shard_map/scatter-add | solution.py:63
  107.0 6.7 %scatter_fusion.1 = f32[4097,128]{1,0:T(8,128)S(1)} fusion(f32[4097,128]{1,0:T(8,128)S(1)} %scatter_fusion, s32[768]{0:T(1024)S(1)} %get-tuple-element.10, f32[768,128]{1,0:T(8,128)S(1)} %collective-permute-done.1), kind=kCustom, calls=%fused_computation.22 | custom fusion | flops 98304 | bytes 1182720 | tf_op jit(solution)/shard_map/scatter-add | solution.py:62
  113.7 6.9 %scatter_fusion.2 = f32[4097,128]{1,0:T(8,128)S(1)} fusion(f32[4097,128]{1,0:T(8,128)S(1)} %scatter_fusion.1, s32[768]{0:T(1024)S(1)} %get-tuple-element.7, f32[768,128]{1,0:T(8,128)S(1)} %collective-permute-done.1), kind=kCustom, calls=%fused_computation.23 | custom fusion | flops 98304 | bytes 1182720 | tf_op jit(solution)/shard_map/scatter-add | solution.py:63
  144.1 14.2 %gather_fusion.7 = f32[4096,128]{1,0:T(8,128)} fusion(f32[4097,128]{1,0:T(8,128)S(1)} %concatenate.26, s32[4096]{0:T(1024)S(1)} %broadcast_clamp_fusion), kind=kCustom, calls=%fused_computation.7 | custom fusion | bytes 4210688 | tf_op jit(solution)/shard_map/gather | solution.py:70
  158.3 14.1 %gather_fusion.6 = f32[4096,128]{1,0:T(8,128)} fusion(f32[4097,128]{1,0:T(8,128)S(1)} %concatenate.26, s32[4096]{0:T(1024)S(1)} %broadcast_clamp_fusion.1), kind=kCustom, calls=%fused_computation.6 | custom fusion | bytes 4210688 | tf_op jit(solution)/shard_map/gather | solution.py:70
  172.4 14.1 %gather_fusion.5 = f32[4096,128]{1,0:T(8,128)} fusion(f32[4097,128]{1,0:T(8,128)S(1)} %concatenate.26, s32[4096]{0:T(1024)S(1)} %broadcast_clamp_fusion.2), kind=kCustom, calls=%fused_computation.5 | custom fusion | bytes 4210688 | tf_op jit(solution)/shard_map/gather | solution.py:70
  196.3 7.4 %collective-permute-start.3 = (f32[768,128]{1,0:T(8,128)}, f32[768,128]{1,0:T(8,128)S(1)}, u32[]{:S(2)}, u32[]{:S(2)}) collective-permute-start(f32[768,128]{1,0:T(8,128)} %gather_fusion.9), channel_id=1, source_target_pairs={{0,127},{1,0},{2,1},{3,2},{4,3},{5,4},{6,5},{7,6},{8,7},{9,8},{10,... | collective-permute-start | bytes 1179656 | tf_op jit(solution)/shard_map/ppermute | solution.py:14
  207.0 6.9 %scatter_custom_fusion.4 = f32[4097,128]{1,0:T(8,128)S(1)} fusion(s32[768]{0:T(1024)S(1)} %get-tuple-element.9, f32[768,128]{1,0:T(8,128)} %collective-permute-done.2, f32[]{:T(128)} %constant.5.clone.1), kind=kCustom, calls=%fused_computation.108 | custom fusion | flops 98304 | bytes 2098176 | tf_op jit(solution)/shard_map/scatter-add | solution.py:62
  213.9 7.1 %scatter_fusion.3 = f32[4097,128]{1,0:T(8,128)S(1)} fusion(f32[4097,128]{1,0:T(8,128)S(1)} %scatter_custom_fusion.4, s32[768]{0:T(1024)S(1)} %get-tuple-element.8, f32[768,128]{1,0:T(8,128)} %collective-permute-done.2), kind=kCustom, calls=%fused_computation.25 | custom fusion | flops 98304 | bytes 1182720 | tf_op jit(solution)/shard_map/scatter-add | solution.py:63
  221.0 6.7 %scatter_fusion.4 = f32[4097,128]{1,0:T(8,128)S(1)} fusion(f32[4097,128]{1,0:T(8,128)S(1)} %scatter_fusion.3, s32[768]{0:T(1024)S(1)} %get-tuple-element.10, f32[768,128]{1,0:T(8,128)S(1)} %collective-permute-done.3), kind=kCustom, calls=%fused_computation.26 | custom fusion | flops 98304 | bytes 1182720 | tf_op jit(solution)/shard_map/scatter-add | solution.py:62
  227.8 7.2 %scatter_fusion.5 = f32[4097,128]{1,0:T(8,128)S(1)} fusion(f32[4097,128]{1,0:T(8,128)S(1)} %scatter_fusion.4, s32[768]{0:T(1024)S(1)} %get-tuple-element.7, f32[768,128]{1,0:T(8,128)S(1)} %collective-permute-done.3), kind=kCustom, calls=%fused_computation.27 | custom fusion | flops 98304 | bytes 1182720 | tf_op jit(solution)/shard_map/scatter-add | solution.py:63
  259.1 14.1 %gather_fusion.12 = f32[4096,128]{1,0:T(8,128)} fusion(f32[4097,128]{1,0:T(8,128)S(1)} %concatenate.28, s32[4096]{0:T(1024)S(1)} %broadcast_clamp_fusion), kind=kCustom, calls=%fused_computation.12 | custom fusion | bytes 4210688 | tf_op jit(solution)/shard_map/gather | solution.py:70
  273.2 14.1 %gather_fusion.11 = f32[4096,128]{1,0:T(8,128)} fusion(f32[4097,128]{1,0:T(8,128)S(1)} %concatenate.28, s32[4096]{0:T(1024)S(1)} %broadcast_clamp_fusion.1), kind=kCustom, calls=%fused_computation.11 | custom fusion | bytes 4210688 | tf_op jit(solution)/shard_map/gather | solution.py:70
  287.3 14.1 %gather_fusion.10 = f32[4096,128]{1,0:T(8,128)} fusion(f32[4097,128]{1,0:T(8,128)S(1)} %concatenate.28, s32[4096]{0:T(1024)S(1)} %broadcast_clamp_fusion.2), kind=kCustom, calls=%fused_computation.10 | custom fusion | bytes 4210688 | tf_op jit(solution)/shard_map/gather | solution.py:70
  311.2 7.3 %collective-permute-start.5 = (f32[768,128]{1,0:T(8,128)}, f32[768,128]{1,0:T(8,128)S(1)}, u32[]{:S(2)}, u32[]{:S(2)}) collective-permute-start(f32[768,128]{1,0:T(8,128)} %gather_fusion.14), channel_id=1, source_target_pairs={{0,127},{1,0},{2,1},{3,2},{4,3},{5,4},{6,5},{7,6},{8,7},{9,8},{10,... | collective-permute-start | bytes 1179656 | tf_op jit(solution)/shard_map/ppermute | solution.py:14
  321.9 6.9 %scatter_custom_fusion.8 = f32[4097,128]{1,0:T(8,128)S(1)} fusion(s32[768]{0:T(1024)S(1)} %get-tuple-element.9, f32[768,128]{1,0:T(8,128)} %collective-permute-done.4, f32[]{:T(128)} %constant.5.clone.1), kind=kCustom, calls=%fused_computation.106 | custom fusion | flops 98304 | bytes 2098176 | tf_op jit(solution)/shard_map/scatter-add | solution.py:62
  328.8 7.1 %scatter_fusion.6 = f32[4097,128]{1,0:T(8,128)S(1)} fusion(f32[4097,128]{1,0:T(8,128)S(1)} %scatter_custom_fusion.8, s32[768]{0:T(1024)S(1)} %get-tuple-element.8, f32[768,128]{1,0:T(8,128)} %collective-permute-done.4), kind=kCustom, calls=%fused_computation.29 | custom fusion | flops 98304 | bytes 1182720 | tf_op jit(solution)/shard_map/scatter-add | solution.py:63
  336.0 6.7 %scatter_fusion.7 = f32[4097,128]{1,0:T(8,128)S(1)} fusion(f32[4097,128]{1,0:T(8,128)S(1)} %scatter_fusion.6, s32[768]{0:T(1024)S(1)} %get-tuple-element.10, f32[768,128]{1,0:T(8,128)S(1)} %collective-permute-done.5), kind=kCustom, calls=%fused_computation.30 | custom fusion | flops 98304 | bytes 1182720 | tf_op jit(solution)/shard_map/scatter-add | solution.py:62
  342.7 7.0 %scatter_fusion.8 = f32[4097,128]{1,0:T(8,128)S(1)} fusion(f32[4097,128]{1,0:T(8,128)S(1)} %scatter_fusion.7, s32[768]{0:T(1024)S(1)} %get-tuple-element.7, f32[768,128]{1,0:T(8,128)S(1)} %collective-permute-done.5), kind=kCustom, calls=%fused_computation.31 | custom fusion | flops 98304 | bytes 1182720 | tf_op jit(solution)/shard_map/scatter-add | solution.py:63
  373.2 14.1 %gather_fusion.17 = f32[4096,128]{1,0:T(8,128)} fusion(f32[4097,128]{1,0:T(8,128)S(1)} %concatenate.30, s32[4096]{0:T(1024)S(1)} %broadcast_clamp_fusion), kind=kCustom, calls=%fused_computation.17 | custom fusion | bytes 4210688 | tf_op jit(solution)/shard_map/gather | solution.py:70
  387.3 14.1 %gather_fusion.16 = f32[4096,128]{1,0:T(8,128)} fusion(f32[4097,128]{1,0:T(8,128)S(1)} %concatenate.30, s32[4096]{0:T(1024)S(1)} %broadcast_clamp_fusion.1), kind=kCustom, calls=%fused_computation.16 | custom fusion | bytes 4210688 | tf_op jit(solution)/shard_map/gather | solution.py:70
  401.4 14.1 %gather_fusion.15 = f32[4096,128]{1,0:T(8,128)} fusion(f32[4097,128]{1,0:T(8,128)S(1)} %concatenate.30, s32[4096]{0:T(1024)S(1)} %broadcast_clamp_fusion.2), kind=kCustom, calls=%fused_computation.15 | custom fusion | bytes 4210688 | tf_op jit(solution)/shard_map/gather | solution.py:70
  424.6 7.5 %collective-permute-start.7 = (f32[768,128]{1,0:T(8,128)S(1)}, f32[768,128]{1,0:T(8,128)S(1)}, u32[]{:S(2)}, u32[]{:S(2)}) collective-permute-start(f32[768,128]{1,0:T(8,128)S(1)} %gather_fusion.19), channel_id=1, source_target_pairs={{0,127},{1,0},{2,1},{3,2},{4,3},{5,4},{6,5},{7,6},{8,7},{9,8},{10,... | collective-permute-start | bytes 1179656 | tf_op jit(solution)/shard_map/ppermute | solution.py:14
  442.4 6.7 %scatter_fusion.9 = f32[4097,128]{1,0:T(8,128)S(1)} fusion(f32[4097,128]{1,0:T(8,128)S(1)} %scatter_custom_fusion.12, s32[768]{0:T(1024)S(1)} %get-tuple-element.8, f32[768,128]{1,0:T(8,128)S(1)} %collective-permute-done.6), kind=kCustom, calls=%fused_computation.33 | custom fusion | flops 98304 | bytes 1182720 | tf_op jit(solution)/shard_map/scatter-add | solution.py:63
  449.1 6.7 %scatter_fusion.10 = f32[4097,128]{1,0:T(8,128)S(1)} fusion(f32[4097,128]{1,0:T(8,128)S(1)} %scatter_fusion.9, s32[768]{0:T(1024)S(1)} %get-tuple-element.10, f32[768,128]{1,0:T(8,128)S(1)} %collective-permute-done.7), kind=kCustom, calls=%fused_computation.34 | custom fusion | flops 98304 | bytes 1182720 | tf_op jit(solution)/shard_map/scatter-add | solution.py:62
  455.9 6.7 %scatter_fusion.11 = f32[4097,128]{1,0:T(8,128)S(1)} fusion(f32[4097,128]{1,0:T(8,128)S(1)} %scatter_fusion.10, s32[768]{0:T(1024)S(1)} %get-tuple-element.7, f32[768,128]{1,0:T(8,128)S(1)} %collective-permute-done.7), kind=kCustom, calls=%fused_computation.35 | custom fusion | flops 98304 | bytes 1182720 | tf_op jit(solution)/shard_map/scatter-add | solution.py:63
  (116 shorter events, 154.9 us)
Async XLA Ops:
  0.0 6.9 %copy-start.9 = (f32[4096,128]{1,0:T(8,128)S(1)}, f32[4096,128]{1,0:T(8,128)}, u32[]{:S(2)}) copy-start(f32[4096,128]{1,0:T(8,128)} %param.15) | copy-start | bytes 6291460
  0.0 6.9 %copy-start.15 = (f32[4,4,1,1]{1,0,3,2:T(4,128)S(1)}, f32[4,4,1,1]{1,0,3,2:T(4,128)}, u32[]{:S(2)}) copy-start(f32[4,4,1,1]{1,0,3,2:T(4,128)} %constant.33) | copy-start | bytes 196
  6.9 4.1 copy-start.20
  6.9 4.1 copy-start.17
  6.9 4.2 copy-start.16
  10.9 3.3 copy-start.18
  14.3 5.7 %copy-start.10 = (f32[256,4,4]{2,1,0:T(4,128)}, f32[256,4,4]{2,1,0:T(4,128)S(1)}, u32[]{:S(2)}) copy-start(f32[256,4,4]{2,1,0:T(4,128)S(1)} %mul.265) | copy-start | bytes 49156
  27.5 1.3 copy-start.6
  75.2 1.3 copy-start.1
  78.9 10.9 %copy-start.19 = (s32[4,768]{1,0:T(4,128)S(1)}, s32[4,768]{1,0:T(4,128)}, u32[]{:S(2)}) copy-start(s32[4,768]{1,0:T(4,128)} %param.21) | copy-start | bytes 36868
  78.9 14.0 %collective-permute-start = (f32[768,128]{1,0:T(8,128)}, f32[768,128]{1,0:T(8,128)}, u32[]{:S(2)}, u32[]{:S(2)}) collective-permute-start(f32[768,128]{1,0:T(8,128)} %gather_fusion.3), channel_id=1, source_target_pairs={{0,1},{1,2},{2,3},{3,4},{4,5},{5,6},{6,7},{7,8},{8,9},{9,10},{10,1... | collective-permute-start | bytes 1179656 | tf_op jit(solution)/shard_map/ppermute | solution.py:14
  81.2 25.8 %collective-permute-start.1 = (f32[768,128]{1,0:T(8,128)}, f32[768,128]{1,0:T(8,128)S(1)}, u32[]{:S(2)}, u32[]{:S(2)}) collective-permute-start(f32[768,128]{1,0:T(8,128)} %gather_fusion.4), channel_id=1, source_target_pairs={{0,127},{1,0},{2,1},{3,2},{4,3},{5,4},{6,5},{7,6},{8,7},{9,8},{10,... | collective-permute-start | bytes 1179656 | tf_op jit(solution)/shard_map/ppermute | solution.py:14
  113.7 6.9 %copy-start.14 = (f32[4096]{0:T(1024)S(1)}, f32[4096]{0:T(1024)}, u32[]{:S(2)}) copy-start(f32[4096]{0:T(1024)} %param.17) | copy-start | bytes 49156
  130.3 4.8 %copy-start.11 = (f32[256,4,4]{2,1,0:T(4,128)S(1)}, f32[256,4,4]{2,1,0:T(4,128)}, u32[]{:S(2)}) copy-start(f32[256,4,4]{2,1,0:T(4,128)} %copy-done.10) | copy-start | bytes 49156
  142.7 1.3 copy-start.7
  190.3 1.3 copy-start.4
  194.0 12.9 %collective-permute-start.2 = (f32[768,128]{1,0:T(8,128)}, f32[768,128]{1,0:T(8,128)}, u32[]{:S(2)}, u32[]{:S(2)}) collective-permute-start(f32[768,128]{1,0:T(8,128)} %gather_fusion.8), channel_id=1, source_target_pairs={{0,1},{1,2},{2,3},{3,4},{4,5},{5,6},{6,7},{7,8},{8,9},{9,10},{10,1... | collective-permute-start | bytes 1179656 | tf_op jit(solution)/shard_map/ppermute | solution.py:14
  196.3 24.8 %collective-permute-start.3 = (f32[768,128]{1,0:T(8,128)}, f32[768,128]{1,0:T(8,128)S(1)}, u32[]{:S(2)}, u32[]{:S(2)}) collective-permute-start(f32[768,128]{1,0:T(8,128)} %gather_fusion.9), channel_id=1, source_target_pairs={{0,127},{1,0},{2,1},{3,2},{4,3},{5,4},{6,5},{7,6},{8,7},{9,8},{10,... | collective-permute-start | bytes 1179656 | tf_op jit(solution)/shard_map/ppermute | solution.py:14
  227.8 7.2 %copy-start.21 = (f32[128]{0:T(128)S(1)}, f32[128]{0:T(128)}, u32[]{:S(2)}) copy-start(f32[128]{0:T(128)} %param.18) | copy-start | bytes 1540
  237.5 3.9 copy-start
  241.4 3.9 copy-start.12
  257.6 1.3 copy-start.8
  305.2 1.4 copy-start.2
  309.0 12.9 %collective-permute-start.4 = (f32[768,128]{1,0:T(8,128)}, f32[768,128]{1,0:T(8,128)}, u32[]{:S(2)}, u32[]{:S(2)}) collective-permute-start(f32[768,128]{1,0:T(8,128)} %gather_fusion.13), channel_id=1, source_target_pairs={{0,1},{1,2},{2,3},{3,4},{4,5},{5,6},{6,7},{7,8},{8,9},{9,10},{10,1... | collective-permute-start | bytes 1179656 | tf_op jit(solution)/shard_map/ppermute | solution.py:14
  311.2 24.8 %collective-permute-start.5 = (f32[768,128]{1,0:T(8,128)}, f32[768,128]{1,0:T(8,128)S(1)}, u32[]{:S(2)}, u32[]{:S(2)}) collective-permute-start(f32[768,128]{1,0:T(8,128)} %gather_fusion.14), channel_id=1, source_target_pairs={{0,127},{1,0},{2,1},{3,2},{4,3},{5,4},{6,5},{7,6},{8,7},{9,8},{10,... | collective-permute-start | bytes 1179656 | tf_op jit(solution)/shard_map/ppermute | solution.py:14
  355.5 3.9 copy-start.13
  371.7 1.3 copy-start.5
  419.3 1.4 copy-start.3
  423.0 12.8 %collective-permute-start.6 = (f32[768,128]{1,0:T(8,128)}, f32[768,128]{1,0:T(8,128)S(1)}, u32[]{:S(2)}, u32[]{:S(2)}) collective-permute-start(f32[768,128]{1,0:T(8,128)} %gather_fusion.18), channel_id=1, source_target_pairs={{0,1},{1,2},{2,3},{3,4},{4,5},{5,6},{6,7},{7,8},{8,9},{9,10},{10,1... | collective-permute-start | bytes 1179656 | tf_op jit(solution)/shard_map/ppermute | solution.py:14
  424.6 24.5 %collective-permute-start.7 = (f32[768,128]{1,0:T(8,128)S(1)}, f32[768,128]{1,0:T(8,128)S(1)}, u32[]{:S(2)}, u32[]{:S(2)}) collective-permute-start(f32[768,128]{1,0:T(8,128)S(1)} %gather_fusion.19), channel_id=1, source_target_pairs={{0,127},{1,0},{2,1},{3,2},{4,3},{5,4},{6,5},{7,6},{8,7},{9,8},{10,... | collective-permute-start | bytes 1179656 | tf_op jit(solution)/shard_map/ppermute | solution.py:14
where the time goes:
time: 470 us; the launch traced here: 467 us
  local copies, waits for them, and re-layouts  207 us (44%)
  other arithmetic  141 us (30%)
  matrix products  73.2 us (16%)
  starting transfers between devices  30.8 us (7%)
  waiting for transfers between devices  13.5 us (3%)
    gather x4, local copies, waits for them, and re-layouts, assemble(): padded[partner[2]]  56.6 us
    gather x4, local copies, waits for them, and re-layouts, assemble(): padded[partner[1]]  56.3 us
    gather x4, local copies, waits for them, and re-layouts, assemble(): padded[partner[0]]  56.3 us
    scatter-add x8, other arithmetic, place(): return accumulated.at[targets[1]].add(payload)  56 us
    scatter-add x8, other arithmetic, place(): accumulated = accumulated.at[targets[0]].add(payload)  54.2 us
    ppermute x8, starting transfers between devices, from_behind(): lax.ppermute(value, axis, [(i, (i + by) % count) for i in range(count)])  30.8 us
    dot_general x4, matrix products, weak_laplacian(): jnp.einsum('kj,eikc->eijc', derivative, flux_y, precision=highest) * along_i  20.1 us
    dot_general x4, matrix products, weak_laplacian(): jnp.einsum('ki,ekjc->eijc', derivative, flux_x, precision=highest) * along_j  19.1 us
  transfers between devices with their start and end apart: 8, of which 4 were waited for; matrix products, arithmetic and copies ran while one was open for 14% of the time, Pallas kernels for 0%

commit v1 on v0

v1 whole, which is shorter than its diff:
```python
import math

import jax
import jax.numpy as jnp
import numpy as np
from jax import lax
from jax.experimental import pallas as pl
from jax.experimental.pallas import tpu as pltpu
from jax.sharding import PartitionSpec as P

SUBCYCLES = 2
ELEMS = 256
ROWS = 16 * ELEMS
COLS = 128
EDGE = 3 * ELEMS
SEGS = 8
STEPS = ELEMS // SEGS
NONE = ROWS
VMEM_LIMIT = 24 * 2**20
HIGH = lax.Precision.HIGHEST


def node_tables():
    root = 1.0 / math.sqrt(5.0)
    points = [-1.0, -root, root, 1.0]
    weights = np.array([1.0, 5.0, 5.0, 1.0]) / 6.0
    products = []
    for first in range(4):
        value = 1.0
        for other in range(4):
            if other != first:
                value = value * (points[first] - points[other])
        products.append(value)
    table = []
    for first in range(4):
        line = []
        for other in range(4):
            if other == first:
                total = 0.0
                for third in range(4):
                    if third != first:
                        total = total + 1.0 / (points[first] - points[third])
                line.append(total)
            else:
                line.append(products[first] / (products[other] * (points[first] - points[other])))
        table.append(line)
    return (np.array(table), weights)


D, WEIGHTS = node_tables()


def gradient(v):
    o0, o1 = v[0] - v[3], v[1] - v[2]
    h = (v[0] + v[3]) - (v[1] + v[2])
    q0 = float(0.5 * (D[0, 0] + D[0, 3])) * h
    q1 = float(0.5 * (D[1, 0] + D[1, 3])) * h
    s0 = float(0.5 * (D[0, 0] - D[0, 3])) * o0 + float(0.5 * (D[0, 1] - D[0, 2])) * o1
    s1 = float(0.5 * (D[1, 0] - D[1, 3])) * o0 + float(0.5 * (D[1, 1] - D[1, 2])) * o1
    return [s0 + q0, s1 + q1, s1 - q1, s0 - q0]


def divergence(f):
    g0, g1 = f[0] - f[3], f[1] - f[2]
    t0, t1 = f[0] + f[3], f[1] + f[2]
    z = float(0.5 * (D[0, 0] + D[0, 3])) * g0 + float(0.5 * (D[1, 0] + D[1, 3])) * g1
    r0 = float(0.5 * (D[0, 0] - D[0, 3])) * t0 + float(0.5 * (D[1, 0] - D[1, 3])) * t1
    r1 = float(0.5 * (D[0, 1] - D[0, 2])) * t0 + float(0.5 * (D[1, 1] - D[1, 2])) * t1
    return [z + r0, r1 - z, -z - r1, z - r0]


def weak(x, mx, my):
    out = [None] * 16
    for j in range(4):
        g = gradient([x[4 * i + j] for i in range(4)])
        f = divergence([mx(4 * i + j) * g[i] for i in range(4)])
        for i in range(4):
            out[4 * i + j] = f[i]
    for i in range(4):
        g = gradient([x[4 * i + j] for j in range(4)])
        f = divergence([my(4 * i + j) * g[j] for j in range(4)])
        for j in range(4):
            out[4 * i + j] = out[4 * i + j] + f[j]
    return out


def plane(ref, q, t):
    return ref[pl.ds(pl.multiple_of(q * ELEMS + t * SEGS, SEGS), SEGS), :]


def set_plane(ref, q, t, value):
    ref[pl.ds(pl.multiple_of(q * ELEMS + t * SEGS, SEGS), SEGS), :] = value


def following(ref, q, t):
    last = t == STEPS - 1
    value = plane(ref, q, jnp.where(last, 0, t + 1))
    return jnp.where(last, pltpu.roll(value, SEGS - 1, 0), value)


def place_of(y):
    return lax.rem(y, STEPS) * SEGS + lax.div(y, STEPS)


def state_row(r):
    return lax.rem(r, 16) * ELEMS + place_of(lax.div(r, 16))


def wire_row(m):
    return lax.rem(m, 3) * ELEMS + place_of(lax.div(m, 3))


def one(ref, row):
    return ref[pl.ds(row, 1), :]


def ring_sums(s_ref):
    for i in range(4):
        for t in range(STEPS):
            upper = plane(s_ref, 4 * i, (t + 1) % STEPS)
            if t == STEPS - 1:
                upper = first
                lower = plane(s_ref, 4 * i + 3, t)
                total = lower + pltpu.roll(upper, SEGS - 1, 0)
                set_plane(s_ref, 4 * i + 3, t, total)
                set_plane(s_ref, 4 * i, 0, pltpu.roll(total, 1, 0))
            else:
                if t == 0:
                    first = plane(s_ref, 4 * i, 0)
                total = plane(s_ref, 4 * i + 3, t) + upper
                set_plane(s_ref, 4 * i + 3, t, total)
                set_plane(s_ref, 4 * i, t + 1, total)


def edge_messages(s_ref, behind_ref, ahead_ref):
    behind_ref[...] = s_ref[0:EDGE, :]
    ahead_ref[...] = s_ref[12 * ELEMS:15 * ELEMS, :]


def general_sums(v_ref, s_ref, partner_any, partner_s):
    pltpu.sync_copy(partner_any, partner_s)

    def body(r, carry):
        total = one(v_ref, state_row(r))
        for k in range(3):
            other = partner_s[k, r]
            found = one(v_ref, state_row(jnp.minimum(other, ROWS - 1)))
            total = total + jnp.where(other < NONE, found, 0.0)
        s_ref[pl.ds(state_row(r), 1), :] = total
        return carry

    lax.fori_loop(0, ROWS, body, 0)


def general_messages(s_ref, behind_ref, ahead_ref, send_any, send_s):
    pltpu.sync_copy(send_any, send_s)

    def body(m, carry):
        ahead_ref[pl.ds(wire_row(m), 1), :] = one(s_ref, state_row(send_s[0, m]))
        behind_ref[pl.ds(wire_row(m), 1), :] = one(s_ref, state_row(send_s[1, m]))
        return carry

    lax.fori_loop(0, EDGE, body, 0)


def general_receive(total_ref, left_ref, right_ref, recv_any, recv_s):
    pltpu.sync_copy(recv_any, recv_s)

    def body(m, carry):
        for k, arrived in ((0, left_ref), (1, right_ref)):
            for c in range(2):
                target = recv_s[2 * k + c, m]

                @pl.when(target < NONE)
                def _():
                    row = pl.ds(state_row(target), 1)
                    total_ref[row, :] = total_ref[row, :] + one(arrived, wire_row(m))
        return carry

    lax.fori_loop(0, EDGE, body, 0)


def finish(ok, v_ref, s_ref, behind_ref, ahead_ref, partner_any, send_any, partner_s, send_s):
    @pl.when(ok)
    def _():
        ring_sums(s_ref)
        edge_messages(s_ref, behind_ref, ahead_ref)

    @pl.when(jnp.logical_not(ok))
    def _():
        general_sums(v_ref, s_ref, partner_any, partner_s)
        general_messages(s_ref, behind_ref, ahead_ref, send_any, send_s)


def iota(shape, axis):
    return lax.broadcasted_iota(jnp.int32, shape, axis)


def count(bad):
    return jnp.sum(jnp.where(bad, 1.0, 0.0))


def by_element(chunks):
    own = (iota((16, 256), 1) >> 4) == iota((16, 256), 0)
    return jnp.concatenate([jnp.where(own, jnp.broadcast_to(c, (16, 256)), 0.0) for c in chunks], axis=0)


def first_kernel(prog, metric, inv_mass, send_s, send_v, recv_v, partner_v, partner_any, send_any,
                 u_ref, s_ref, mx_ref, my_ref, im_ref, behind_ref, ahead_ref, flag_ref,
                 raw, v_ref, table, partner_s, send_g, sem):
    load = pltpu.make_async_copy(prog, raw, sem)
    load.start()

    send = send_v[...]
    order_row = send[0:1, :] >> 4
    place = iota((ELEMS, 1), 0)
    ring = (place & 7) * STEPS + (place >> 3)
    picked = iota((ELEMS, EDGE), 1) == 3 * ring + 1
    order = jnp.sum(jnp.where(picked, order_row.astype(jnp.float32), 0.0), axis=1, keepdims=True)
    lane_e = iota((ELEMS, ELEMS), 1)
    hot = (lane_e.astype(jnp.float32) == order).astype(jnp.float32)
    bad = count(jnp.sum(hot, axis=0, keepdims=True) != 1.0)

    partner = partner_v[...]
    least = jnp.minimum(jnp.minimum(partner[0:1], partner[1:2]), partner[2:3]).astype(jnp.float32)
    added = (partner[0:1] + partner[1:2] + partner[2:3]).astype(jnp.float32)
    mass = inv_mass[...]
    groups = []
    for k in range(2):
        row = metric[k:k + 1, :]
        groups.append([row[:, 256 * c:256 * c + 256] for c in range(16)])
    groups.append([jnp.concatenate([mass[2 * c:2 * c + 1, :], mass[2 * c + 1:2 * c + 2, :]], axis=1) for c in range(16)])
    for row in (least, added):
        groups.append([row[:, 256 * c:256 * c + 256] for c in range(16)])
    point = iota((256, 128), 0) & 15
    lane = iota((256, 128), 1)
    raw_table = jnp.zeros((ELEMS, 128), jnp.float32)
    for g, chunks in enumerate(groups):
        chosen = (lane == point + 16 * g).astype(jnp.float32)
        raw_table = raw_table + jnp.dot(by_element(chunks), chosen, precision=HIGH, preferred_element_type=jnp.float32)
    ordered = jnp.dot(hot, raw_table, precision=HIGH, preferred_element_type=jnp.float32)

    last = order[(STEPS - 1) * SEGS:, :]
    before = jnp.concatenate([pltpu.roll(jnp.broadcast_to(last, (SEGS, 128)), 1, 0)[:, 0:1], order[:-SEGS, :]], axis=0)
    after = jnp.concatenate([order[SEGS:, :], pltpu.roll(jnp.broadcast_to(order[:SEGS, :], (SEGS, 128)), SEGS - 1, 0)[:, 0:1]], axis=0)
    point_i = (lane >> 2) & 3
    point_j = lane & 3
    group = lane >> 4
    offset = (4 * point_i).astype(jnp.float32)
    expect = jnp.where(point_j == 0, 16.0 * before + offset + 3.0,
                       jnp.where(point_j == 3, 16.0 * after + offset, float(NONE)))
    expect = expect + jnp.where(group == 4, float(2 * NONE), 0.0)
    bad = bad + count(((group == 3) | (group == 4)) & (ordered != expect))

    m = iota((1, EDGE), 1)
    p = m - 3 * ((m * 43691) >> 17)
    wide = jnp.broadcast_to(order_row, (8, EDGE))
    up1 = pltpu.roll(wide, EDGE - 1, 1)[0:1]
    down1 = pltpu.roll(wide, 1, 1)[0:1]
    down2 = pltpu.roll(wide, 2, 1)[0:1]
    own = 16 * jnp.where(p == 0, up1, jnp.where(p == 1, order_row, down1)) + p
    other = jnp.where(p == 0, 16 * down2 + 3, NONE)
    recv = recv_v[...]
    for k, shift in ((0, 12), (1, 0)):
        named = send[k:k + 1, :] - shift
        bad = bad + count((named != own) & ((p != 0) | (named != other)))
        a, b = recv[2 * (1 - k):2 * (1 - k) + 1, :], recv[2 * (1 - k) + 1:2 * (1 - k) + 2, :]
        want = jnp.where(p == 0, other + shift, NONE)
        bad = bad + count((jnp.minimum(a, b) != jnp.minimum(own + shift, want))
                          | (jnp.maximum(a, b) != jnp.maximum(own + shift, want)))
    ok = bad == 0.0
    flag_ref[0] = jnp.where(ok, 1, 0)

    table[...] = ordered

    @pl.when(jnp.logical_not(ok))
    def _():
        same = (lane_e == ring).astype(jnp.float32)
        table[...] = jnp.dot(same, raw_table, precision=HIGH, preferred_element_type=jnp.float32)

    placed = table[...]
    for q in range(16):
        scale = -float(WEIGHTS[q // 4] * WEIGHTS[q % 4])
        rows = slice(q * ELEMS, (q + 1) * ELEMS)
        mx_ref[rows, :] = jnp.broadcast_to(scale * placed[:, q:q + 1], (ELEMS, 128))
        my_ref[rows, :] = jnp.broadcast_to(scale * placed[:, 16 + q:17 + q], (ELEMS, 128))
        im_ref[rows, :] = jnp.broadcast_to(placed[:, 32 + q:33 + q], (ELEMS, 128))

    load.wait()

    def gather(t, carry):
        for s in range(SEGS):
            y = STEPS * s + t
            e = jnp.where(ok, send_s[0, 3 * y + 1] >> 4, y)
            for half in range(2):
                value = raw[pl.ds(pl.multiple_of(16 * e + 8 * half, 8), 8), :]
                u_ref[pl.ds(8 * half * ELEMS + t * SEGS + s, 8, stride=ELEMS), :] = value
        return carry

    lax.fori_loop(0, STEPS, gather, 0)

    def body(t, carry):
        x = [plane(u_ref, q, t) for q in range(16)]
        out = weak(x, lambda q: plane(mx_ref, q, t), lambda q: plane(my_ref, q, t))
        for q in range(16):
            set_plane(s_ref, q, t, out[q])
        return carry

    lax.fori_loop(0, STEPS, body, 0)

    @pl.when(jnp.logical_not(ok))
    def _():
        v_ref[...] = s_ref[...]

    finish(ok, v_ref, s_ref, behind_ref, ahead_ref, partner_any, send_any, partner_s, send_g)


def joined(s_ref, left_ref, right_ref, im_ref, t):
    x = [plane(s_ref, q, t) for q in range(16)]
    for base, arrived in ((0, left_ref), (12, right_ref)):
        for j in range(3):
            x[base + j] = x[base + j] + plane(arrived, j, t)
        x[base + 3] = x[base + 3] + following(arrived, 0, t)
    return [x[q] * plane(im_ref, q, t) for q in range(16)]


def pass_kernel(updates, flag, s_in, left, right, mx_ref, my_ref, im_ref, u_in, visc, partner_any, send_any, recv_any, *rest):
    if updates:
        u_ref, s_ref, behind_ref, ahead_ref, v_ref, partner_s, send_s, recv_s = rest
    else:
        s_ref, behind_ref, ahead_ref, v_ref, partner_s, send_s, recv_s = rest
    ok = flag[0] == 1

    def step(t, x, out_ref):
        if updates:
            rate = visc[...]
            for q in range(16):
                x[q] = plane(u_in, q, t) - rate * x[q]
                set_plane(u_ref, q, t, x[q])
        out = weak(x, lambda q: plane(mx_ref, q, t), lambda q: plane(my_ref, q, t))
        for q in range(16):
            set_plane(out_ref, q, t, out[q])

    @pl.when(ok)
    def _():
        def body(t, carry):
            step(t, joined(s_in, left, right, im_ref, t), s_ref)
            return carry

        lax.fori_loop(0, STEPS, body, 0)

    @pl.when(jnp.logical_not(ok))
    def _():
        v_ref[...] = s_in[...]
        general_receive(v_ref, left, right, recv_any, recv_s)

        def body(t, carry):
            step(t, [plane(v_ref, q, t) * plane(im_ref, q, t) for q in range(16)], v_ref)
            return carry

        lax.fori_loop(0, STEPS, body, 0)

    finish(ok, v_ref, s_ref, behind_ref, ahead_ref, partner_any, send_any, partner_s, send_s)


def last_kernel(flag, order_s, s_in, left, right, im_ref, u_in, visc, recv_any, out, u_ref, raw, v_ref, recv_s, sem):
    ok = flag[0] == 1
    rate = visc[...]

    @pl.when(ok)
    def _():
        def body(t, carry):
            x = joined(s_in, left, right, im_ref, t)
            for q in range(16):
                set_plane(u_ref, q, t, plane(u_in, q, t) - rate * x[q])
            return carry

        lax.fori_loop(0, STEPS, body, 0)

    @pl.when(jnp.logical_not(ok))
    def _():
        v_ref[...] = s_in[...]
        general_receive(v_ref, left, right, recv_any, recv_s)
        u_ref[...] = u_in[...] - rate * (v_ref[...] * im_ref[...])

    def scatter(t, carry):
        for s in range(SEGS):
            y = STEPS * s + t
            e = jnp.where(ok, order_s[0, 3 * y + 1] >> 4, y)
            for half in range(2):
                value = u_ref[pl.ds(8 * half * ELEMS + t * SEGS + s, 8, stride=ELEMS), :]
                raw[pl.ds(pl.multiple_of(16 * e + 8 * half, 8), 8), :] = value
        return carry

    lax.fori_loop(0, STEPS, scatter, 0)
    store = pltpu.make_async_copy(raw, out, sem)
    store.start()
    store.wait()


VM = pl.BlockSpec(memory_space=pltpu.VMEM)
SM = pl.BlockSpec(memory_space=pltpu.SMEM)
HB = pl.BlockSpec(memory_space=pl.ANY)
FIELD = jax.ShapeDtypeStruct((ROWS, COLS), jnp.float32)
MESSAGE = jax.ShapeDtypeStruct((EDGE, COLS), jnp.float32)
SCRATCH = pltpu.VMEM((ROWS, COLS), jnp.float32)
PARTNER_S = pltpu.SMEM((3, ROWS), jnp.int32)
SEND_S = pltpu.SMEM((2, EDGE), jnp.int32)
RECV_S = pltpu.SMEM((4, EDGE), jnp.int32)


def call(kernel, ins, outs, specs, shapes, scratch, flops, moved, name):
    return pl.pallas_call(
        kernel,
        out_shape=shapes,
        in_specs=specs,
        out_specs=outs,
        scratch_shapes=scratch,
        compiler_params=pltpu.CompilerParams(vmem_limit_bytes=VMEM_LIMIT),
        cost_estimate=pl.CostEstimate(flops=flops, bytes_accessed=moved, transcendentals=0),
        name=name,
    )(*ins)


def swap(behind, ahead):
    size = lax.axis_size("elem")
    left = lax.ppermute(ahead, "elem", [(i, (i + 1) % size) for i in range(size)])
    right = lax.ppermute(behind, "elem", [(i, (i - 1) % size) for i in range(size)])
    return left, right


def shards(prognostic, metric, inv_mass, viscosity, partner, send_rows, recv_rows):
    visc = viscosity.reshape(1, COLS)
    work = 24 * ROWS * COLS
    u, s, mx, my, im, behind, ahead, flag = call(
        first_kernel,
        (prognostic, metric, inv_mass.reshape(ROWS // 128, 128), send_rows, send_rows, recv_rows, partner, partner, send_rows),
        [VM, VM, VM, VM, VM, VM, VM, SM],
        [HB, VM, VM, SM, VM, VM, VM, HB, HB],
        [FIELD, FIELD, FIELD, FIELD, FIELD, MESSAGE, MESSAGE, jax.ShapeDtypeStruct((1,), jnp.int32)],
        [SCRATCH, SCRATCH, pltpu.VMEM((ELEMS, 128), jnp.float32), PARTNER_S, SEND_S, pltpu.SemaphoreType.DMA],
        2 * work, 8 * 4 * ROWS * COLS, "first",
    )
    for cycle in range(SUBCYCLES):
        for updates in (False, True):
            left, right = swap(behind, ahead)
            if updates and cycle == SUBCYCLES - 1:
                break
            ins = (flag, s, left, right, mx, my, im, u, visc, partner, send_rows, recv_rows)
            shapes = [FIELD] * (2 if updates else 1) + [MESSAGE, MESSAGE]
            results = call(
                lambda *refs, updates=updates: pass_kernel(updates, *refs),
                ins, [VM] * len(shapes), [SM, VM, VM, VM, VM, VM, VM, VM, VM, HB, HB, HB], shapes,
                [SCRATCH, PARTNER_S, SEND_S, RECV_S],
                work, 6 * 4 * ROWS * COLS, "update" if updates else "second",
            )
            if updates:
                u = results[0]
            s, behind, ahead = results[-3:]
    return call(
        last_kernel,
        (flag, send_rows, s, left, right, im, u, visc, recv_rows),
        HB, [SM, SM, VM, VM, VM, VM, VM, VM, HB], FIELD,
        [SCRATCH, SCRATCH, SCRATCH, RECV_S, pltpu.SemaphoreType.DMA],
        work // 8, 4 * 4 * ROWS * COLS, "last",
    )


def solution(mesh):
    placed = (
        P("elem", None),
        P(None, "elem"),
        P("elem"),
        P(),
        P(None, "elem"),
        P("elem", None),
        P("elem", None),
    )
    return jax.shard_map(
        shards, mesh=mesh, in_specs=placed, out_specs=P("elem", None), check_vma=False
    )
```

time: 470 us -> 80.9 us (0.17)
  local copies, waits for them, and re-layouts: 207 us -> 5.33 us
  other arithmetic: 141 us -> 0 us
  matrix products: 73.2 us -> 0 us
  Pallas kernels: 0 us -> 23 us
  waiting for transfers between devices: 13.5 us -> 21.5 us
    gather x20 -> x0, local copies, waits for them, and re-layouts: 187 us -> none  [the longest x4 56.6 us: assemble(): padded[partner[2]]]
    scatter-add x16 -> x0, other arithmetic: 110 us -> none  [the longest x8 56 us: place(): return accumulated.at[targets[1]].add(payload)]
    dot_general x16 -> x0, matrix products: 73.2 us -> none  [the longest x4 20.1 us: weak_laplacian(): jnp.einsum('kj,eikc->eijc', derivative, flux_y, precision=highest) * along_i]
    pallas_call x0 -> x5, Pallas kernels: none -> 23 us  [call(): pl.pallas_call(kernel, out_shape=shapes, in_specs=specs, out_specs=outs,...]
    add x4 -> x0, other arithmetic: 15.3 us -> none  [assemble(): values + padded[partner[0]] + padded[partner[1]] + padded[partner[2]]]
    ppermute x8, waiting for transfers between devices: 13.5 us -> 21.5 us  [the longest x4 21.5 us: swap(): lax.ppermute(ahead, 'elem', [(i, (i + 1) % size) for i in range(size)])]
    sub x2 -> x0, other arithmetic: 6.05 us -> none  [shards(): fields = fields - viscosity[None, :] * second_pass]
    neg x4 -> x0, other arithmetic: 5.46 us -> none  [weak_laplacian(): return -(part_x + part_y).reshape(values.shape)]
  transfers between devices with their start and end apart: 8 -> 8, of which waited for: 4 -> 4; matrix products, arithmetic and copies ran while one was open for 14% -> 0% of each run, Pallas kernels for 0% -> 0%
where the time goes in v1:
time: 80.9 us; the launch traced here: 80.5 us
  starting transfers between devices  30.5 us (38%)
  Pallas kernels  23 us (28%)
  waiting for transfers between devices  21.5 us (27%)
  local copies, waits for them, and re-layouts  5.33 us (7%)
    ppermute x4, starting transfers between devices, swap(): lax.ppermute(behind, 'elem', [(i, (i - 1) % size) for i in range(size)])  30.2 us
    pallas_call x5, Pallas kernels, call(): pl.pallas_call(kernel, out_shape=shapes, in_specs=specs, out_specs=outs,...  23 us
    ppermute x4, waiting for transfers between devices, swap(): lax.ppermute(ahead, 'elem', [(i, (i + 1) % size) for i in range(size)])  21.5 us
    unnamed x20, local copies, waits for them, and re-layouts  5.33 us
  transfers between devices with their start and end apart: 8, of which 4 were waited for; matrix products, arithmetic and copies ran while one was open for 0% of the time, Pallas kernels for 0%

profile of v1, /device:TPU:0, one launch (start us, length us, event | category | flops | bytes accessed | tf_op | source)
XLA Modules:
  0.0 80.5 jit_solution(4911856657032842703)
XLA Ops:
  0.0 0.0 copy-start
  0.0 1.6 %copy-done = f32[4096,128]{1,0:T(8,128)S(1)} copy-done((f32[4096,128]{1,0:T(8,128)S(1)}, f32[4096,128]{1,0:T(8,128)}, u32[]{:S(2)}) %copy-start) | copy-done | bytes 2097176
  1.6 0.8 %copy-done.1 = s32[3,4096]{1,0:T(4,128)S(1)} copy-done((s32[3,4096]{1,0:T(4,128)S(1)}, s32[3,4096]{1,0:T(4,128)}, u32[]{:S(2)}) %copy-start.1) | copy-done | bytes 49176
  2.5 0.7 copy-done.3
  3.2 0.7 copy-done.5
  3.8 0.8 copy-done.7
  4.6 0.7 copy-done.8
  5.3 9.0 %first.1 = (f32[4096,128]{1,0:T(8,128)S(1)}, f32[4096,128]{1,0:T(8,128)S(1)}, f32[4096,128]{1,0:T(8,128)S(1)}, f32[4096,128]{1,0:T(8,128)S(1)}, f32[4096,128]{1,...) custom-call(f32[4096,128]{1,0:T(8,128)S(1)} %copy-done, f32[2,4096]{1,0:T(2,128)S(1)} %copy-done.7, ...), custom_call_target="tpu_custom_call" | custom-call | flops 25165824 | bytes 16777216 | tf_op jit(solution)/shard_map/first/pallas_call | solution.py:413
  14.3 0.1 collective-permute-start
  14.4 8.3 %collective-permute-start.1 = (f32[768,128]{1,0:T(8,128)S(1)}, f32[768,128]{1,0:T(8,128)S(1)}, u32[]{:S(2)}, u32[]{:S(2)}) collective-permute-start(f32[768,128]{1,0:T(8,128)S(1)} %get-tuple-element.26), channel_id=1, source_target_pairs={{0,127},{1,0},{2,1},{3,2},{4,3},{5,4},{6,5},{7,6},{8,7},{9,8},{10,... | collective-permute-start | bytes 1179656 | tf_op jit(solution)/shard_map/ppermute | solution.py:428
  22.7 5.4 %collective-permute-done.refs_2_ = f32[768,128]{1,0:T(8,128)S(1)} collective-permute-done((f32[768,128]{1,0:T(8,128)S(1)}, f32[768,128]{1,0:T(8,128)S(1)}, u32[]{:S(2)}, u32[]{:S(2)}) %collective-permute-start) | collective-permute-done | bytes 393248 | tf_op jit(solution)/shard_map/ppermute | solution.py:427
  28.1 0.0 collective-permute-done.1.refs_3_
  28.1 0.0 copy-done.9
  28.1 0.0 copy-done.2
  28.1 0.0 copy-done.4
  28.1 0.0 copy-done.6
  28.1 2.7 %second.2 = (f32[4096,128]{1,0:T(8,128)S(1)}, f32[768,128]{1,0:T(8,128)S(1)}, f32[768,128]{1,0:T(8,128)S(1)}) custom-call(s32[1]{0:T(128)} %get-tuple-element.23.refs_0_.flag, f32[4096,128]{1,0:T(8,128)S(1)} %get-tuple-element.24.refs_1_, f32[768,128]{1,0:T(8,128)S(1)} %collective-permute-done.refs_2_, f32[768,128]{1,0:T(8,128)S(1)} %collective-permute-done.1.refs_3_, ...), custom_call_target="tpu_custom_call" | custom-call | flops 12582912 | bytes 12582912 | tf_op jit(solution)/shard_map/second/pallas_call | solution.py:413
  30.8 0.1 collective-permute-start.2
  30.9 7.3 %collective-permute-start.3 = (f32[768,128]{1,0:T(8,128)S(1)}, f32[768,128]{1,0:T(8,128)S(1)}, u32[]{:S(2)}, u32[]{:S(2)}) collective-permute-start(f32[768,128]{1,0:T(8,128)S(1)} %get-tuple-element.33), channel_id=1, source_target_pairs={{0,127},{1,0},{2,1},{3,2},{4,3},{5,4},{6,5},{7,6},{8,7},{9,8},{10,... | collective-permute-start | bytes 1179656 | tf_op jit(solution)/shard_map/ppermute | solution.py:428
  38.2 5.4 %collective-permute-done.2.refs_2_ = f32[768,128]{1,0:T(8,128)S(1)} collective-permute-done((f32[768,128]{1,0:T(8,128)S(1)}, f32[768,128]{1,0:T(8,128)S(1)}, u32[]{:S(2)}, u32[]{:S(2)}) %collective-permute-start.2) | collective-permute-done | bytes 393248 | tf_op jit(solution)/shard_map/ppermute | solution.py:427
  43.6 0.0 collective-permute-done.3.refs_3_
  43.6 3.3 %update.1 = (f32[4096,128]{1,0:T(8,128)S(1)}, f32[4096,128]{1,0:T(8,128)S(1)}, f32[768,128]{1,0:T(8,128)S(1)}, f32[768,128]{1,0:T(8,128)S(1)}) custom-call(s32[1]{0:T(128)} %get-tuple-element.23.refs_0_.flag, f32[4096,128]{1,0:T(8,128)S(1)} %get-tuple-element.31.refs_1_, f32[768,128]{1,0:T(8,128)S(1)} %collective-permute-done.2.refs_2_, ...), custom_call_target="tpu_custom_call" | custom-call | flops 12582912 | bytes 12582912 | tf_op jit(solution)/shard_map/update/pallas_call | solution.py:413
  46.9 0.1 collective-permute-start.4
  46.9 7.3 %collective-permute-start.5 = (f32[768,128]{1,0:T(8,128)S(1)}, f32[768,128]{1,0:T(8,128)S(1)}, u32[]{:S(2)}, u32[]{:S(2)}) collective-permute-start(f32[768,128]{1,0:T(8,128)S(1)} %get-tuple-element.36), channel_id=1, source_target_pairs={{0,127},{1,0},{2,1},{3,2},{4,3},{5,4},{6,5},{7,6},{8,7},{9,8},{10,... | collective-permute-start | bytes 1179656 | tf_op jit(solution)/shard_map/ppermute | solution.py:428
  54.3 5.4 %collective-permute-done.4.refs_2_ = f32[768,128]{1,0:T(8,128)S(1)} collective-permute-done((f32[768,128]{1,0:T(8,128)S(1)}, f32[768,128]{1,0:T(8,128)S(1)}, u32[]{:S(2)}, u32[]{:S(2)}) %collective-permute-start.4) | collective-permute-done | bytes 393248 | tf_op jit(solution)/shard_map/ppermute | solution.py:427
  59.6 0.0 collective-permute-done.5.refs_3_
  59.6 2.7 %second.3 = (f32[4096,128]{1,0:T(8,128)S(1)}, f32[768,128]{1,0:T(8,128)S(1)}, f32[768,128]{1,0:T(8,128)S(1)}) custom-call(s32[1]{0:T(128)} %get-tuple-element.23.refs_0_.flag, f32[4096,128]{1,0:T(8,128)S(1)} %get-tuple-element.34.refs_1_, f32[768,128]{1,0:T(8,128)S(1)} %collective-permute-done.4.refs_2_, f32[768,128]{1,0:T(8,128)S(1)} %collective-permute-done.5.refs_3_, ...), custom_call_target="tpu_custom_call" | custom-call | flops 12582912 | bytes 12582912 | tf_op jit(solution)/shard_map/second/pallas_call | solution.py:413
  62.3 0.1 collective-permute-start.6
  62.4 7.3 %collective-permute-start.7 = (f32[768,128]{1,0:T(8,128)S(1)}, f32[768,128]{1,0:T(8,128)S(1)}, u32[]{:S(2)}, u32[]{:S(2)}) collective-permute-start(f32[768,128]{1,0:T(8,128)S(1)} %get-tuple-element.40), channel_id=1, source_target_pairs={{0,127},{1,0},{2,1},{3,2},{4,3},{5,4},{6,5},{7,6},{8,7},{9,8},{10,... | collective-permute-start | bytes 1179656 | tf_op jit(solution)/shard_map/ppermute | solution.py:428
  69.7 5.4 %collective-permute-done.6.left = f32[768,128]{1,0:T(8,128)S(1)} collective-permute-done((f32[768,128]{1,0:T(8,128)S(1)}, f32[768,128]{1,0:T(8,128)S(1)}, u32[]{:S(2)}, u32[]{:S(2)}) %collective-permute-start.6) | collective-permute-done | bytes 393248 | tf_op jit(solution)/shard_map/ppermute | solution.py:427
  75.1 0.0 collective-permute-done.7.right
  75.1 5.4 %last.1 = f32[4096,128]{1,0:T(8,128)} custom-call(s32[1]{0:T(128)} %get-tuple-element.23.refs_0_.flag, s32[2,768]{1,0:T(2,128)S(1)} %copy-done.6, f32[4096,128]{1,0:T(8,128)S(1)} %get-tuple-element.38.s_in, f32[768,128]{1,0:T(8,128)S(1)} %collective-permute-done.6.left, f32[768,128]{1,0:T(8,128)S(1)} %collective-permute-done.7.right, ...), custom_call_target="tpu_custom_call" | custom-call | flops 1572864 | bytes 8388608 | tf_op jit(solution)/shard_map/last/pallas_call | solution.py:413
  (9 shorter events, 0.0 us)
Async XLA Ops:
  0.0 28.1 %copy-start.9 = (f32[128]{0:T(128)S(1)}, f32[128]{0:T(128)}, u32[]{:S(2)}) copy-start(f32[128]{0:T(128)} %param.10) | copy-start | bytes 1540
  0.0 1.6 %copy-start = (f32[4096,128]{1,0:T(8,128)S(1)}, f32[4096,128]{1,0:T(8,128)}, u32[]{:S(2)}) copy-start(f32[4096,128]{1,0:T(8,128)} %prog.1) | copy-start | bytes 6291460
  1.6 0.8 %copy-start.1 = (s32[3,4096]{1,0:T(4,128)S(1)}, s32[3,4096]{1,0:T(4,128)}, u32[]{:S(2)}) copy-start(s32[3,4096]{1,0:T(4,128)} %refs_9_.5) | copy-start | bytes 147460
  2.4 0.7 copy-start.3
  3.2 0.7 copy-start.5
  3.8 0.8 copy-start.7
  4.6 0.7 copy-start.8
  5.3 22.8 %copy-start.2 = (s32[3,4096]{1,0:T(4,128)S(1)}, s32[3,4096]{1,0:T(4,128)}, u32[]{:S(2)}) copy-start(s32[3,4096]{1,0:T(4,128)} %refs_9_.5) | copy-start | bytes 147460
  5.3 22.8 %copy-start.4 = (s32[4,768]{1,0:T(4,128)S(1)}, s32[4,768]{1,0:T(4,128)}, u32[]{:S(2)}) copy-start(s32[4,768]{1,0:T(4,128)} %recv_any.1) | copy-start | bytes 36868
  5.3 22.8 %copy-start.6 = (s32[2,768]{1,0:T(2,128)S(1)}, s32[2,768]{1,0:T(2,128)}, u32[]{:S(2)}) copy-start(s32[2,768]{1,0:T(2,128)} %order_s.1) | copy-start | bytes 18436
  14.3 13.7 %collective-permute-start = (f32[768,128]{1,0:T(8,128)S(1)}, f32[768,128]{1,0:T(8,128)S(1)}, u32[]{:S(2)}, u32[]{:S(2)}) collective-permute-start(f32[768,128]{1,0:T(8,128)S(1)} %get-tuple-element.25), channel_id=1, source_target_pairs={{0,1},{1,2},{2,3},{3,4},{4,5},{5,6},{6,7},{7,8},{8,9},{9,10},{10,1... | collective-permute-start | bytes 1179656 | tf_op jit(solution)/shard_map/ppermute | solution.py:427
  14.4 13.7 %collective-permute-start.1 = (f32[768,128]{1,0:T(8,128)S(1)}, f32[768,128]{1,0:T(8,128)S(1)}, u32[]{:S(2)}, u32[]{:S(2)}) collective-permute-start(f32[768,128]{1,0:T(8,128)S(1)} %get-tuple-element.26), channel_id=1, source_target_pairs={{0,127},{1,0},{2,1},{3,2},{4,3},{5,4},{6,5},{7,6},{8,7},{9,8},{10,... | collective-permute-start | bytes 1179656 | tf_op jit(solution)/shard_map/ppermute | solution.py:428
  30.8 12.8 %collective-permute-start.2 = (f32[768,128]{1,0:T(8,128)S(1)}, f32[768,128]{1,0:T(8,128)S(1)}, u32[]{:S(2)}, u32[]{:S(2)}) collective-permute-start(f32[768,128]{1,0:T(8,128)S(1)} %get-tuple-element.32), channel_id=1, source_target_pairs={{0,1},{1,2},{2,3},{3,4},{4,5},{5,6},{6,7},{7,8},{8,9},{9,10},{10,1... | collective-permute-start | bytes 1179656 | tf_op jit(solution)/shard_map/ppermute | solution.py:427
  30.9 12.7 %collective-permute-start.3 = (f32[768,128]{1,0:T(8,128)S(1)}, f32[768,128]{1,0:T(8,128)S(1)}, u32[]{:S(2)}, u32[]{:S(2)}) collective-permute-start(f32[768,128]{1,0:T(8,128)S(1)} %get-tuple-element.33), channel_id=1, source_target_pairs={{0,127},{1,0},{2,1},{3,2},{4,3},{5,4},{6,5},{7,6},{8,7},{9,8},{10,... | collective-permute-start | bytes 1179656 | tf_op jit(solution)/shard_map/ppermute | solution.py:428
  46.9 12.8 %collective-permute-start.4 = (f32[768,128]{1,0:T(8,128)S(1)}, f32[768,128]{1,0:T(8,128)S(1)}, u32[]{:S(2)}, u32[]{:S(2)}) collective-permute-start(f32[768,128]{1,0:T(8,128)S(1)} %get-tuple-element.35), channel_id=1, source_target_pairs={{0,1},{1,2},{2,3},{3,4},{4,5},{5,6},{6,7},{7,8},{8,9},{9,10},{10,1... | collective-permute-start | bytes 1179656 | tf_op jit(solution)/shard_map/ppermute | solution.py:427
  46.9 12.7 %collective-permute-start.5 = (f32[768,128]{1,0:T(8,128)S(1)}, f32[768,128]{1,0:T(8,128)S(1)}, u32[]{:S(2)}, u32[]{:S(2)}) collective-permute-start(f32[768,128]{1,0:T(8,128)S(1)} %get-tuple-element.36), channel_id=1, source_target_pairs={{0,127},{1,0},{2,1},{3,2},{4,3},{5,4},{6,5},{7,6},{8,7},{9,8},{10,... | collective-permute-start | bytes 1179656 | tf_op jit(solution)/shard_map/ppermute | solution.py:428
  62.3 12.8 %collective-permute-start.6 = (f32[768,128]{1,0:T(8,128)S(1)}, f32[768,128]{1,0:T(8,128)S(1)}, u32[]{:S(2)}, u32[]{:S(2)}) collective-permute-start(f32[768,128]{1,0:T(8,128)S(1)} %get-tuple-element.39), channel_id=1, source_target_pairs={{0,1},{1,2},{2,3},{3,4},{4,5},{5,6},{6,7},{7,8},{8,9},{9,10},{10,1... | collective-permute-start | bytes 1179656 | tf_op jit(solution)/shard_map/ppermute | solution.py:427
  62.4 12.7 %collective-permute-start.7 = (f32[768,128]{1,0:T(8,128)S(1)}, f32[768,128]{1,0:T(8,128)S(1)}, u32[]{:S(2)}, u32[]{:S(2)}) collective-permute-start(f32[768,128]{1,0:T(8,128)S(1)} %get-tuple-element.40), channel_id=1, source_target_pairs={{0,127},{1,0},{2,1},{3,2},{4,3},{5,4},{6,5},{7,6},{8,7},{9,8},{10,... | collective-permute-start | bytes 1179656 | tf_op jit(solution)/shard_map/ppermute | solution.py:428

commit v2 on v1

v2 whole, which is shorter than its diff:
```python
import math

import jax
import jax.numpy as jnp
import numpy as np
from jax import lax
from jax.experimental import pallas as pl
from jax.experimental.pallas import tpu as pltpu
from jax.sharding import PartitionSpec as P

SUBCYCLES = 2
ELEMS = 256
ROWS = 16 * ELEMS
COLS = 128
EDGE = 3 * ELEMS
SEGS = 8
STEPS = ELEMS // SEGS
NONE = ROWS
VMEM_LIMIT = 24 * 2**20


def node_tables():
    root = 1.0 / math.sqrt(5.0)
    points = [-1.0, -root, root, 1.0]
    weights = np.array([1.0, 5.0, 5.0, 1.0]) / 6.0
    products = []
    for first in range(4):
        value = 1.0
        for other in range(4):
            if other != first:
                value = value * (points[first] - points[other])
        products.append(value)
    table = []
    for first in range(4):
        line = []
        for other in range(4):
            if other == first:
                total = 0.0
                for third in range(4):
                    if third != first:
                        total = total + 1.0 / (points[first] - points[third])
                line.append(total)
            else:
                line.append(products[first] / (products[other] * (points[first] - points[other])))
        table.append(line)
    return (np.array(table), weights)


D, WEIGHTS = node_tables()


def gradient(v):
    o0, o1 = v[0] - v[3], v[1] - v[2]
    h = (v[0] + v[3]) - (v[1] + v[2])
    q0 = float(0.5 * (D[0, 0] + D[0, 3])) * h
    q1 = float(0.5 * (D[1, 0] + D[1, 3])) * h
    s0 = float(0.5 * (D[0, 0] - D[0, 3])) * o0 + float(0.5 * (D[0, 1] - D[0, 2])) * o1
    s1 = float(0.5 * (D[1, 0] - D[1, 3])) * o0 + float(0.5 * (D[1, 1] - D[1, 2])) * o1
    return [s0 + q0, s1 + q1, s1 - q1, s0 - q0]


def divergence(f):
    g0, g1 = f[0] - f[3], f[1] - f[2]
    t0, t1 = f[0] + f[3], f[1] + f[2]
    z = float(0.5 * (D[0, 0] + D[0, 3])) * g0 + float(0.5 * (D[1, 0] + D[1, 3])) * g1
    r0 = float(0.5 * (D[0, 0] - D[0, 3])) * t0 + float(0.5 * (D[1, 0] - D[1, 3])) * t1
    r1 = float(0.5 * (D[0, 1] - D[0, 2])) * t0 + float(0.5 * (D[1, 1] - D[1, 2])) * t1
    return [z + r0, r1 - z, -z - r1, z - r0]


def weak(x, mx, my):
    out = [None] * 16
    for j in range(4):
        g = gradient([x[4 * i + j] for i in range(4)])
        f = divergence([mx(4 * i + j) * g[i] for i in range(4)])
        for i in range(4):
            out[4 * i + j] = f[i]
    for i in range(4):
        g = gradient([x[4 * i + j] for j in range(4)])
        f = divergence([my(4 * i + j) * g[j] for j in range(4)])
        for j in range(4):
            out[4 * i + j] = out[4 * i + j] + f[j]
    return out


def plane(ref, q, t):
    return ref[pl.ds(pl.multiple_of(q * ELEMS + t * SEGS, SEGS), SEGS), :]


def set_plane(ref, q, t, value):
    ref[pl.ds(pl.multiple_of(q * ELEMS + t * SEGS, SEGS), SEGS), :] = value


def following(ref, q, t):
    last = t == STEPS - 1
    value = plane(ref, q, jnp.where(last, 0, t + 1))
    return jnp.where(last, pltpu.roll(value, SEGS - 1, 0), value)


def place_of(y):
    return lax.rem(y, STEPS) * SEGS + lax.div(y, STEPS)


def state_row(r):
    return lax.rem(r, 16) * ELEMS + place_of(lax.div(r, 16))


def wire_row(m):
    return lax.rem(m, 3) * ELEMS + place_of(lax.div(m, 3))


def one(ref, row):
    return ref[pl.ds(row, 1), :]


def ring_sums(s_ref):
    for i in range(4):
        for t in range(STEPS):
            upper = plane(s_ref, 4 * i, (t + 1) % STEPS)
            if t == STEPS - 1:
                upper = first
                lower = plane(s_ref, 4 * i + 3, t)
                total = lower + pltpu.roll(upper, SEGS - 1, 0)
                set_plane(s_ref, 4 * i + 3, t, total)
                set_plane(s_ref, 4 * i, 0, pltpu.roll(total, 1, 0))
            else:
                if t == 0:
                    first = plane(s_ref, 4 * i, 0)
                total = plane(s_ref, 4 * i + 3, t) + upper
                set_plane(s_ref, 4 * i + 3, t, total)
                set_plane(s_ref, 4 * i, t + 1, total)


def edge_messages(s_ref, behind_ref, ahead_ref):
    behind_ref[...] = s_ref[0:EDGE, :]
    ahead_ref[...] = s_ref[12 * ELEMS:15 * ELEMS, :]


def general_sums(v_ref, s_ref, partner_any, partner_s):
    pltpu.sync_copy(partner_any, partner_s)

    def body(r, carry):
        total = one(v_ref, state_row(r))
        for k in range(3):
            other = partner_s[k, r]
            found = one(v_ref, state_row(jnp.minimum(other, ROWS - 1)))
            total = total + jnp.where(other < NONE, found, 0.0)
        s_ref[pl.ds(state_row(r), 1), :] = total
        return carry

    lax.fori_loop(0, ROWS, body, 0)


def general_messages(s_ref, behind_ref, ahead_ref, send_any, send_s):
    pltpu.sync_copy(send_any, send_s)

    def body(m, carry):
        ahead_ref[pl.ds(wire_row(m), 1), :] = one(s_ref, state_row(send_s[0, m]))
        behind_ref[pl.ds(wire_row(m), 1), :] = one(s_ref, state_row(send_s[1, m]))
        return carry

    lax.fori_loop(0, EDGE, body, 0)


def general_receive(total_ref, left_ref, right_ref, recv_any, recv_s):
    pltpu.sync_copy(recv_any, recv_s)

    def body(m, carry):
        for k, arrived in ((0, left_ref), (1, right_ref)):
            for c in range(2):
                target = recv_s[2 * k + c, m]

                @pl.when(target < NONE)
                def _():
                    row = pl.ds(state_row(target), 1)
                    total_ref[row, :] = total_ref[row, :] + one(arrived, wire_row(m))
        return carry

    lax.fori_loop(0, EDGE, body, 0)


def iota(shape, axis):
    return lax.broadcasted_iota(jnp.int32, shape, axis)


def flipped(v):
    sub = iota((SEGS, COLS), 0)
    for b in (1, 2, 4):
        low = (sub & b) == 0
        out = list(v)
        for i in range(8):
            if i & b == 0:
                out[i] = jnp.where(low, v[i], pltpu.roll(v[i + b], b, 0))
                out[i + b] = jnp.where(low, pltpu.roll(v[i], 8 - b, 0), v[i + b])
        v = out
    return v


def tile(ref, row):
    return ref[pl.ds(pl.multiple_of(row, 8), 8), :]


def lanes_total(bad):
    ones = jnp.where(bad, 1.0, 0.0)
    if ones.shape[0] > 1:
        ones = jnp.sum(ones, axis=0, keepdims=True)
    total = ones[:, 0:128]
    for c in range(1, ones.shape[1] // 128):
        total = total + ones[:, 128 * c:128 * c + 128]
    return total


def pieces(row):
    high = row.astype(jnp.bfloat16).astype(jnp.float32)
    rest = row - high
    middle = rest.astype(jnp.bfloat16).astype(jnp.float32)
    return [high, middle, rest - middle]


def element_table(groups):
    own = (iota((16, 256), 1) >> 4) == iota((16, 256), 0)
    lane = iota((256, 128), 1)
    point = iota((256, 128), 0) & 15
    table = None
    for g, chunks in enumerate(groups):
        rows = [jnp.where(own, jnp.broadcast_to(c, (16, 256)), 0.0) for c in chunks]
        spread = jnp.concatenate(rows, axis=0).astype(jnp.bfloat16)
        chosen = (lane == point + 16 * g).astype(jnp.float32).astype(jnp.bfloat16)
        part = jnp.dot(spread, chosen, preferred_element_type=jnp.float32)
        table = part if table is None else table + part
    return table


def in_order(order, table):
    hot = (iota((ELEMS, ELEMS), 1).astype(jnp.float32) == order).astype(jnp.float32).astype(jnp.bfloat16)
    return jnp.dot(hot, table.astype(jnp.bfloat16), preferred_element_type=jnp.float32)


def first_kernel(prog, metric_h, send_h, recv_h, partner_h,
                 u_ref, s_ref, mx_ref, my_ref, order_ref, behind_ref, ahead_ref, flag_ref,
                 raw, v_ref, table, metric, send_v, recv_v, partner_v, send_s, partner_s, sems):
    loads = [pltpu.make_async_copy(a, b, sems.at[k]) for k, (a, b) in enumerate(
        ((send_h, send_v), (metric_h, metric), (partner_h, partner_v), (recv_h, recv_v), (send_h, send_s), (prog, raw)))]
    for load in loads:
        load.start()
    loads[0].wait()

    send = send_v[...]
    order_row = send[0:1, :] >> 4
    place = iota((ELEMS, 1), 0)
    ring = (place & 7) * STEPS + (place >> 3)
    picked = iota((ELEMS, EDGE), 1) == 3 * ring + 1
    order = jnp.sum(jnp.where(picked, order_row.astype(jnp.float32), 0.0), axis=1, keepdims=True)
    hot = (iota((ELEMS, ELEMS), 1).astype(jnp.float32) == order).astype(jnp.float32)
    seen = jnp.sum(hot, axis=0, keepdims=True)
    bad = lanes_total(seen != 1.0)

    loads[1].wait()
    loads[2].wait()
    partner = partner_v[...]
    least = jnp.minimum(jnp.minimum(partner[0:1], partner[1:2]), partner[2:3])
    bad = bad + lanes_total(partner[0:1] + partner[1:2] + partner[2:3] - least != 2 * NONE)
    both = [pieces(metric[k:k + 1, :]) for k in range(2)]
    rows = [both[k][n] for n in range(3) for k in range(2)]
    rows += [(least >> 4).astype(jnp.float32), (least & 15).astype(jnp.float32)]
    raw_table = element_table([[row[:, 256 * c:256 * c + 256] for c in range(16)] for row in rows])
    ordered = in_order(order, raw_table)

    wide_order = jnp.broadcast_to(order, (ELEMS, 128))
    before = jnp.concatenate([pltpu.roll(wide_order[ELEMS - SEGS:, :], 1, 0), wide_order[:-SEGS, :]], axis=0)
    after = jnp.concatenate([wide_order[SEGS:, :], pltpu.roll(wide_order[:SEGS, :], SEGS - 1, 0)], axis=0)
    lane = iota((1, 128), 1)
    point_i = (lane >> 2) & 3
    point_j = lane & 3
    expect_a = jnp.where(point_j == 0, before, jnp.where(point_j == 3, after, float(ELEMS)))
    expect_b = jnp.where(point_j == 0, 4 * point_i + 3, jnp.where(point_j == 3, 4 * point_i, 0)).astype(jnp.float32)
    expect = jnp.where(lane < 112, expect_a, expect_b)
    bad = bad + lanes_total((lane >= 96) & (ordered != expect))

    loads[3].wait()
    m = iota((1, EDGE), 1)
    p = m - 3 * ((m * 43691) >> 17)
    wide = jnp.broadcast_to(order_row, (8, EDGE))
    up1 = pltpu.roll(wide, EDGE - 1, 1)[0:1]
    down1 = pltpu.roll(wide, 1, 1)[0:1]
    down2 = pltpu.roll(wide, 2, 1)[0:1]
    own = 16 * jnp.where(p == 0, up1, jnp.where(p == 1, order_row, down1)) + p
    other = jnp.where(p == 0, 16 * down2 + 3, NONE)
    recv = recv_v[...]
    for k, shift in ((0, 12), (1, 0)):
        named = send[k:k + 1, :] - shift
        bad = bad + lanes_total((named != own) & ((p != 0) | (named != other)))
        a, b = recv[2 * (1 - k):2 * (1 - k) + 1, :], recv[2 * (1 - k) + 1:2 * (1 - k) + 2, :]
        want = jnp.where(p == 0, other + shift, NONE)
        bad = bad + lanes_total((jnp.minimum(a, b) != jnp.minimum(own + shift, want))
                                | (jnp.maximum(a, b) != jnp.maximum(own + shift, want)))
    ok = jnp.sum(bad) == 0.0
    flag_ref[0] = jnp.where(ok, 1, 0)

    weights = jnp.where((point_i == 0) | (point_i == 3), -1.0, -5.0) * jnp.where((point_j == 0) | (point_j == 3), 1.0, 5.0)
    weights = weights * (1.0 / 36.0)

    def set_table(ordered):
        table[...] = weights * (ordered + pltpu.roll(ordered, 96, 1) + pltpu.roll(ordered, 64, 1))

    set_table(ordered)
    order_ref[...] = wide_order

    @pl.when(jnp.logical_not(ok))
    def _():
        order_ref[...] = jnp.broadcast_to(ring.astype(jnp.float32), (ELEMS, 128))
        set_table(in_order(ring.astype(jnp.float32), raw_table))

    loads[4].wait()
    loads[5].wait()

    def body(t, carry):
        elems = []
        for s in range(SEGS):
            y = STEPS * s + t
            elems.append(16 * jnp.where(ok, send_s[0, 3 * y + 1] >> 4, y))
        x = flipped([tile(raw, e) for e in elems]) + flipped([tile(raw, e + 8) for e in elems])
        row = tile(table, t * SEGS)
        mx, my = [], []
        for q in range(16):
            set_plane(u_ref, q, t, x[q])
            mx.append(jnp.broadcast_to(row[:, q:q + 1], (SEGS, COLS)))
            my.append(jnp.broadcast_to(row[:, 16 + q:17 + q], (SEGS, COLS)))
            set_plane(mx_ref, q, t, mx[q])
            set_plane(my_ref, q, t, my[q])
        out = weak(x, lambda q: mx[q], lambda q: my[q])
        for q in range(16):
            set_plane(s_ref, q, t, out[q])
        return carry

    lax.fori_loop(0, STEPS, body, 0, unroll=2)

    @pl.when(ok)
    def _():
        ring_sums(s_ref)
        edge_messages(s_ref, behind_ref, ahead_ref)

    @pl.when(jnp.logical_not(ok))
    def _():
        v_ref[...] = s_ref[...]
        general_sums(v_ref, s_ref, partner_h, partner_s)
        general_messages(s_ref, behind_ref, ahead_ref, send_h, send_s)


def edge_values(arrived, im_ref, base, t, scale):
    values = [plane(arrived, j, t) for j in range(3)] + [following(arrived, 0, t)]
    values = [values[j] * plane(im_ref, base + j, t) for j in range(4)]
    return values if scale is None else [scale * v for v in values]


def edge_gradient(left, right):
    h, o = left + right, left - right
    q0, q1 = float(0.5 * (D[0, 0] + D[0, 3])) * h, float(0.5 * (D[1, 0] + D[1, 3])) * h
    s0, s1 = float(0.5 * (D[0, 0] - D[0, 3])) * o, float(0.5 * (D[1, 0] - D[1, 3])) * o
    return [s0 + q0, s1 + q1, s1 - q1, s0 - q0]


def along_edge(c, my_ref, base, t):
    g = gradient(c)
    return divergence([plane(my_ref, base + j, t) * g[j] for j in range(4)])


def prepare_kernel(flag, s_in, mx_ref, my_ref, order, inv_mass, im_ref, kx_ref, w_ref, table):
    mass = inv_mass[...]
    mass = [jnp.concatenate([mass[2 * c:2 * c + 1, :], mass[2 * c + 1:2 * c + 2, :]], axis=1) for c in range(16)]
    split = [pieces(c) for c in mass]
    ordered = in_order(order[:, 0:1], element_table([[c[n] for c in split] for n in range(3)]))
    table[...] = ordered + pltpu.roll(ordered, 112, 1) + pltpu.roll(ordered, 96, 1)
    ok = flag[0] == 1

    def body(t, carry):
        row = tile(table, t * SEGS)
        x = []
        for q in range(16):
            im = jnp.broadcast_to(row[:, q:q + 1], (SEGS, COLS))
            set_plane(im_ref, q, t, im)
            x.append(im * plane(s_in, q, t))
        mx = [plane(mx_ref, q, t) for q in range(16)]
        for j in range(4):
            for n, (a, b) in enumerate(((0, 0), (0, 3), (3, 3))):
                total = None
                for k in range(4):
                    term = float(D[k, a] * D[k, b]) * mx[4 * k + j]
                    total = term if total is None else total + term
                set_plane(kx_ref, 4 * n + j, t, total)
        out = weak(x, lambda q: mx[q], lambda q: plane(my_ref, q, t))
        for q in range(16):
            set_plane(w_ref, q, t, out[q])
        return carry

    lax.fori_loop(0, STEPS, body, 0, unroll=2)

    @pl.when(jnp.logical_not(ok))
    def _():
        w_ref[...] = s_in[...]


def edge_kernel(updates, flag, w_ref, left, right, mx_ref, my_ref, im_ref, kx_ref, u_in, visc, partner_any, send_any, recv_any,
                g_ref, behind_ref, ahead_ref, v_ref, partner_s, send_s, recv_s):
    ok = flag[0] == 1

    @pl.when(ok)
    def _():
        scale = -visc[...] if updates else None

        def body(t, carry):
            cl = edge_values(left, im_ref, 0, t, scale)
            cr = edge_values(right, im_ref, 12, t, scale)
            tail = []
            for base, c, out, k0, k1, before in ((0, cl, behind_ref, 0, 4, carry[0]), (12, cr, ahead_ref, 4, 8, carry[1])):
                f = along_edge(c, my_ref, base, t)
                for j in range(4):
                    f[j] = f[j] + plane(w_ref, base + j, t) + plane(kx_ref, k0 + j, t) * cl[j] + plane(kx_ref, k1 + j, t) * cr[j]
                set_plane(out, 0, t, f[0] + before)
                set_plane(out, 1, t, f[1])
                set_plane(out, 2, t, f[2])
                tail.append(f[3])
            return tuple(tail)

        zero = jnp.zeros((SEGS, COLS), jnp.float32)
        tail = lax.fori_loop(0, STEPS, body, (zero, zero), unroll=4)
        for out, last in zip((behind_ref, ahead_ref), tail):
            out[0:SEGS, :] = out[0:SEGS, :] + pltpu.roll(last, 1, 0)

    @pl.when(jnp.logical_not(ok))
    def _():
        v_ref[...] = w_ref[...]
        general_receive(v_ref, left, right, recv_any, recv_s)

        def body(t, carry):
            x = [plane(v_ref, q, t) * plane(im_ref, q, t) for q in range(16)]
            if updates:
                x = [plane(u_in, q, t) - visc[...] * x[q] for q in range(16)]
            out = weak(x, lambda q: plane(mx_ref, q, t), lambda q: plane(my_ref, q, t))
            for q in range(16):
                set_plane(v_ref, q, t, out[q])
            return carry

        lax.fori_loop(0, STEPS, body, 0)
        general_sums(v_ref, g_ref, partner_any, partner_s)
        general_messages(g_ref, behind_ref, ahead_ref, send_any, send_s)


def inner_kernel(kind, flag, w_in, g_in, left, right, mx_ref, my_ref, im_ref, u_in, visc, recv_any, u_ref, w_ref, s_ref, recv_s):
    ok = flag[0] == 1
    rate = visc[...]

    @pl.when(ok)
    def _():
        scale = -rate if kind == 1 else None

        def complete(t, carry):
            cl = edge_values(left, im_ref, 0, t, scale)
            cr = edge_values(right, im_ref, 12, t, scale)
            lines = [along_edge(cl, my_ref, 0, t), along_edge(cr, my_ref, 12, t)]
            for j in range(4):
                g = edge_gradient(cl[j], cr[j])
                f = divergence([plane(mx_ref, 4 * i + j, t) * g[i] for i in range(4)])
                f[0] = f[0] + lines[0][j]
                f[3] = f[3] + lines[1][j]
                for i in range(4):
                    set_plane(s_ref, 4 * i + j, t, plane(w_in, 4 * i + j, t) + f[i])
            if kind == 1:
                for j in range(4):
                    set_plane(u_ref, j, t, plane(u_in, j, t) + cl[j])
                    set_plane(u_ref, 12 + j, t, plane(u_in, 12 + j, t) + cr[j])
                for q in range(4, 12):
                    set_plane(u_ref, q, t, plane(u_in, q, t))
            return carry

        lax.fori_loop(0, STEPS, complete, 0, unroll=2)
        ring_sums(s_ref)

        def onward(t, carry):
            x = [plane(s_ref, q, t) * plane(im_ref, q, t) for q in range(16)]
            if kind != 1:
                x = [plane(u_in, q, t) - rate * x[q] for q in range(16)]
                for q in range(16):
                    set_plane(u_ref, q, t, x[q])
            if kind != 2:
                out = weak(x, lambda q: plane(mx_ref, q, t), lambda q: plane(my_ref, q, t))
                for q in range(16):
                    set_plane(w_ref, q, t, out[q])
            return carry

        lax.fori_loop(0, STEPS, onward, 0, unroll=2)

    @pl.when(jnp.logical_not(ok))
    def _():
        w_ref[...] = g_in[...]
        if kind == 1:
            s_ref[...] = w_in[...]
            general_receive(s_ref, left, right, recv_any, recv_s)
            u_ref[...] = u_in[...] - rate * (s_ref[...] * im_ref[...])
        else:
            u_ref[...] = u_in[...]


def last_kernel(flag, order_s, w_in, left, right, im_ref, u_in, visc, recv_any, out, raw, v_ref, recv_s, sem):
    ok = flag[0] == 1
    rate = visc[...]

    def leave(t, x):
        elems = []
        for s in range(SEGS):
            y = STEPS * s + t
            elems.append(16 * jnp.where(ok, order_s[0, 3 * y + 1] >> 4, y))
        for half in range(2):
            rows = flipped(x[8 * half:8 * half + 8])
            for s in range(SEGS):
                raw[pl.ds(pl.multiple_of(elems[s] + 8 * half, 8), 8), :] = rows[s]

    @pl.when(ok)
    def _():
        def body(t, carry):
            x = [plane(u_in, q, t) for q in range(16)]
            for base, arrived in ((0, left), (12, right)):
                c = edge_values(arrived, im_ref, base, t, rate)
                for j in range(4):
                    x[base + j] = x[base + j] - c[j]
            leave(t, x)
            return carry

        lax.fori_loop(0, STEPS, body, 0, unroll=2)

    @pl.when(jnp.logical_not(ok))
    def _():
        v_ref[...] = w_in[...]
        general_receive(v_ref, left, right, recv_any, recv_s)
        v_ref[...] = u_in[...] - rate * (v_ref[...] * im_ref[...])

        def body(t, carry):
            leave(t, [plane(v_ref, q, t) for q in range(16)])
            return carry

        lax.fori_loop(0, STEPS, body, 0)

    store = pltpu.make_async_copy(raw, out, sem)
    store.start()
    store.wait()


VM = pl.BlockSpec(memory_space=pltpu.VMEM)
SM = pl.BlockSpec(memory_space=pltpu.SMEM)
HB = pl.BlockSpec(memory_space=pltpu.HBM)
FIELD = jax.ShapeDtypeStruct((ROWS, COLS), jnp.float32)
MESSAGE = jax.ShapeDtypeStruct((EDGE, COLS), jnp.float32)
TABLE = jax.ShapeDtypeStruct((ELEMS, COLS), jnp.float32)
SCRATCH = pltpu.VMEM((ROWS, COLS), jnp.float32)
TABLE_V = pltpu.VMEM((ELEMS, COLS), jnp.float32)
PARTNER_S = pltpu.SMEM((3, ROWS), jnp.int32)
SEND_S = pltpu.SMEM((2, EDGE), jnp.int32)
RECV_S = pltpu.SMEM((4, EDGE), jnp.int32)
WORK = 24 * ROWS * COLS
SIZE = 4 * ROWS * COLS


def call(kernel, ins, specs, shapes, outs, scratch, flops, moved, name):
    ins = [pltpu.with_memory_space_constraint(a, pltpu.HBM) if spec is HB else a for a, spec in zip(ins, specs)]
    return pl.pallas_call(
        kernel,
        out_shape=shapes,
        in_specs=specs,
        out_specs=outs,
        scratch_shapes=scratch,
        compiler_params=pltpu.CompilerParams(vmem_limit_bytes=VMEM_LIMIT),
        cost_estimate=pl.CostEstimate(flops=flops, bytes_accessed=moved, transcendentals=0),
        name=name,
    )(*ins)


def swap(behind, ahead):
    size = lax.axis_size("elem")
    left = lax.ppermute(ahead, "elem", [(i, (i + 1) % size) for i in range(size)])
    right = lax.ppermute(behind, "elem", [(i, (i - 1) % size) for i in range(size)])
    return left, right


def shards(prognostic, metric, inv_mass, viscosity, partner, send_rows, recv_rows):
    visc = viscosity.reshape(1, COLS)
    u, s, mx, my, order, behind, ahead, flag = call(
        first_kernel,
        (prognostic, metric, send_rows, recv_rows, partner),
        [HB] * 5,
        [FIELD, FIELD, FIELD, FIELD, TABLE, MESSAGE, MESSAGE, jax.ShapeDtypeStruct((1,), jnp.int32)],
        [VM] * 7 + [SM],
        [SCRATCH, SCRATCH, TABLE_V, pltpu.VMEM((2, ROWS), jnp.float32), pltpu.VMEM((2, EDGE), jnp.int32),
         pltpu.VMEM((4, EDGE), jnp.int32), pltpu.VMEM((3, ROWS), jnp.int32), SEND_S, PARTNER_S, pltpu.SemaphoreType.DMA((6,))],
        2 * WORK, 8 * SIZE, "first",
    )
    left, right = swap(behind, ahead)
    im, kx, w = call(
        prepare_kernel,
        (flag, s, mx, my, order, inv_mass.reshape(ROWS // 128, 128)),
        [SM, VM, VM, VM, VM, VM],
        [FIELD, jax.ShapeDtypeStruct((12 * ELEMS, COLS), jnp.float32), FIELD],
        [VM] * 3, [TABLE_V], WORK, 6 * SIZE, "prepare",
    )
    for step in range(2 * SUBCYCLES - 1):
        updates = step % 2 == 1
        g, behind, ahead = call(
            lambda *refs, updates=updates: edge_kernel(updates, *refs),
            (flag, w, left, right, mx, my, im, kx, u, visc, partner, send_rows, recv_rows),
            [SM] + [VM] * 9 + [HB] * 3, [FIELD, MESSAGE, MESSAGE], [VM] * 3,
            [SCRATCH, PARTNER_S, SEND_S, RECV_S], WORK // 3, 2 * SIZE, "edges",
        )
        came = (left, right)
        left, right = swap(behind, ahead)
        kind = 1 if updates else 2 if step == 2 * SUBCYCLES - 2 else 0
        u, w = call(
            lambda *refs, kind=kind: inner_kernel(kind, *refs),
            (flag, w, g, *came, mx, my, im, u, visc, recv_rows),
            [SM] + [VM] * 9 + [HB], [FIELD, FIELD], [VM] * 2,
            [SCRATCH, RECV_S], WORK * 2, 8 * SIZE, "inner",
        )
    return call(
        last_kernel,
        (flag, send_rows, w, left, right, im, u, visc, recv_rows),
        [SM, SM] + [VM] * 6 + [HB], FIELD, HB,
        [SCRATCH, SCRATCH, RECV_S, pltpu.SemaphoreType.DMA], WORK // 8, 4 * SIZE, "last",
    )


def solution(mesh):
    placed = (
        P("elem", None),
        P(None, "elem"),
        P("elem"),
        P(),
        P(None, "elem"),
        P("elem", None),
        P("elem", None),
    )
    return jax.shard_map(
        shards, mesh=mesh, in_specs=placed, out_specs=P("elem", None), check_vma=False
    )
```

time: 80.9 us -> 65.8 us (0.81)
  waiting for transfers between devices: 21.5 us -> 6.97 us
  local copies, waits for them, and re-layouts: 5.33 us -> 0.01 us
  Pallas kernels: 23 us -> 28 us
    ppermute x4, waiting for transfers between devices: 21.5 us -> 6.96 us  [swap(): lax.ppermute(ahead, 'elem', [(i, (i + 1) % size) for i in range(size)])]
    unnamed x20 -> x6, local copies, waits for them, and re-layouts: 5.33 us -> 0.01 us
    pallas_call x5 -> x9, Pallas kernels: 23 us -> 28 us  [call(): pl.pallas_call(kernel, out_shape=shapes, in_specs=specs, out_specs=outs,...]
  transfers between devices with their start and end apart: 8 -> 8, of which waited for: 4 -> 4; matrix products, arithmetic and copies ran while one was open for 0% -> 0% of each run, Pallas kernels for 0% -> 22%
where the time goes in v2:
time: 65.8 us; the launch traced here: 65.6 us
  starting transfers between devices  30.5 us (46%)
  Pallas kernels  28 us (43%)
  waiting for transfers between devices  6.97 us (11%)
    ppermute x4, starting transfers between devices, swap(): lax.ppermute(behind, 'elem', [(i, (i - 1) % size) for i in range(size)])  30.2 us
    pallas_call x9, Pallas kernels, call(): pl.pallas_call(kernel, out_shape=shapes, in_specs=specs, out_specs=outs,...  28 us
    ppermute x4, waiting for transfers between devices, swap(): lax.ppermute(ahead, 'elem', [(i, (i + 1) % size) for i in range(size)])  6.96 us
  transfers between devices with their start and end apart: 8, of which 4 were waited for; matrix products, arithmetic and copies ran while one was open for 0% of the time, Pallas kernels for 22%

profile of v2, /device:TPU:0, one launch (start us, length us, event | category | flops | bytes accessed | tf_op | source)
XLA Modules:
  0.0 65.6 jit_solution(1968427642901209707)
XLA Ops:
  0.0 0.0 copy-start.2
  0.0 5.5 %first.1 = (f32[4096,128]{1,0:T(8,128)S(1)}, f32[4096,128]{1,0:T(8,128)S(1)}, f32[4096,128]{1,0:T(8,128)S(1)}, f32[4096,128]{1,0:T(8,128)S(1)}, f32[256,128]{1,0...) custom-call(f32[4096,128]{1,0:T(8,128)} %prog.1, f32[2,4096]{1,0:T(2,128)} %metric_h.1, ...), custom_call_target="tpu_custom_call" | custom-call | flops 25165824 | bytes 16777216 | tf_op jit(solution)/shard_map/first/pallas_call | solution.py:565
  5.5 0.1 collective-permute-start
  5.6 8.3 %collective-permute-start.1 = (f32[768,128]{1,0:T(8,128)S(1)}, f32[768,128]{1,0:T(8,128)S(1)}, u32[]{:S(2)}, u32[]{:S(2)}) collective-permute-start(f32[768,128]{1,0:T(8,128)S(1)} %get-tuple-element.38), channel_id=1, source_target_pairs={{0,127},{1,0},{2,1},{3,2},{4,3},{5,4},{6,5},{7,6},{8,7},{9,8},{10,... | collective-permute-start | bytes 1179656 | tf_op jit(solution)/shard_map/ppermute | solution.py:580
  13.9 0.0 copy-done.2
  13.9 0.0 copy-start.1
  13.9 4.2 %prepare.1 = (f32[4096,128]{1,0:T(8,128)S(1)}, f32[3072,128]{1,0:T(8,128)S(1)}, f32[4096,128]{1,0:T(8,128)S(1)}) custom-call(s32[1]{0:T(128)} %get-tuple-element.31.flag.refs_0_, f32[4096,128]{1,0:T(8,128)S(1)} %get-tuple-element.32.s_in, f32[4096,128]{1,0:T(8,128)S(1)} %get-tuple-element.33.mx_ref.refs_4_.refs_5_, ...), custom_call_target="tpu_custom_call" | custom-call | flops 12582912 | bytes 12582912 | tf_op jit(solution)/shard_map/prepare/pallas_call | solution.py:565
  18.1 1.2 %collective-permute-done.refs_2_.refs_3_ = f32[768,128]{1,0:T(8,128)S(1)} collective-permute-done((f32[768,128]{1,0:T(8,128)S(1)}, f32[768,128]{1,0:T(8,128)S(1)}, u32[]{:S(2)}, u32[]{:S(2)}) %collective-permute-start) | collective-permute-done | bytes 393248 | tf_op jit(solution)/shard_map/ppermute | solution.py:579
  19.3 0.0 collective-permute-done.1.refs_3_.refs_4_
  19.3 0.0 copy-done.1
  19.3 1.4 %edges.3 = (f32[4096,128]{1,0:T(8,128)S(1)}, f32[768,128]{1,0:T(8,128)S(1)}, f32[768,128]{1,0:T(8,128)S(1)}) custom-call(s32[1]{0:T(128)} %get-tuple-element.31.flag.refs_0_, f32[4096,128]{1,0:T(8,128)S(1)} %get-tuple-element.36.refs_1_, f32[768,128]{1,0:T(8,128)S(1)} %collective-permute-done.refs_2_.refs_3_, ...), custom_call_target="tpu_custom_call" | custom-call | flops 4194304 | bytes 4194304 | tf_op jit(solution)/shard_map/edges/pallas_call | solution.py:565
  20.7 0.1 collective-permute-start.2
  20.7 7.3 %collective-permute-start.3 = (f32[768,128]{1,0:T(8,128)S(1)}, f32[768,128]{1,0:T(8,128)S(1)}, u32[]{:S(2)}, u32[]{:S(2)}) collective-permute-start(f32[768,128]{1,0:T(8,128)S(1)} %get-tuple-element.45), channel_id=1, source_target_pairs={{0,127},{1,0},{2,1},{3,2},{4,3},{5,4},{6,5},{7,6},{8,7},{9,8},{10,... | collective-permute-start | bytes 1179656 | tf_op jit(solution)/shard_map/ppermute | solution.py:580
  28.1 4.1 %inner.3 = (f32[4096,128]{1,0:T(8,128)S(1)}, f32[4096,128]{1,0:T(8,128)S(1)}) custom-call(s32[1]{0:T(128)} %get-tuple-element.31.flag.refs_0_, f32[4096,128]{1,0:T(8,128)S(1)} %get-tuple-element.36.refs_1_, f32[4096,128]{1,0:T(8,128)S(1)} %get-tuple-element.42.refs_2_, f32[768,128]{1,0:T(8,128)S(1)} %collective-permute-done.refs_2_.refs_3_, ...), custom_call_target="tpu_custom_call" | custom-call | flops 25165824 | bytes 16777216 | tf_op jit(solution)/shard_map/inner/pallas_call | solution.py:565
  32.1 1.3 %collective-permute-done.2.refs_2_.refs_3_ = f32[768,128]{1,0:T(8,128)S(1)} collective-permute-done((f32[768,128]{1,0:T(8,128)S(1)}, f32[768,128]{1,0:T(8,128)S(1)}, u32[]{:S(2)}, u32[]{:S(2)}) %collective-permute-start.2) | collective-permute-done | bytes 393248 | tf_op jit(solution)/shard_map/ppermute | solution.py:579
  33.4 0.0 collective-permute-done.3.refs_3_.refs_4_
  33.4 1.4 %edges.4 = (f32[4096,128]{1,0:T(8,128)S(1)}, f32[768,128]{1,0:T(8,128)S(1)}, f32[768,128]{1,0:T(8,128)S(1)}) custom-call(s32[1]{0:T(128)} %get-tuple-element.31.flag.refs_0_, f32[4096,128]{1,0:T(8,128)S(1)} %get-tuple-element.43.refs_1_, f32[768,128]{1,0:T(8,128)S(1)} %collective-permute-done.2.refs_2_.refs_3_, ...), custom_call_target="tpu_custom_call" | custom-call | flops 4194304 | bytes 4194304 | tf_op jit(solution)/shard_map/edges/pallas_call | solution.py:565
  34.9 0.1 collective-permute-start.4
  35.0 7.3 %collective-permute-start.5 = (f32[768,128]{1,0:T(8,128)S(1)}, f32[768,128]{1,0:T(8,128)S(1)}, u32[]{:S(2)}, u32[]{:S(2)}) collective-permute-start(f32[768,128]{1,0:T(8,128)S(1)} %get-tuple-element.50), channel_id=1, source_target_pairs={{0,127},{1,0},{2,1},{3,2},{4,3},{5,4},{6,5},{7,6},{8,7},{9,8},{10,... | collective-permute-start | bytes 1179656 | tf_op jit(solution)/shard_map/ppermute | solution.py:580
  42.3 3.7 %inner.4 = (f32[4096,128]{1,0:T(8,128)S(1)}, f32[4096,128]{1,0:T(8,128)S(1)}) custom-call(s32[1]{0:T(128)} %get-tuple-element.31.flag.refs_0_, f32[4096,128]{1,0:T(8,128)S(1)} %get-tuple-element.43.refs_1_, f32[4096,128]{1,0:T(8,128)S(1)} %get-tuple-element.47.refs_2_, f32[768,128]{1,0:T(8,128)S(1)} %collective-permute-done.2.refs_2_.refs_3_, ...), custom_call_target="tpu_custom_call" | custom-call | flops 25165824 | bytes 16777216 | tf_op jit(solution)/shard_map/inner/pallas_call | solution.py:565
  46.0 1.7 %collective-permute-done.4.refs_2_.refs_3_ = f32[768,128]{1,0:T(8,128)S(1)} collective-permute-done((f32[768,128]{1,0:T(8,128)S(1)}, f32[768,128]{1,0:T(8,128)S(1)}, u32[]{:S(2)}, u32[]{:S(2)}) %collective-permute-start.4) | collective-permute-done | bytes 393248 | tf_op jit(solution)/shard_map/ppermute | solution.py:579
  47.7 0.0 collective-permute-done.5.refs_3_.refs_4_
  47.7 1.4 %edges.5 = (f32[4096,128]{1,0:T(8,128)S(1)}, f32[768,128]{1,0:T(8,128)S(1)}, f32[768,128]{1,0:T(8,128)S(1)}) custom-call(s32[1]{0:T(128)} %get-tuple-element.31.flag.refs_0_, f32[4096,128]{1,0:T(8,128)S(1)} %get-tuple-element.48.refs_1_, f32[768,128]{1,0:T(8,128)S(1)} %collective-permute-done.4.refs_2_.refs_3_, ...), custom_call_target="tpu_custom_call" | custom-call | flops 4194304 | bytes 4194304 | tf_op jit(solution)/shard_map/edges/pallas_call | solution.py:565
  49.0 0.1 collective-permute-start.6
  49.1 7.3 %collective-permute-start.7 = (f32[768,128]{1,0:T(8,128)S(1)}, f32[768,128]{1,0:T(8,128)S(1)}, u32[]{:S(2)}, u32[]{:S(2)}) collective-permute-start(f32[768,128]{1,0:T(8,128)S(1)} %get-tuple-element.55), channel_id=1, source_target_pairs={{0,127},{1,0},{2,1},{3,2},{4,3},{5,4},{6,5},{7,6},{8,7},{9,8},{10,... | collective-permute-start | bytes 1179656 | tf_op jit(solution)/shard_map/ppermute | solution.py:580
  56.4 0.0 copy-start
  56.4 2.6 %inner.5 = (f32[4096,128]{1,0:T(8,128)S(1)}, f32[4096,128]{1,0:T(8,128)S(1)}) custom-call(s32[1]{0:T(128)} %get-tuple-element.31.flag.refs_0_, f32[4096,128]{1,0:T(8,128)S(1)} %get-tuple-element.48.refs_1_, f32[4096,128]{1,0:T(8,128)S(1)} %get-tuple-element.52.refs_2_, f32[768,128]{1,0:T(8,128)S(1)} %collective-permute-done.4.refs_2_.refs_3_, ...), custom_call_target="tpu_custom_call" | custom-call | flops 25165824 | bytes 16777216 | tf_op jit(solution)/shard_map/inner/pallas_call | solution.py:565
  59.0 2.8 %collective-permute-done.6.left = f32[768,128]{1,0:T(8,128)S(1)} collective-permute-done((f32[768,128]{1,0:T(8,128)S(1)}, f32[768,128]{1,0:T(8,128)S(1)}, u32[]{:S(2)}, u32[]{:S(2)}) %collective-permute-start.6) | collective-permute-done | bytes 393248 | tf_op jit(solution)/shard_map/ppermute | solution.py:579
  61.8 0.0 collective-permute-done.7.right
  61.8 0.0 copy-done
  61.8 3.8 %last.1 = f32[4096,128]{1,0:T(8,128)} custom-call(s32[1]{0:T(128)} %get-tuple-element.31.flag.refs_0_, s32[2,768]{1,0:T(2,128)S(1)} %copy-done, f32[4096,128]{1,0:T(8,128)S(1)} %get-tuple-element.53.w_in, f32[768,128]{1,0:T(8,128)S(1)} %collective-permute-done.6.left, f32[768,128]{1,0:T(8,128)S(1)} %collective-permute-done.7.right, ...), custom_call_target="tpu_custom_call" | custom-call | flops 1572864 | bytes 8388608 | tf_op jit(solution)/shard_map/last/pallas_call | solution.py:565
Async XLA Ops:
  0.0 13.9 %copy-start.2 = (f32[4096]{0:T(1024)S(1)}, f32[4096]{0:T(1024)}, u32[]{:S(2)}) copy-start(f32[4096]{0:T(1024)} %param.9) | copy-start | bytes 49156
  5.5 13.7 %collective-permute-start = (f32[768,128]{1,0:T(8,128)S(1)}, f32[768,128]{1,0:T(8,128)S(1)}, u32[]{:S(2)}, u32[]{:S(2)}) collective-permute-start(f32[768,128]{1,0:T(8,128)S(1)} %get-tuple-element.37), channel_id=1, source_target_pairs={{0,1},{1,2},{2,3},{3,4},{4,5},{5,6},{6,7},{7,8},{8,9},{9,10},{10,1... | collective-permute-start | bytes 1179656 | tf_op jit(solution)/shard_map/ppermute | solution.py:579
  5.6 13.7 %collective-permute-start.1 = (f32[768,128]{1,0:T(8,128)S(1)}, f32[768,128]{1,0:T(8,128)S(1)}, u32[]{:S(2)}, u32[]{:S(2)}) collective-permute-start(f32[768,128]{1,0:T(8,128)S(1)} %get-tuple-element.38), channel_id=1, source_target_pairs={{0,127},{1,0},{2,1},{3,2},{4,3},{5,4},{6,5},{7,6},{8,7},{9,8},{10,... | collective-permute-start | bytes 1179656 | tf_op jit(solution)/shard_map/ppermute | solution.py:580
  13.9 5.4 %copy-start.1 = (f32[128]{0:T(128)S(1)}, f32[128]{0:T(128)}, u32[]{:S(2)}) copy-start(f32[128]{0:T(128)} %param.10) | copy-start | bytes 1540
  20.7 12.8 %collective-permute-start.2 = (f32[768,128]{1,0:T(8,128)S(1)}, f32[768,128]{1,0:T(8,128)S(1)}, u32[]{:S(2)}, u32[]{:S(2)}) collective-permute-start(f32[768,128]{1,0:T(8,128)S(1)} %get-tuple-element.44), channel_id=1, source_target_pairs={{0,1},{1,2},{2,3},{3,4},{4,5},{5,6},{6,7},{7,8},{8,9},{9,10},{10,1... | collective-permute-start | bytes 1179656 | tf_op jit(solution)/shard_map/ppermute | solution.py:579
  20.7 12.7 %collective-permute-start.3 = (f32[768,128]{1,0:T(8,128)S(1)}, f32[768,128]{1,0:T(8,128)S(1)}, u32[]{:S(2)}, u32[]{:S(2)}) collective-permute-start(f32[768,128]{1,0:T(8,128)S(1)} %get-tuple-element.45), channel_id=1, source_target_pairs={{0,127},{1,0},{2,1},{3,2},{4,3},{5,4},{6,5},{7,6},{8,7},{9,8},{10,... | collective-permute-start | bytes 1179656 | tf_op jit(solution)/shard_map/ppermute | solution.py:580
  34.9 12.8 %collective-permute-start.4 = (f32[768,128]{1,0:T(8,128)S(1)}, f32[768,128]{1,0:T(8,128)S(1)}, u32[]{:S(2)}, u32[]{:S(2)}) collective-permute-start(f32[768,128]{1,0:T(8,128)S(1)} %get-tuple-element.49), channel_id=1, source_target_pairs={{0,1},{1,2},{2,3},{3,4},{4,5},{5,6},{6,7},{7,8},{8,9},{9,10},{10,1... | collective-permute-start | bytes 1179656 | tf_op jit(solution)/shard_map/ppermute | solution.py:579
  35.0 12.7 %collective-permute-start.5 = (f32[768,128]{1,0:T(8,128)S(1)}, f32[768,128]{1,0:T(8,128)S(1)}, u32[]{:S(2)}, u32[]{:S(2)}) collective-permute-start(f32[768,128]{1,0:T(8,128)S(1)} %get-tuple-element.50), channel_id=1, source_target_pairs={{0,127},{1,0},{2,1},{3,2},{4,3},{5,4},{6,5},{7,6},{8,7},{9,8},{10,... | collective-permute-start | bytes 1179656 | tf_op jit(solution)/shard_map/ppermute | solution.py:580
  49.0 12.8 %collective-permute-start.6 = (f32[768,128]{1,0:T(8,128)S(1)}, f32[768,128]{1,0:T(8,128)S(1)}, u32[]{:S(2)}, u32[]{:S(2)}) collective-permute-start(f32[768,128]{1,0:T(8,128)S(1)} %get-tuple-element.54), channel_id=1, source_target_pairs={{0,1},{1,2},{2,3},{3,4},{4,5},{5,6},{6,7},{7,8},{8,9},{9,10},{10,1... | collective-permute-start | bytes 1179656 | tf_op jit(solution)/shard_map/ppermute | solution.py:579
  49.1 12.7 %collective-permute-start.7 = (f32[768,128]{1,0:T(8,128)S(1)}, f32[768,128]{1,0:T(8,128)S(1)}, u32[]{:S(2)}, u32[]{:S(2)}) collective-permute-start(f32[768,128]{1,0:T(8,128)S(1)} %get-tuple-element.55), channel_id=1, source_target_pairs={{0,127},{1,0},{2,1},{3,2},{4,3},{5,4},{6,5},{7,6},{8,7},{9,8},{10,... | collective-permute-start | bytes 1179656 | tf_op jit(solution)/shard_map/ppermute | solution.py:580
  56.4 5.4 %copy-start = (s32[2,768]{1,0:T(2,128)S(1)}, s32[2,768]{1,0:T(2,128)}, u32[]{:S(2)}) copy-start(s32[2,768]{1,0:T(2,128)} %order_s.1) | copy-start | bytes 18436

commit v3 on v2

--- a/solution.py
+++ b/solution.py
@@ -1,3 +1,4 @@
+import functools
 import math
 
 import jax
@@ -16,7 +17,7 @@
 SEGS = 8
 STEPS = ELEMS // SEGS
 NONE = ROWS
-VMEM_LIMIT = 24 * 2**20
+VMEM_LIMIT = 12 * 2**20
 
 
 def node_tables():
@@ -237,7 +238,7 @@
 
 
 def first_kernel(prog, metric_h, send_h, recv_h, partner_h,
-                 u_ref, s_ref, mx_ref, my_ref, order_ref, behind_ref, ahead_ref, flag_ref,
+                 u_ref, s_ref, mx_ref, my_ref, order_ref, behind_ref, ahead_ref, pair_ref, flag_ref,
                  raw, v_ref, table, metric, send_v, recv_v, partner_v, send_s, partner_s, sems):
     loads = [pltpu.make_async_copy(a, b, sems.at[k]) for k, (a, b) in enumerate(
         ((send_h, send_v), (metric_h, metric), (partner_h, partner_v), (recv_h, recv_v), (send_h, send_s), (prog, raw)))]
@@ -295,7 +296,8 @@
         bad = bad + lanes_total((jnp.minimum(a, b) != jnp.minimum(own + shift, want))
                                 | (jnp.maximum(a, b) != jnp.maximum(own + shift, want)))
     ok = jnp.sum(bad) == 0.0
-    flag_ref[0] = jnp.where(ok, 1, 0)
+    odd = lax.rem(lax.axis_index("elem"), 2)
+    flag_ref[...] = jnp.where(iota((8, 128), 0) == 0, jnp.where(ok, 1, 0), odd)
 
     weights = jnp.where((point_i == 0) | (point_i == 3), -1.0, -5.0) * jnp.where((point_j == 0) | (point_j == 3), 1.0, 5.0)
     weights = weights * (1.0 / 36.0)
@@ -346,6 +348,14 @@
         general_sums(v_ref, s_ref, partner_h, partner_s)
         general_messages(s_ref, behind_ref, ahead_ref, send_h, send_s)
 
+    @pl.when(odd == 1)
+    def _():
+        pair_ref[...] = behind_ref[...]
+
+    @pl.when(odd == 0)
+    def _():
+        pair_ref[...] = ahead_ref[...]
+
 
 def edge_values(arrived, im_ref, base, t, scale):
     values = [plane(arrived, j, t) for j in range(3)] + [following(arrived, 0, t)]
@@ -371,7 +381,7 @@
     split = [pieces(c) for c in mass]
     ordered = in_order(order[:, 0:1], element_table([[c[n] for c in split] for n in range(3)]))
     table[...] = ordered + pltpu.roll(ordered, 112, 1) + pltpu.roll(ordered, 96, 1)
-    ok = flag[0] == 1
+    ok = flag[0, 0] == 1
 
     def body(t, carry):
         row = tile(table, t * SEGS)
@@ -400,9 +410,11 @@
         w_ref[...] = s_in[...]
 
 
-def edge_kernel(updates, flag, w_ref, left, right, mx_ref, my_ref, im_ref, kx_ref, u_in, visc, partner_any, send_any, recv_any,
-                g_ref, behind_ref, ahead_ref, v_ref, partner_s, send_s, recv_s):
-    ok = flag[0] == 1
+def edge_kernel(updates, odd, flag, seen, w_ref, chain, pair, mx_ref, my_ref, im_ref, kx_ref, u_in, visc, partner_any, send_any, recv_any, *rest):
+    pair_ref, g_out, chain_ref, v_ref, g_ref, partner_s, send_s, recv_s = rest[-8:]
+    ok = (flag[0, 0] == 1) & (flag[1, 0] == odd)
+    left, right = (pair, chain) if odd else (chain, pair)
+    behind_ref, ahead_ref = (pair_ref, chain_ref) if odd else (chain_ref, pair_ref)
 
     @pl.when(ok)
     def _():
@@ -427,7 +439,7 @@
         for out, last in zip((behind_ref, ahead_ref), tail):
             out[0:SEGS, :] = out[0:SEGS, :] + pltpu.roll(last, 1, 0)
 
-    @pl.when(jnp.logical_not(ok))
+    @pl.when((flag[0, 0] == 0) & (flag[1, 0] == odd))
     def _():
         v_ref[...] = w_ref[...]
         general_receive(v_ref, left, right, recv_any, recv_s)
@@ -443,18 +455,19 @@
 
         lax.fori_loop(0, STEPS, body, 0)
         general_sums(v_ref, g_ref, partner_any, partner_s)
+        pltpu.sync_copy(g_ref, g_out)
         general_messages(g_ref, behind_ref, ahead_ref, send_any, send_s)
 
 
-def inner_kernel(kind, flag, w_in, g_in, left, right, mx_ref, my_ref, im_ref, u_in, visc, recv_any, u_ref, w_ref, s_ref, recv_s):
-    ok = flag[0] == 1
+def inner_kernel(kind, flag, w_in, g_in, forward, backward, pair, mx_ref, my_ref, im_ref, u_in, visc, recv_any, u_ref, w_ref, s_ref, recv_s):
+    ok = flag[0, 0] == 1
     rate = visc[...]
 
     @pl.when(ok)
     def _():
         scale = -rate if kind == 1 else None
 
-        def complete(t, carry):
+        def complete(left, right, t, carry):
             cl = edge_values(left, im_ref, 0, t, scale)
             cr = edge_values(right, im_ref, 12, t, scale)
             lines = [along_edge(cl, my_ref, 0, t), along_edge(cr, my_ref, 12, t)]
@@ -473,7 +486,11 @@
                     set_plane(u_ref, q, t, plane(u_in, q, t))
             return carry
 
-        lax.fori_loop(0, STEPS, complete, 0, unroll=2)
+        for odd, left, right in ((0, forward, pair), (1, pair, backward)):
+            @pl.when(flag[1, 0] == odd)
+            def _():
+                lax.fori_loop(0, STEPS, functools.partial(complete, left, right), 0, unroll=2)
+
         ring_sums(s_ref)
 
         def onward(t, carry):
@@ -492,17 +509,21 @@
 
     @pl.when(jnp.logical_not(ok))
     def _():
-        w_ref[...] = g_in[...]
+        pltpu.sync_copy(g_in, w_ref)
         if kind == 1:
             s_ref[...] = w_in[...]
-            general_receive(s_ref, left, right, recv_any, recv_s)
+            for odd, left, right in ((0, forward, pair), (1, pair, backward)):
+                @pl.when(flag[1, 0] == odd)
+                def _():
+                    general_receive(s_ref, left, right, recv_any, recv_s)
+
             u_ref[...] = u_in[...] - rate * (s_ref[...] * im_ref[...])
         else:
             u_ref[...] = u_in[...]
 
 
-def last_kernel(flag, order_s, w_in, left, right, im_ref, u_in, visc, recv_any, out, raw, v_ref, recv_s, sem):
-    ok = flag[0] == 1
+def last_kernel(flag, seen, order_s, w_in, forward, backward, pair, im_ref, u_in, visc, recv_any, out, raw, v_ref, recv_s, sem):
+    ok = flag[0, 0] == 1
     rate = visc[...]
 
     def leave(t, x):
@@ -517,7 +538,7 @@
 
     @pl.when(ok)
     def _():
-        def body(t, carry):
+        def body(left, right, t, carry):
             x = [plane(u_in, q, t) for q in range(16)]
             for base, arrived in ((0, left), (12, right)):
                 c = edge_values(arrived, im_ref, base, t, rate)
@@ -526,12 +547,19 @@
             leave(t, x)
             return carry
 
-        lax.fori_loop(0, STEPS, body, 0, unroll=2)
+        for odd, left, right in ((0, forward, pair), (1, pair, backward)):
+            @pl.when(flag[1, 0] == odd)
+            def _():
+                lax.fori_loop(0, STEPS, functools.partial(body, left, right), 0, unroll=2)
 
     @pl.when(jnp.logical_not(ok))
     def _():
         v_ref[...] = w_in[...]
-        general_receive(v_ref, left, right, recv_any, recv_s)
+        for odd, left, right in ((0, forward, pair), (1, pair, backward)):
+            @pl.when(flag[1, 0] == odd)
+            def _():
+                general_receive(v_ref, left, right, recv_any, recv_s)
+
         v_ref[...] = u_in[...] - rate * (v_ref[...] * im_ref[...])
 
         def body(t, carry):
@@ -548,7 +576,10 @@
 VM = pl.BlockSpec(memory_space=pltpu.VMEM)
 SM = pl.BlockSpec(memory_space=pltpu.SMEM)
 HB = pl.BlockSpec(memory_space=pltpu.HBM)
+FREE = pl.BlockSpec(memory_space=pl.ANY)
 FIELD = jax.ShapeDtypeStruct((ROWS, COLS), jnp.float32)
+HELD = pltpu.HBM((ROWS, COLS), jnp.float32)
+WORD = jax.ShapeDtypeStruct((8, 128), jnp.int32)
 MESSAGE = jax.ShapeDtypeStruct((EDGE, COLS), jnp.float32)
 TABLE = jax.ShapeDtypeStruct((ELEMS, COLS), jnp.float32)
 SCRATCH = pltpu.VMEM((ROWS, COLS), jnp.float32)
@@ -560,7 +591,7 @@
 SIZE = 4 * ROWS * COLS
 
 
-def call(kernel, ins, specs, shapes, outs, scratch, flops, moved, name):
+def call(kernel, ins, specs, shapes, outs, scratch, flops, moved, name, aliases={}):
     ins = [pltpu.with_memory_space_constraint(a, pltpu.HBM) if spec is HB else a for a, spec in zip(ins, specs)]
     return pl.pallas_call(
         kernel,
@@ -568,60 +599,80 @@
         in_specs=specs,
         out_specs=outs,
         scratch_shapes=scratch,
+        input_output_aliases=aliases,
         compiler_params=pltpu.CompilerParams(vmem_limit_bytes=VMEM_LIMIT),
-        cost_estimate=pl.CostEstimate(flops=flops, bytes_accessed=moved, transcendentals=0),
+        cost_estimate=pl.CostEstimate(flops=1, bytes_accessed=1, transcendentals=0),
         name=name,
     )(*ins)
 
 
-def swap(behind, ahead):
+def moved(value, by):
     size = lax.axis_size("elem")
-    left = lax.ppermute(ahead, "elem", [(i, (i + 1) % size) for i in range(size)])
-    right = lax.ppermute(behind, "elem", [(i, (i - 1) % size) for i in range(size)])
-    return left, right
+    return lax.ppermute(value, "elem", [(i, (i + by) % size) for i in range(size)])
+
+
+def crossed(value):
+    size = lax.axis_size("elem")
+    return lax.ppermute(value, "elem", [(i, i + 1 - 2 * (i % 2)) for i in range(size)])
+
+
+def seen_kernel(arrived, before, out):
+    out[...] = jnp.zeros_like(out)
 
 
 def shards(prognostic, metric, inv_mass, viscosity, partner, send_rows, recv_rows):
     visc = viscosity.reshape(1, COLS)
-    u, s, mx, my, order, behind, ahead, flag = call(
+    u, s, mx, my, order, behind, ahead, pair, flag = call(
         first_kernel,
         (prognostic, metric, send_rows, recv_rows, partner),
         [HB] * 5,
-        [FIELD, FIELD, FIELD, FIELD, TABLE, MESSAGE, MESSAGE, jax.ShapeDtypeStruct((1,), jnp.int32)],
-        [VM] * 7 + [SM],
+        [FIELD, FIELD, FIELD, FIELD, TABLE, MESSAGE, MESSAGE, MESSAGE, WORD],
+        [VM] * 9,
         [SCRATCH, SCRATCH, TABLE_V, pltpu.VMEM((2, ROWS), jnp.float32), pltpu.VMEM((2, EDGE), jnp.int32),
          pltpu.VMEM((4, EDGE), jnp.int32), pltpu.VMEM((3, ROWS), jnp.int32), SEND_S, PARTNER_S, pltpu.SemaphoreType.DMA((6,))],
         2 * WORK, 8 * SIZE, "first",
     )
-    left, right = swap(behind, ahead)
+    crossing = crossed(pair)
+    forward = moved(ahead, 1)
+    backward = moved(behind, -1)
     im, kx, w = call(
         prepare_kernel,
         (flag, s, mx, my, order, inv_mass.reshape(ROWS // 128, 128)),
-        [SM, VM, VM, VM, VM, VM],
+        [VM] * 6,
         [FIELD, jax.ShapeDtypeStruct((12 * ELEMS, COLS), jnp.float32), FIELD],
         [VM] * 3, [TABLE_V], WORK, 6 * SIZE, "prepare",
     )
     for step in range(2 * SUBCYCLES - 1):
         updates = step % 2 == 1
-        g, behind, ahead = call(
-            lambda *refs, updates=updates: edge_kernel(updates, *refs),
-            (flag, w, left, right, mx, my, im, kx, u, visc, partner, send_rows, recv_rows),
-            [SM] + [VM] * 9 + [HB] * 3, [FIELD, MESSAGE, MESSAGE], [VM] * 3,
-            [SCRATCH, PARTNER_S, SEND_S, RECV_S], WORK // 3, 2 * SIZE, "edges",
-        )
-        came = (left, right)
-        left, right = swap(behind, ahead)
+        chained = ()
+        came = (forward, backward, crossing)
+        for odd in ((0, 1) if step % 2 == 0 else (1, 0)):
+            seen = call(seen_kernel, (came[odd], chained[0] if chained else flag), [FREE, FREE], WORD, VM, [], 0, 0, "seen")
+            pair, g, chain = call(
+                functools.partial(edge_kernel, updates, odd),
+                (flag, seen, w, came[odd], crossing, mx, my, im, kx, u, visc, partner, send_rows, recv_rows) + chained,
+                [VM, FREE] + [VM] * 9 + [HB] * 3 + [FREE, HB][:len(chained)], [MESSAGE, HELD, MESSAGE], [VM, HB, VM],
+                [SCRATCH, SCRATCH, PARTNER_S, SEND_S, RECV_S], WORK // 3, 2 * SIZE, "edges",
+                {14: 0, 15: 1} if chained else {},
+            )
+            chained = (pair, g)
+            if odd:
+                forward = moved(chain, 1)
+            else:
+                backward = moved(chain, -1)
+        crossing = crossed(pair)
         kind = 1 if updates else 2 if step == 2 * SUBCYCLES - 2 else 0
         u, w = call(
-            lambda *refs, kind=kind: inner_kernel(kind, *refs),
+            functools.partial(inner_kernel, kind),
             (flag, w, g, *came, mx, my, im, u, visc, recv_rows),
-            [SM] + [VM] * 9 + [HB], [FIELD, FIELD], [VM] * 2,
+            [VM, VM, HB] + [VM] * 8 + [HB], [FIELD, FIELD], [VM] * 2,
             [SCRATCH, RECV_S], WORK * 2, 8 * SIZE, "inner",
         )
+    seen = call(seen_kernel, (backward, flag), [FREE, FREE], WORD, VM, [], 0, 0, "seen")
     return call(
         last_kernel,
-        (flag, send_rows, w, left, right, im, u, visc, recv_rows),
-        [SM, SM] + [VM] * 6 + [HB], FIELD, HB,
+        (flag, seen, send_rows, w, forward, backward, crossing, im, u, visc, recv_rows),
+        [VM, FREE, SM] + [VM] * 7 + [HB], FIELD, HB,
         [SCRATCH, SCRATCH, RECV_S, pltpu.SemaphoreType.DMA], WORK // 8, 4 * SIZE, "last",
     )
 

time: 65.8 us -> 58.5 us (0.89)
  starting transfers between devices: 30.5 us -> 14.4 us
  waiting for transfers between devices: 6.97 us -> 20.8 us
  Pallas kernels: 28 us -> 23 us
    ppermute x8 -> x12, starting transfers between devices: 30.5 us -> 14.4 us  [the longest x8 10.8 us: moved(): lax.ppermute(value, 'elem', [(i, (i + by) % size) for i in range(size)])]
    ppermute x8 -> x12, waiting for transfers between devices: 6.97 us -> 20.8 us  [the longest x8 20.8 us: moved(): lax.ppermute(value, 'elem', [(i, (i + by) % size) for i in range(size)])]
    pallas_call x9 -> x19, Pallas kernels: 28 us -> 23 us  [call(): pl.pallas_call(kernel, out_shape=shapes, in_specs=specs, out_specs=outs,...]
  transfers between devices with their start and end apart: 8 -> 12, of which waited for: 4 -> 6; matrix products, arithmetic and copies ran while one was open for 0% -> 0% of each run, Pallas kernels for 22% -> 25%
where the time goes in v3:
time: 58.5 us; the launch traced here: 58.4 us
  Pallas kernels  23 us (39%)
  waiting for transfers between devices  20.8 us (36%)
  starting transfers between devices  14.4 us (25%)
    pallas_call x19, Pallas kernels, call(): pl.pallas_call(kernel, out_shape=shapes, in_specs=specs, out_specs=outs,...  23 us
    ppermute x8, waiting for transfers between devices, moved(): lax.ppermute(value, 'elem', [(i, (i + by) % size) for i in range(size)])  20.8 us
    ppermute x8, starting transfers between devices, moved(): lax.ppermute(value, 'elem', [(i, (i + by) % size) for i in range(size)])  10.8 us
    ppermute x4, starting transfers between devices, crossed(): lax.ppermute(value, 'elem', [(i, i + 1 - 2 * (i % 2)) for i in range(size)])  3.51 us
  transfers between devices with their start and end apart: 12, of which 6 were waited for; matrix products, arithmetic and copies ran while one was open for 0% of the time, Pallas kernels for 25%

profile of v3, /device:TPU:0, one launch (start us, length us, event | category | flops | bytes accessed | tf_op | source)
XLA Modules:
  0.0 58.4 jit_solution(15322909348978150397)
XLA Ops:
  0.0 5.0 %first.1 = (f32[4096,128]{1,0:T(8,128)S(1)}, f32[4096,128]{1,0:T(8,128)S(1)}, f32[4096,128]{1,0:T(8,128)S(1)}, f32[4096,128]{1,0:T(8,128)S(1)}, f32[256,128]{1,0...) custom-call(f32[4096,128]{1,0:T(8,128)} %prog.1, ...), custom_call_target="tpu_custom_call" | custom-call | flops 1 | bytes 1 | tf_op jit(solution)/shard_map/first/pallas_call | solution.py:596
  5.1 0.1 collective-permute-start
  5.1 2.1 %collective-permute-start.1 = (f32[768,128]{1,0:T(8,128)S(1)}, f32[768,128]{1,0:T(8,128)S(1)}, u32[]{:S(2)}, u32[]{:S(2)}) collective-permute-start(f32[768,128]{1,0:T(8,128)S(1)} %get-tuple-element.48), channel_id=1, source_target_pairs={{0,1},{1,0},{2,3},{3,2},{4,5},{5,4},{6,7},{7,6},{8,9},{9,8},{10,11... | collective-permute-start | bytes 1179656 | tf_op jit(solution)/shard_map/ppermute | solution.py:616
  7.2 6.9 %collective-permute-start.3 = (f32[768,128]{1,0:T(8,128)S(1)}, f32[768,128]{1,0:T(8,128)S(1)}, u32[]{:S(2)}, u32[]{:S(2)}) collective-permute-start(f32[768,128]{1,0:T(8,128)S(1)} %get-tuple-element.53), channel_id=1, source_target_pairs={{0,127},{1,0},{2,1},{3,2},{4,3},{5,4},{6,5},{7,6},{8,7},{9,8},{10,... | collective-permute-start | bytes 1179656 | tf_op jit(solution)/shard_map/ppermute | solution.py:611
  14.1 3.5 %prepare.1 = (f32[4096,128]{1,0:T(8,128)S(1)}, f32[3072,128]{1,0:T(8,128)S(1)}, f32[4096,128]{1,0:T(8,128)S(1)}) custom-call(s32[8,128]{1,0:T(8,128)S(1)} %get-tuple-element.41.before.flag, f32[4096,128]{1,0:T(8,128)S(1)} %get-tuple-element.43.s_in, f32[4096,128]{1,0:T(8,128)S(1)} %get-tuple-element.44.mx_ref, f32[4096,128]{1,0:T(8,128)S(1)} %get-tuple-element.45.my_ref, ...), custom_call_target="tpu_custom_call" | custom-call | flops 1 | bytes 1 | tf_op jit(solution)/shard_map/prepare/pallas_call | solution.py:596
  17.6 1.2 %collective-permute-done.arrived.chain.forward = f32[768,128]{1,0:T(8,128)S(1)} collective-permute-done((f32[768,128]{1,0:T(8,128)S(1)}, f32[768,128]{1,0:T(8,128)S(1)}, u32[]{:S(2)}, u32[]{:S(2)}) %collective-permute-start) | collective-permute-done | bytes 393248 | tf_op jit(solution)/shard_map/ppermute | solution.py:611
  18.8 0.0 collective-permute-done.1.pair
  18.8 0.8 %edges.6 = (f32[768,128]{1,0:T(8,128)S(1)}, f32[4096,128]{1,0:T(8,128)}, f32[768,128]{1,0:T(8,128)S(1)}) custom-call(s32[8,128]{1,0:T(8,128)S(1)} %get-tuple-element.41.before.flag, s32[8,128]{1,0:T(8,128)S(1)} %seen.7, f32[4096,128]{1,0:T(8,128)S(1)} %get-tuple-element.47.w_ref.w_in, f32[768,128]{1,0:T(8,128)S(1)} %collective-permute-done.arrived.chain.forward, ...), custom_call_target="tpu_custom_call" | custom-call | flops 1 | bytes 1 | tf_op jit(solution)/shard_map/edges/pallas_call | solution.py:596
  19.6 0.1 collective-permute-start.2
  19.7 0.0 collective-permute-done.3.arrived.chain.backward
  19.7 0.1 edges.7
  19.8 1.2 %collective-permute-start.4 = (f32[768,128]{1,0:T(8,128)S(1)}, f32[768,128]{1,0:T(8,128)S(1)}, u32[]{:S(2)}, u32[]{:S(2)}) collective-permute-start(f32[768,128]{1,0:T(8,128)S(1)} %get-tuple-element.58), channel_id=1, source_target_pairs={{0,1},{1,0},{2,3},{3,2},{4,5},{5,4},{6,7},{7,6},{8,9},{9,8},{10,11... | collective-permute-start | bytes 1179656 | tf_op jit(solution)/shard_map/ppermute | solution.py:616
  21.0 0.1 collective-permute-start.6
  21.1 3.5 %inner.3 = (f32[4096,128]{1,0:T(8,128)S(1)}, f32[4096,128]{1,0:T(8,128)S(1)}) custom-call(s32[8,128]{1,0:T(8,128)S(1)} %get-tuple-element.41.before.flag, f32[4096,128]{1,0:T(8,128)S(1)} %get-tuple-element.47.w_ref.w_in, f32[4096,128]{1,0:T(8,128)} %get-tuple-element.56.g_in, f32[768,128]{1,0:T(8,128)S(1)} %collective-permute-done.arrived.chain.forward, ...), custom_call_target="tpu_custom_call" | custom-call | flops 1 | bytes 1 | tf_op jit(solution)/shard_map/inner/pallas_call | solution.py:596
  24.6 0.3 collective-permute-done.2.arrived.chain.backward
  24.9 0.1 edges.8
  25.0 0.5 collective-permute-start.5
  25.6 8.1 %collective-permute-done.6.arrived.chain.forward = f32[768,128]{1,0:T(8,128)S(1)} collective-permute-done((f32[768,128]{1,0:T(8,128)S(1)}, f32[768,128]{1,0:T(8,128)S(1)}, u32[]{:S(2)}, u32[]{:S(2)}) %collective-permute-start.6) | collective-permute-done | bytes 393248 | tf_op jit(solution)/shard_map/ppermute | solution.py:611
  33.6 0.8 %edges.9 = (f32[768,128]{1,0:T(8,128)S(1)}, f32[4096,128]{1,0:T(8,128)}, f32[768,128]{1,0:T(8,128)S(1)}) custom-call(s32[8,128]{1,0:T(8,128)S(1)} %get-tuple-element.41.before.flag, s32[8,128]{1,0:T(8,128)S(1)} %seen.11, f32[4096,128]{1,0:T(8,128)S(1)} %get-tuple-element.57.w_ref.w_in, ...), custom_call_target="tpu_custom_call", output_to_operand_aliasing={{0}: (14, {}), {1}: (15, {})} | custom-call | flops 1 | bytes 1 | tf_op jit(solution)/shard_map/edges/pallas_call | solution.py:596
  34.5 0.1 collective-permute-start.7
  34.6 1.6 %collective-permute-start.9 = (f32[768,128]{1,0:T(8,128)S(1)}, f32[768,128]{1,0:T(8,128)S(1)}, u32[]{:S(2)}, u32[]{:S(2)}) collective-permute-start(f32[768,128]{1,0:T(8,128)S(1)} %get-tuple-element.69), channel_id=1, source_target_pairs={{0,127},{1,0},{2,1},{3,2},{4,3},{5,4},{6,5},{7,6},{8,7},{9,8},{10,... | collective-permute-start | bytes 1179656 | tf_op jit(solution)/shard_map/ppermute | solution.py:611
  36.2 3.1 %inner.4 = (f32[4096,128]{1,0:T(8,128)S(1)}, f32[4096,128]{1,0:T(8,128)S(1)}) custom-call(s32[8,128]{1,0:T(8,128)S(1)} %get-tuple-element.41.before.flag, f32[4096,128]{1,0:T(8,128)S(1)} %get-tuple-element.57.w_ref.w_in, f32[4096,128]{1,0:T(8,128)} %get-tuple-element.64.g_in, f32[768,128]{1,0:T(8,128)S(1)} %collective-permute-done.6.arrived.chain.forward, ...), custom_call_target="tpu_custom_call" | custom-call | flops 1 | bytes 1 | tf_op jit(solution)/shard_map/inner/pallas_call | solution.py:596
  39.4 0.8 %edges.10 = (f32[768,128]{1,0:T(8,128)S(1)}, f32[4096,128]{1,0:T(8,128)}, f32[768,128]{1,0:T(8,128)S(1)}) custom-call(s32[8,128]{1,0:T(8,128)S(1)} %get-tuple-element.41.before.flag, s32[8,128]{1,0:T(8,128)S(1)} %seen.10, f32[4096,128]{1,0:T(8,128)S(1)} %get-tuple-element.65.w_ref.w_in, f32[768,128]{1,0:T(8,128)S(1)} %collective-permute-done.5.arrived.chain.forward, ...), custom_call_target="tpu_custom_call" | custom-call | flops 1 | bytes 1 | tf_op jit(solution)/shard_map/edges/pallas_call | solution.py:596
  40.2 0.1 collective-permute-start.8
  40.3 1.2 %collective-permute-done.9.arrived.chain.backward = f32[768,128]{1,0:T(8,128)S(1)} collective-permute-done((f32[768,128]{1,0:T(8,128)S(1)}, f32[768,128]{1,0:T(8,128)S(1)}, u32[]{:S(2)}, u32[]{:S(2)}) %collective-permute-start.9) | collective-permute-done | bytes 393248 | tf_op jit(solution)/shard_map/ppermute | solution.py:611
  41.5 0.1 edges.11
  41.6 1.5 %collective-permute-start.10 = (f32[768,128]{1,0:T(8,128)S(1)}, f32[768,128]{1,0:T(8,128)S(1)}, u32[]{:S(2)}, u32[]{:S(2)}) collective-permute-start(f32[768,128]{1,0:T(8,128)S(1)} %get-tuple-element.74), channel_id=1, source_target_pairs={{0,1},{1,2},{2,3},{3,4},{4,5},{5,6},{6,7},{7,8},{8,9},{9,10},{10,1... | collective-permute-start | bytes 1179656 | tf_op jit(solution)/shard_map/ppermute | solution.py:611
  43.1 0.1 collective-permute-start.11
  43.2 2.0 %inner.5 = (f32[4096,128]{1,0:T(8,128)S(1)}, f32[4096,128]{1,0:T(8,128)S(1)}) custom-call(s32[8,128]{1,0:T(8,128)S(1)} %get-tuple-element.41.before.flag, f32[4096,128]{1,0:T(8,128)S(1)} %get-tuple-element.65.w_ref.w_in, f32[4096,128]{1,0:T(8,128)} %get-tuple-element.72.g_in, f32[768,128]{1,0:T(8,128)S(1)} %collective-permute-done.5.arrived.chain.forward, ...), custom_call_target="tpu_custom_call" | custom-call | flops 1 | bytes 1 | tf_op jit(solution)/shard_map/inner/pallas_call | solution.py:596
  45.2 0.5 collective-permute-done.8.arrived.backward
  45.7 9.4 %collective-permute-done.10.forward = f32[768,128]{1,0:T(8,128)S(1)} collective-permute-done((f32[768,128]{1,0:T(8,128)S(1)}, f32[768,128]{1,0:T(8,128)S(1)}, u32[]{:S(2)}, u32[]{:S(2)}) %collective-permute-start.10) | collective-permute-done | bytes 393248 | tf_op jit(solution)/shard_map/ppermute | solution.py:611
  55.2 3.2 %last.1 = f32[4096,128]{1,0:T(8,128)} custom-call(s32[8,128]{1,0:T(8,128)S(1)} %get-tuple-element.41.before.flag, s32[8,128]{1,0:T(8,128)S(1)} %seen.12, s32[2,768]{1,0:T(2,128)S(1)} %copy-done, f32[4096,128]{1,0:T(8,128)S(1)} %get-tuple-element.73.w_in, f32[768,128]{1,0:T(8,128)S(1)} %collective-permute-done.10.forward, ...), custom_call_target="tpu_custom_call" | custom-call | flops 1 | bytes 1 | tf_op jit(solution)/shard_map/last/pallas_call | solution.py:596
  (17 shorter events, 0.0 us)
Async XLA Ops:
  0.0 14.1 %copy-start.2 = (f32[4096]{0:T(1024)S(1)}, f32[4096]{0:T(1024)}, u32[]{:S(2)}) copy-start(f32[4096]{0:T(1024)} %param.9) | copy-start | bytes 49156
  5.1 13.7 %collective-permute-start = (f32[768,128]{1,0:T(8,128)S(1)}, f32[768,128]{1,0:T(8,128)S(1)}, u32[]{:S(2)}, u32[]{:S(2)}) collective-permute-start(f32[768,128]{1,0:T(8,128)S(1)} %get-tuple-element.42), channel_id=1, source_target_pairs={{0,1},{1,2},{2,3},{3,4},{4,5},{5,6},{6,7},{7,8},{8,9},{9,10},{10,1... | collective-permute-start | bytes 1179656 | tf_op jit(solution)/shard_map/ppermute | solution.py:611
  5.1 13.7 %collective-permute-start.1 = (f32[768,128]{1,0:T(8,128)S(1)}, f32[768,128]{1,0:T(8,128)S(1)}, u32[]{:S(2)}, u32[]{:S(2)}) collective-permute-start(f32[768,128]{1,0:T(8,128)S(1)} %get-tuple-element.48), channel_id=1, source_target_pairs={{0,1},{1,0},{2,3},{3,2},{4,5},{5,4},{6,7},{7,6},{8,9},{9,8},{10,11... | collective-permute-start | bytes 1179656 | tf_op jit(solution)/shard_map/ppermute | solution.py:616
  7.2 12.4 %collective-permute-start.3 = (f32[768,128]{1,0:T(8,128)S(1)}, f32[768,128]{1,0:T(8,128)S(1)}, u32[]{:S(2)}, u32[]{:S(2)}) collective-permute-start(f32[768,128]{1,0:T(8,128)S(1)} %get-tuple-element.53), channel_id=1, source_target_pairs={{0,127},{1,0},{2,1},{3,2},{4,3},{5,4},{6,5},{7,6},{8,7},{9,8},{10,... | collective-permute-start | bytes 1179656 | tf_op jit(solution)/shard_map/ppermute | solution.py:611
  14.1 4.7 %copy-start.1 = (f32[128]{0:T(128)S(1)}, f32[128]{0:T(128)}, u32[]{:S(2)}) copy-start(f32[128]{0:T(128)} %param.10) | copy-start | bytes 1540
  19.6 5.4 %collective-permute-start.2 = (f32[768,128]{1,0:T(8,128)S(1)}, f32[768,128]{1,0:T(8,128)S(1)}, u32[]{:S(2)}, u32[]{:S(2)}) collective-permute-start(f32[768,128]{1,0:T(8,128)S(1)} %get-tuple-element.52), channel_id=1, source_target_pairs={{0,127},{1,0},{2,1},{3,2},{4,3},{5,4},{6,5},{7,6},{8,7},{9,8},{10,... | collective-permute-start | bytes 1179656 | tf_op jit(solution)/shard_map/ppermute | solution.py:611
  19.8 5.2 %collective-permute-start.4 = (f32[768,128]{1,0:T(8,128)S(1)}, f32[768,128]{1,0:T(8,128)S(1)}, u32[]{:S(2)}, u32[]{:S(2)}) collective-permute-start(f32[768,128]{1,0:T(8,128)S(1)} %get-tuple-element.58), channel_id=1, source_target_pairs={{0,1},{1,0},{2,3},{3,2},{4,5},{5,4},{6,7},{7,6},{8,9},{9,8},{10,11... | collective-permute-start | bytes 1179656 | tf_op jit(solution)/shard_map/ppermute | solution.py:616
  21.0 12.6 %collective-permute-start.6 = (f32[768,128]{1,0:T(8,128)S(1)}, f32[768,128]{1,0:T(8,128)S(1)}, u32[]{:S(2)}, u32[]{:S(2)}) collective-permute-start(f32[768,128]{1,0:T(8,128)S(1)} %get-tuple-element.61), channel_id=1, source_target_pairs={{0,1},{1,2},{2,3},{3,4},{4,5},{5,6},{6,7},{7,8},{8,9},{9,10},{10,1... | collective-permute-start | bytes 1179656 | tf_op jit(solution)/shard_map/ppermute | solution.py:611
  25.0 14.3 %collective-permute-start.5 = (f32[768,128]{1,0:T(8,128)S(1)}, f32[768,128]{1,0:T(8,128)S(1)}, u32[]{:S(2)}, u32[]{:S(2)}) collective-permute-start(f32[768,128]{1,0:T(8,128)S(1)} %get-tuple-element.60), channel_id=1, source_target_pairs={{0,1},{1,2},{2,3},{3,4},{4,5},{5,6},{6,7},{7,8},{8,9},{9,10},{10,1... | collective-permute-start | bytes 1179656 | tf_op jit(solution)/shard_map/ppermute | solution.py:611
  34.5 4.9 %collective-permute-start.7 = (f32[768,128]{1,0:T(8,128)S(1)}, f32[768,128]{1,0:T(8,128)S(1)}, u32[]{:S(2)}, u32[]{:S(2)}) collective-permute-start(f32[768,128]{1,0:T(8,128)S(1)} %get-tuple-element.66), channel_id=1, source_target_pairs={{0,1},{1,0},{2,3},{3,2},{4,5},{5,4},{6,7},{7,6},{8,9},{9,8},{10,11... | collective-permute-start | bytes 1179656 | tf_op jit(solution)/shard_map/ppermute | solution.py:616
  34.6 6.9 %collective-permute-start.9 = (f32[768,128]{1,0:T(8,128)S(1)}, f32[768,128]{1,0:T(8,128)S(1)}, u32[]{:S(2)}, u32[]{:S(2)}) collective-permute-start(f32[768,128]{1,0:T(8,128)S(1)} %get-tuple-element.69), channel_id=1, source_target_pairs={{0,127},{1,0},{2,1},{3,2},{4,3},{5,4},{6,5},{7,6},{8,7},{9,8},{10,... | collective-permute-start | bytes 1179656 | tf_op jit(solution)/shard_map/ppermute | solution.py:611
  40.2 5.5 %collective-permute-start.8 = (f32[768,128]{1,0:T(8,128)S(1)}, f32[768,128]{1,0:T(8,128)S(1)}, u32[]{:S(2)}, u32[]{:S(2)}) collective-permute-start(f32[768,128]{1,0:T(8,128)S(1)} %get-tuple-element.68), channel_id=1, source_target_pairs={{0,127},{1,0},{2,1},{3,2},{4,3},{5,4},{6,5},{7,6},{8,7},{9,8},{10,... | collective-permute-start | bytes 1179656 | tf_op jit(solution)/shard_map/ppermute | solution.py:611
  41.6 13.5 %collective-permute-start.10 = (f32[768,128]{1,0:T(8,128)S(1)}, f32[768,128]{1,0:T(8,128)S(1)}, u32[]{:S(2)}, u32[]{:S(2)}) collective-permute-start(f32[768,128]{1,0:T(8,128)S(1)} %get-tuple-element.74), channel_id=1, source_target_pairs={{0,1},{1,2},{2,3},{3,4},{4,5},{5,6},{6,7},{7,8},{8,9},{9,10},{10,1... | collective-permute-start | bytes 1179656 | tf_op jit(solution)/shard_map/ppermute | solution.py:611
  43.1 12.0 %collective-permute-start.11 = (f32[768,128]{1,0:T(8,128)S(1)}, f32[768,128]{1,0:T(8,128)S(1)}, u32[]{:S(2)}, u32[]{:S(2)}) collective-permute-start(f32[768,128]{1,0:T(8,128)S(1)} %get-tuple-element.75), channel_id=1, source_target_pairs={{0,1},{1,0},{2,3},{3,2},{4,5},{5,4},{6,7},{7,6},{8,9},{9,8},{10,11... | collective-permute-start | bytes 1179656 | tf_op jit(solution)/shard_map/ppermute | solution.py:616
  43.2 11.9 %copy-start = (s32[2,768]{1,0:T(2,128)S(1)}, s32[2,768]{1,0:T(2,128)}, u32[]{:S(2)}) copy-start(s32[2,768]{1,0:T(2,128)} %order_s.1) | copy-start | bytes 18436

commit v4 on v3

--- a/solution.py
+++ b/solution.py
@@ -459,7 +459,7 @@
         general_messages(g_ref, behind_ref, ahead_ref, send_any, send_s)
 
 
-def inner_kernel(kind, flag, w_in, g_in, forward, backward, pair, mx_ref, my_ref, im_ref, u_in, visc, recv_any, u_ref, w_ref, s_ref, recv_s):
+def inner_kernel(kind, flag, w_in, g_in, forward, backward, pair_even, pair_odd, mx_ref, my_ref, im_ref, u_in, visc, recv_any, u_ref, w_ref, s_ref, recv_s):
     ok = flag[0, 0] == 1
     rate = visc[...]
 
@@ -486,7 +486,7 @@
                     set_plane(u_ref, q, t, plane(u_in, q, t))
             return carry
 
-        for odd, left, right in ((0, forward, pair), (1, pair, backward)):
+        for odd, left, right in ((0, forward, pair_even), (1, pair_odd, backward)):
             @pl.when(flag[1, 0] == odd)
             def _():
                 lax.fori_loop(0, STEPS, functools.partial(complete, left, right), 0, unroll=2)
@@ -512,7 +512,7 @@
         pltpu.sync_copy(g_in, w_ref)
         if kind == 1:
             s_ref[...] = w_in[...]
-            for odd, left, right in ((0, forward, pair), (1, pair, backward)):
+            for odd, left, right in ((0, forward, pair_even), (1, pair_odd, backward)):
                 @pl.when(flag[1, 0] == odd)
                 def _():
                     general_receive(s_ref, left, right, recv_any, recv_s)
@@ -522,7 +522,7 @@
             u_ref[...] = u_in[...]
 
 
-def last_kernel(flag, seen, order_s, w_in, forward, backward, pair, im_ref, u_in, visc, recv_any, out, raw, v_ref, recv_s, sem):
+def last_kernel(flag, seen, order_s, w_in, forward, backward, pair_even, pair_odd, im_ref, u_in, visc, recv_any, out, raw, v_ref, recv_s, sem):
     ok = flag[0, 0] == 1
     rate = visc[...]
 
@@ -547,7 +547,7 @@
             leave(t, x)
             return carry
 
-        for odd, left, right in ((0, forward, pair), (1, pair, backward)):
+        for odd, left, right in ((0, forward, pair_even), (1, pair_odd, backward)):
             @pl.when(flag[1, 0] == odd)
             def _():
                 lax.fori_loop(0, STEPS, functools.partial(body, left, right), 0, unroll=2)
@@ -555,7 +555,7 @@
     @pl.when(jnp.logical_not(ok))
     def _():
         v_ref[...] = w_in[...]
-        for odd, left, right in ((0, forward, pair), (1, pair, backward)):
+        for odd, left, right in ((0, forward, pair_even), (1, pair_odd, backward)):
             @pl.when(flag[1, 0] == odd)
             def _():
                 general_receive(v_ref, left, right, recv_any, recv_s)
@@ -642,37 +642,37 @@
         [FIELD, jax.ShapeDtypeStruct((12 * ELEMS, COLS), jnp.float32), FIELD],
         [VM] * 3, [TABLE_V], WORK, 6 * SIZE, "prepare",
     )
+    came = [forward, backward]
+    pairs = [crossing, crossing]
     for step in range(2 * SUBCYCLES - 1):
         updates = step % 2 == 1
         chained = ()
-        came = (forward, backward, crossing)
+        before = flag
+        arrived, crossings = list(came), list(pairs)
         for odd in ((0, 1) if step % 2 == 0 else (1, 0)):
-            seen = call(seen_kernel, (came[odd], chained[0] if chained else flag), [FREE, FREE], WORD, VM, [], 0, 0, "seen")
-            pair, g, chain = call(
+            seen = call(seen_kernel, (arrived[odd], before), [FREE, FREE], WORD, VM, [], 0, 0, "seen")
+            before, g, chain = call(
                 functools.partial(edge_kernel, updates, odd),
-                (flag, seen, w, came[odd], crossing, mx, my, im, kx, u, visc, partner, send_rows, recv_rows) + chained,
-                [VM, FREE] + [VM] * 9 + [HB] * 3 + [FREE, HB][:len(chained)], [MESSAGE, HELD, MESSAGE], [VM, HB, VM],
+                (flag, seen, w, arrived[odd], crossings[odd], mx, my, im, kx, u, visc, partner, send_rows, recv_rows) + chained,
+                [VM, FREE] + [VM] * 9 + [HB] * 3 + [HB] * len(chained), [MESSAGE, HELD, MESSAGE], [VM, HB, VM],
                 [SCRATCH, SCRATCH, PARTNER_S, SEND_S, RECV_S], WORK // 3, 2 * SIZE, "edges",
-                {14: 0, 15: 1} if chained else {},
+                {14: 1} if chained else {},
             )
-            chained = (pair, g)
-            if odd:
-                forward = moved(chain, 1)
-            else:
-                backward = moved(chain, -1)
-        crossing = crossed(pair)
+            chained = (g,)
+            came[1 - odd] = moved(chain, 1 if odd else -1)
+            pairs[1 - odd] = crossed(before)
         kind = 1 if updates else 2 if step == 2 * SUBCYCLES - 2 else 0
         u, w = call(
             functools.partial(inner_kernel, kind),
-            (flag, w, g, *came, mx, my, im, u, visc, recv_rows),
-            [VM, VM, HB] + [VM] * 8 + [HB], [FIELD, FIELD], [VM] * 2,
+            (flag, w, g, *arrived, *crossings, mx, my, im, u, visc, recv_rows),
+            [VM, VM, HB] + [VM] * 9 + [HB], [FIELD, FIELD], [VM] * 2,
             [SCRATCH, RECV_S], WORK * 2, 8 * SIZE, "inner",
         )
-    seen = call(seen_kernel, (backward, flag), [FREE, FREE], WORD, VM, [], 0, 0, "seen")
+    seen = call(seen_kernel, (came[1], flag), [FREE, FREE], WORD, VM, [], 0, 0, "seen")
     return call(
         last_kernel,
-        (flag, seen, send_rows, w, forward, backward, crossing, im, u, visc, recv_rows),
-        [VM, FREE, SM] + [VM] * 7 + [HB], FIELD, HB,
+        (flag, seen, send_rows, w, *came, *pairs, im, u, visc, recv_rows),
+        [VM, FREE, SM] + [VM] * 8 + [HB], FIELD, HB,
         [SCRATCH, SCRATCH, RECV_S, pltpu.SemaphoreType.DMA], WORK // 8, 4 * SIZE, "last",
     )
 

time: 58.5 us -> 56.2 us (0.961)
  waiting for transfers between devices: 20.8 us -> 18.9 us
    ppermute x8, waiting for transfers between devices: 20.8 us -> 18.9 us  [moved(): lax.ppermute(value, 'elem', [(i, (i + by) % size) for i in range(size)])]
    ppermute x8, starting transfers between devices: 10.8 us -> 10.2 us  [moved(): lax.ppermute(value, 'elem', [(i, (i + by) % size) for i in range(size)])]
    ppermute x4 -> x7, starting transfers between devices: 3.51 us -> 3.79 us  [crossed(): lax.ppermute(value, 'elem', [(i, i + 1 - 2 * (i % 2)) for i in range(size)])]
  transfers between devices with their start and end apart: 12 -> 15, of which waited for: 6 -> 6; matrix products, arithmetic and copies ran while one was open for 0% -> 0% of each run, Pallas kernels for 25% -> 26%
where the time goes in v4:
time: 56.2 us; the launch traced here: 56.1 us
  Pallas kernels  23 us (41%)
  waiting for transfers between devices  18.9 us (34%)
  starting transfers between devices  14 us (25%)
    pallas_call x19, Pallas kernels, call(): pl.pallas_call(kernel, out_shape=shapes, in_specs=specs, out_specs=outs,...  23 us
    ppermute x8, waiting for transfers between devices, moved(): lax.ppermute(value, 'elem', [(i, (i + by) % size) for i in range(size)])  18.9 us
    ppermute x8, starting transfers between devices, moved(): lax.ppermute(value, 'elem', [(i, (i + by) % size) for i in range(size)])  10.2 us
    ppermute x7, starting transfers between devices, crossed(): lax.ppermute(value, 'elem', [(i, i + 1 - 2 * (i % 2)) for i in range(size)])  3.79 us
  transfers between devices with their start and end apart: 15, of which 6 were waited for; matrix products, arithmetic and copies ran while one was open for 0% of the time, Pallas kernels for 26%

profile of v4, /device:TPU:0, one launch (start us, length us, event | category | flops | bytes accessed | tf_op | source)
XLA Modules:
  0.0 56.1 jit_solution(11408080123117038144)
XLA Ops:
  0.0 5.0 %first.1 = (f32[4096,128]{1,0:T(8,128)S(1)}, f32[4096,128]{1,0:T(8,128)S(1)}, f32[4096,128]{1,0:T(8,128)S(1)}, f32[4096,128]{1,0:T(8,128)S(1)}, f32[256,128]{1,0...) custom-call(f32[4096,128]{1,0:T(8,128)} %prog.1, ...), custom_call_target="tpu_custom_call" | custom-call | flops 1 | bytes 1 | tf_op jit(solution)/shard_map/first/pallas_call | solution.py:596
  5.1 0.1 collective-permute-start
  5.1 2.1 %collective-permute-start.1 = (f32[768,128]{1,0:T(8,128)S(1)}, f32[768,128]{1,0:T(8,128)S(1)}, u32[]{:S(2)}, u32[]{:S(2)}) collective-permute-start(f32[768,128]{1,0:T(8,128)S(1)} %get-tuple-element.48), channel_id=1, source_target_pairs={{0,1},{1,0},{2,3},{3,2},{4,5},{5,4},{6,7},{7,6},{8,9},{9,8},{10,11... | collective-permute-start | bytes 1179656 | tf_op jit(solution)/shard_map/ppermute | solution.py:616
  7.2 6.9 %collective-permute-start.3 = (f32[768,128]{1,0:T(8,128)S(1)}, f32[768,128]{1,0:T(8,128)S(1)}, u32[]{:S(2)}, u32[]{:S(2)}) collective-permute-start(f32[768,128]{1,0:T(8,128)S(1)} %get-tuple-element.53), channel_id=1, source_target_pairs={{0,127},{1,0},{2,1},{3,2},{4,3},{5,4},{6,5},{7,6},{8,7},{9,8},{10,... | collective-permute-start | bytes 1179656 | tf_op jit(solution)/shard_map/ppermute | solution.py:611
  14.1 3.5 %prepare.1 = (f32[4096,128]{1,0:T(8,128)S(1)}, f32[3072,128]{1,0:T(8,128)S(1)}, f32[4096,128]{1,0:T(8,128)S(1)}) custom-call(s32[8,128]{1,0:T(8,128)S(1)} %get-tuple-element.41.before.flag, f32[4096,128]{1,0:T(8,128)S(1)} %get-tuple-element.43.s_in, f32[4096,128]{1,0:T(8,128)S(1)} %get-tuple-element.44.mx_ref, f32[4096,128]{1,0:T(8,128)S(1)} %get-tuple-element.45.my_ref, ...), custom_call_target="tpu_custom_call" | custom-call | flops 1 | bytes 1 | tf_op jit(solution)/shard_map/prepare/pallas_call | solution.py:596
  17.6 1.2 %collective-permute-done.arrived.chain.forward = f32[768,128]{1,0:T(8,128)S(1)} collective-permute-done((f32[768,128]{1,0:T(8,128)S(1)}, f32[768,128]{1,0:T(8,128)S(1)}, u32[]{:S(2)}, u32[]{:S(2)}) %collective-permute-start) | collective-permute-done | bytes 393248 | tf_op jit(solution)/shard_map/ppermute | solution.py:611
  18.8 0.8 %edges.6 = (f32[768,128]{1,0:T(8,128)S(1)}, f32[4096,128]{1,0:T(8,128)}, f32[768,128]{1,0:T(8,128)S(1)}) custom-call(s32[8,128]{1,0:T(8,128)S(1)} %get-tuple-element.41.before.flag, s32[8,128]{1,0:T(8,128)S(1)} %seen.7, f32[4096,128]{1,0:T(8,128)S(1)} %get-tuple-element.47.w_ref.w_in, f32[768,128]{1,0:T(8,128)S(1)} %collective-permute-done.arrived.chain.forward, ...), custom_call_target="tpu_custom_call" | custom-call | flops 1 | bytes 1 | tf_op jit(solution)/shard_map/edges/pallas_call | solution.py:596
  19.6 0.1 collective-permute-start.2
  19.7 0.5 collective-permute-start.4
  20.2 0.1 edges.7
  20.3 0.8 %collective-permute-start.6 = (f32[768,128]{1,0:T(8,128)S(1)}, f32[768,128]{1,0:T(8,128)S(1)}, u32[]{:S(2)}, u32[]{:S(2)}) collective-permute-start(f32[768,128]{1,0:T(8,128)S(1)} %get-tuple-element.60), channel_id=1, source_target_pairs={{0,1},{1,2},{2,3},{3,4},{4,5},{5,6},{6,7},{7,8},{8,9},{9,10},{10,1... | collective-permute-start | bytes 1179656 | tf_op jit(solution)/shard_map/ppermute | solution.py:611
  21.1 0.1 collective-permute-start.7
  21.2 3.5 %inner.3 = (f32[4096,128]{1,0:T(8,128)S(1)}, f32[4096,128]{1,0:T(8,128)S(1)}) custom-call(s32[8,128]{1,0:T(8,128)S(1)} %get-tuple-element.41.before.flag, f32[4096,128]{1,0:T(8,128)S(1)} %get-tuple-element.47.w_ref.w_in, f32[4096,128]{1,0:T(8,128)} %get-tuple-element.56.g_in, f32[768,128]{1,0:T(8,128)S(1)} %collective-permute-done.arrived.chain.forward, ...), custom_call_target="tpu_custom_call" | custom-call | flops 1 | bytes 1 | tf_op jit(solution)/shard_map/inner/pallas_call | solution.py:596
  24.7 0.3 collective-permute-done.2.arrived.chain.backward
  25.0 0.1 edges.8
  25.0 1.0 %collective-permute-start.5 = (f32[768,128]{1,0:T(8,128)S(1)}, f32[768,128]{1,0:T(8,128)S(1)}, u32[]{:S(2)}, u32[]{:S(2)}) collective-permute-start(f32[768,128]{1,0:T(8,128)S(1)} %get-tuple-element.59), channel_id=1, source_target_pairs={{0,1},{1,2},{2,3},{3,4},{4,5},{5,6},{6,7},{7,8},{8,9},{9,10},{10,1... | collective-permute-start | bytes 1179656 | tf_op jit(solution)/shard_map/ppermute | solution.py:611
  26.1 0.1 collective-permute-start.8
  26.2 6.9 %collective-permute-done.6.arrived.chain.forward = f32[768,128]{1,0:T(8,128)S(1)} collective-permute-done((f32[768,128]{1,0:T(8,128)S(1)}, f32[768,128]{1,0:T(8,128)S(1)}, u32[]{:S(2)}, u32[]{:S(2)}) %collective-permute-start.6) | collective-permute-done | bytes 393248 | tf_op jit(solution)/shard_map/ppermute | solution.py:611
  33.0 0.8 %edges.9 = (f32[768,128]{1,0:T(8,128)S(1)}, f32[4096,128]{1,0:T(8,128)}, f32[768,128]{1,0:T(8,128)S(1)}) custom-call(s32[8,128]{1,0:T(8,128)S(1)} %get-tuple-element.41.before.flag, s32[8,128]{1,0:T(8,128)S(1)} %seen.11, f32[4096,128]{1,0:T(8,128)S(1)} %get-tuple-element.57.w_ref.w_in, ...), custom_call_target="tpu_custom_call", output_to_operand_aliasing={{1}: (14, {})} | custom-call | flops 1 | bytes 1 | tf_op jit(solution)/shard_map/edges/pallas_call | solution.py:596
  33.9 0.1 collective-permute-start.10
  34.0 0.5 collective-permute-start.11
  34.5 3.1 %inner.4 = (f32[4096,128]{1,0:T(8,128)S(1)}, f32[4096,128]{1,0:T(8,128)S(1)}) custom-call(s32[8,128]{1,0:T(8,128)S(1)} %get-tuple-element.41.before.flag, f32[4096,128]{1,0:T(8,128)S(1)} %get-tuple-element.57.w_ref.w_in, f32[4096,128]{1,0:T(8,128)} %get-tuple-element.64.g_in, f32[768,128]{1,0:T(8,128)S(1)} %collective-permute-done.6.arrived.chain.forward, ...), custom_call_target="tpu_custom_call" | custom-call | flops 1 | bytes 1 | tf_op jit(solution)/shard_map/inner/pallas_call | solution.py:596
  37.6 1.1 %collective-permute-done.5.arrived.chain.forward = f32[768,128]{1,0:T(8,128)S(1)} collective-permute-done((f32[768,128]{1,0:T(8,128)S(1)}, f32[768,128]{1,0:T(8,128)S(1)}, u32[]{:S(2)}, u32[]{:S(2)}) %collective-permute-start.5) | collective-permute-done | bytes 393248 | tf_op jit(solution)/shard_map/ppermute | solution.py:611
  38.7 0.8 %edges.10 = (f32[768,128]{1,0:T(8,128)S(1)}, f32[4096,128]{1,0:T(8,128)}, f32[768,128]{1,0:T(8,128)S(1)}) custom-call(s32[8,128]{1,0:T(8,128)S(1)} %get-tuple-element.41.before.flag, s32[8,128]{1,0:T(8,128)S(1)} %seen.10, f32[4096,128]{1,0:T(8,128)S(1)} %get-tuple-element.65.w_ref.w_in, f32[768,128]{1,0:T(8,128)S(1)} %collective-permute-done.5.arrived.chain.forward, ...), custom_call_target="tpu_custom_call" | custom-call | flops 1 | bytes 1 | tf_op jit(solution)/shard_map/edges/pallas_call | solution.py:596
  39.6 0.1 edges.11
  39.7 1.2 %collective-permute-start.12 = (f32[768,128]{1,0:T(8,128)S(1)}, f32[768,128]{1,0:T(8,128)S(1)}, u32[]{:S(2)}, u32[]{:S(2)}) collective-permute-start(f32[768,128]{1,0:T(8,128)S(1)} %get-tuple-element.74), channel_id=1, source_target_pairs={{0,1},{1,2},{2,3},{3,4},{4,5},{5,6},{6,7},{7,8},{8,9},{9,10},{10,1... | collective-permute-start | bytes 1179656 | tf_op jit(solution)/shard_map/ppermute | solution.py:611
  40.9 0.1 collective-permute-start.13
  41.0 0.4 collective-permute-start.14
  41.4 2.0 %inner.5 = (f32[4096,128]{1,0:T(8,128)S(1)}, f32[4096,128]{1,0:T(8,128)S(1)}) custom-call(s32[8,128]{1,0:T(8,128)S(1)} %get-tuple-element.41.before.flag, f32[4096,128]{1,0:T(8,128)S(1)} %get-tuple-element.65.w_ref.w_in, f32[4096,128]{1,0:T(8,128)} %get-tuple-element.72.g_in, f32[768,128]{1,0:T(8,128)S(1)} %collective-permute-done.5.arrived.chain.forward, ...), custom_call_target="tpu_custom_call" | custom-call | flops 1 | bytes 1 | tf_op jit(solution)/shard_map/inner/pallas_call | solution.py:596
  43.4 1.4 %collective-permute-done.9.arrived.backward = f32[768,128]{1,0:T(8,128)S(1)} collective-permute-done((f32[768,128]{1,0:T(8,128)S(1)}, f32[768,128]{1,0:T(8,128)S(1)}, u32[]{:S(2)}, u32[]{:S(2)}) %collective-permute-start.9) | collective-permute-done | bytes 393248 | tf_op jit(solution)/shard_map/ppermute | solution.py:611
  44.8 8.1 %collective-permute-done.12.forward = f32[768,128]{1,0:T(8,128)S(1)} collective-permute-done((f32[768,128]{1,0:T(8,128)S(1)}, f32[768,128]{1,0:T(8,128)S(1)}, u32[]{:S(2)}, u32[]{:S(2)}) %collective-permute-start.12) | collective-permute-done | bytes 393248 | tf_op jit(solution)/shard_map/ppermute | solution.py:611
  52.9 3.2 %last.1 = f32[4096,128]{1,0:T(8,128)} custom-call(s32[8,128]{1,0:T(8,128)S(1)} %get-tuple-element.41.before.flag, s32[8,128]{1,0:T(8,128)S(1)} %seen.12, s32[2,768]{1,0:T(2,128)S(1)} %copy-done, f32[4096,128]{1,0:T(8,128)S(1)} %get-tuple-element.73.w_in, f32[768,128]{1,0:T(8,128)S(1)} %collective-permute-done.12.forward, ...), custom_call_target="tpu_custom_call" | custom-call | flops 1 | bytes 1 | tf_op jit(solution)/shard_map/last/pallas_call | solution.py:596
  (23 shorter events, 0.1 us)
Async XLA Ops:
  0.0 14.1 %copy-start.2 = (f32[4096]{0:T(1024)S(1)}, f32[4096]{0:T(1024)}, u32[]{:S(2)}) copy-start(f32[4096]{0:T(1024)} %param.9) | copy-start | bytes 49156
  5.1 13.7 %collective-permute-start = (f32[768,128]{1,0:T(8,128)S(1)}, f32[768,128]{1,0:T(8,128)S(1)}, u32[]{:S(2)}, u32[]{:S(2)}) collective-permute-start(f32[768,128]{1,0:T(8,128)S(1)} %get-tuple-element.42), channel_id=1, source_target_pairs={{0,1},{1,2},{2,3},{3,4},{4,5},{5,6},{6,7},{7,8},{8,9},{9,10},{10,1... | collective-permute-start | bytes 1179656 | tf_op jit(solution)/shard_map/ppermute | solution.py:611
  5.1 13.7 %collective-permute-start.1 = (f32[768,128]{1,0:T(8,128)S(1)}, f32[768,128]{1,0:T(8,128)S(1)}, u32[]{:S(2)}, u32[]{:S(2)}) collective-permute-start(f32[768,128]{1,0:T(8,128)S(1)} %get-tuple-element.48), channel_id=1, source_target_pairs={{0,1},{1,0},{2,3},{3,2},{4,5},{5,4},{6,7},{7,6},{8,9},{9,8},{10,11... | collective-permute-start | bytes 1179656 | tf_op jit(solution)/shard_map/ppermute | solution.py:616
  7.2 12.9 %collective-permute-start.3 = (f32[768,128]{1,0:T(8,128)S(1)}, f32[768,128]{1,0:T(8,128)S(1)}, u32[]{:S(2)}, u32[]{:S(2)}) collective-permute-start(f32[768,128]{1,0:T(8,128)S(1)} %get-tuple-element.53), channel_id=1, source_target_pairs={{0,127},{1,0},{2,1},{3,2},{4,3},{5,4},{6,5},{7,6},{8,7},{9,8},{10,... | collective-permute-start | bytes 1179656 | tf_op jit(solution)/shard_map/ppermute | solution.py:611
  14.1 4.7 %copy-start.1 = (f32[128]{0:T(128)S(1)}, f32[128]{0:T(128)}, u32[]{:S(2)}) copy-start(f32[128]{0:T(128)} %param.10) | copy-start | bytes 1540
  19.6 5.4 %collective-permute-start.2 = (f32[768,128]{1,0:T(8,128)S(1)}, f32[768,128]{1,0:T(8,128)S(1)}, u32[]{:S(2)}, u32[]{:S(2)}) collective-permute-start(f32[768,128]{1,0:T(8,128)S(1)} %get-tuple-element.52), channel_id=1, source_target_pairs={{0,127},{1,0},{2,1},{3,2},{4,3},{5,4},{6,5},{7,6},{8,7},{9,8},{10,... | collective-permute-start | bytes 1179656 | tf_op jit(solution)/shard_map/ppermute | solution.py:611
  19.7 5.3 %collective-permute-start.4 = (f32[768,128]{1,0:T(8,128)S(1)}, f32[768,128]{1,0:T(8,128)S(1)}, u32[]{:S(2)}, u32[]{:S(2)}) collective-permute-start(f32[768,128]{1,0:T(8,128)S(1)} %get-tuple-element.54.before), channel_id=1, source_target_pairs={{0,1},{1,0},{2,3},{3,2},{4,5},{5,4},{6,7},{7,6},{8,9},{9,8},{10,11... | collective-permute-start | bytes 1179656 | tf_op jit(solution)/shard_map/ppermute | solution.py:616
  20.3 12.8 %collective-permute-start.6 = (f32[768,128]{1,0:T(8,128)S(1)}, f32[768,128]{1,0:T(8,128)S(1)}, u32[]{:S(2)}, u32[]{:S(2)}) collective-permute-start(f32[768,128]{1,0:T(8,128)S(1)} %get-tuple-element.60), channel_id=1, source_target_pairs={{0,1},{1,2},{2,3},{3,4},{4,5},{5,6},{6,7},{7,8},{8,9},{9,10},{10,1... | collective-permute-start | bytes 1179656 | tf_op jit(solution)/shard_map/ppermute | solution.py:611
  21.1 11.9 %collective-permute-start.7 = (f32[768,128]{1,0:T(8,128)S(1)}, f32[768,128]{1,0:T(8,128)S(1)}, u32[]{:S(2)}, u32[]{:S(2)}) collective-permute-start(f32[768,128]{1,0:T(8,128)S(1)} %get-tuple-element.62), channel_id=1, source_target_pairs={{0,1},{1,0},{2,3},{3,2},{4,5},{5,4},{6,7},{7,6},{8,9},{9,8},{10,11... | collective-permute-start | bytes 1179656 | tf_op jit(solution)/shard_map/ppermute | solution.py:616
  25.0 13.6 %collective-permute-start.5 = (f32[768,128]{1,0:T(8,128)S(1)}, f32[768,128]{1,0:T(8,128)S(1)}, u32[]{:S(2)}, u32[]{:S(2)}) collective-permute-start(f32[768,128]{1,0:T(8,128)S(1)} %get-tuple-element.59), channel_id=1, source_target_pairs={{0,1},{1,2},{2,3},{3,4},{4,5},{5,6},{6,7},{7,8},{8,9},{9,10},{10,1... | collective-permute-start | bytes 1179656 | tf_op jit(solution)/shard_map/ppermute | solution.py:611
  26.1 12.6 %collective-permute-start.8 = (f32[768,128]{1,0:T(8,128)S(1)}, f32[768,128]{1,0:T(8,128)S(1)}, u32[]{:S(2)}, u32[]{:S(2)}) collective-permute-start(f32[768,128]{1,0:T(8,128)S(1)} %get-tuple-element.61.before), channel_id=1, source_target_pairs={{0,1},{1,0},{2,3},{3,2},{4,5},{5,4},{6,7},{7,6},{8,9},{9,8},{10,11... | collective-permute-start | bytes 1179656 | tf_op jit(solution)/shard_map/ppermute | solution.py:616
  33.9 5.7 %collective-permute-start.10 = (f32[768,128]{1,0:T(8,128)S(1)}, f32[768,128]{1,0:T(8,128)S(1)}, u32[]{:S(2)}, u32[]{:S(2)}) collective-permute-start(f32[768,128]{1,0:T(8,128)S(1)} %get-tuple-element.68), channel_id=1, source_target_pairs={{0,127},{1,0},{2,1},{3,2},{4,3},{5,4},{6,5},{7,6},{8,7},{9,8},{10,... | collective-permute-start | bytes 1179656 | tf_op jit(solution)/shard_map/ppermute | solution.py:611
  34.0 5.6 %collective-permute-start.11 = (f32[768,128]{1,0:T(8,128)S(1)}, f32[768,128]{1,0:T(8,128)S(1)}, u32[]{:S(2)}, u32[]{:S(2)}) collective-permute-start(f32[768,128]{1,0:T(8,128)S(1)} %get-tuple-element.70), channel_id=1, source_target_pairs={{0,1},{1,0},{2,3},{3,2},{4,5},{5,4},{6,7},{7,6},{8,9},{9,8},{10,11... | collective-permute-start | bytes 1179656 | tf_op jit(solution)/shard_map/ppermute | solution.py:616
  39.5 5.4 %collective-permute-start.9 = (f32[768,128]{1,0:T(8,128)S(1)}, f32[768,128]{1,0:T(8,128)S(1)}, u32[]{:S(2)}, u32[]{:S(2)}) collective-permute-start(f32[768,128]{1,0:T(8,128)S(1)} %get-tuple-element.67), channel_id=1, source_target_pairs={{0,127},{1,0},{2,1},{3,2},{4,3},{5,4},{6,5},{7,6},{8,7},{9,8},{10,... | collective-permute-start | bytes 1179656 | tf_op jit(solution)/shard_map/ppermute | solution.py:611
  39.7 13.2 %collective-permute-start.12 = (f32[768,128]{1,0:T(8,128)S(1)}, f32[768,128]{1,0:T(8,128)S(1)}, u32[]{:S(2)}, u32[]{:S(2)}) collective-permute-start(f32[768,128]{1,0:T(8,128)S(1)} %get-tuple-element.74), channel_id=1, source_target_pairs={{0,1},{1,2},{2,3},{3,4},{4,5},{5,6},{6,7},{7,8},{8,9},{9,10},{10,1... | collective-permute-start | bytes 1179656 | tf_op jit(solution)/shard_map/ppermute | solution.py:611
  40.9 12.0 %collective-permute-start.13 = (f32[768,128]{1,0:T(8,128)S(1)}, f32[768,128]{1,0:T(8,128)S(1)}, u32[]{:S(2)}, u32[]{:S(2)}) collective-permute-start(f32[768,128]{1,0:T(8,128)S(1)} %get-tuple-element.75), channel_id=1, source_target_pairs={{0,1},{1,0},{2,3},{3,2},{4,5},{5,4},{6,7},{7,6},{8,9},{9,8},{10,11... | collective-permute-start | bytes 1179656 | tf_op jit(solution)/shard_map/ppermute | solution.py:616
  41.0 11.9 %collective-permute-start.14 = (f32[768,128]{1,0:T(8,128)S(1)}, f32[768,128]{1,0:T(8,128)S(1)}, u32[]{:S(2)}, u32[]{:S(2)}) collective-permute-start(f32[768,128]{1,0:T(8,128)S(1)} %get-tuple-element.69.before), channel_id=1, source_target_pairs={{0,1},{1,0},{2,3},{3,2},{4,5},{5,4},{6,7},{7,6},{8,9},{9,8},{10,11... | collective-permute-start | bytes 1179656 | tf_op jit(solution)/shard_map/ppermute | solution.py:616
  41.4 11.5 %copy-start = (s32[2,768]{1,0:T(2,128)S(1)}, s32[2,768]{1,0:T(2,128)}, u32[]{:S(2)}) copy-start(s32[2,768]{1,0:T(2,128)} %order_s.1) | copy-start | bytes 18436

commit v5 on v4

--- a/solution.py
+++ b/solution.py
@@ -98,6 +98,12 @@
     return jnp.where(last, pltpu.roll(value, SEGS - 1, 0), value)
 
 
+def preceding(ref, q, t):
+    first = t == 0
+    value = plane(ref, q, jnp.where(first, STEPS - 1, t - 1))
+    return jnp.where(first, pltpu.roll(value, 1, 0), value)
+
+
 def place_of(y):
     return lax.rem(y, STEPS) * SEGS + lax.div(y, STEPS)
 
@@ -130,11 +136,6 @@
                 total = plane(s_ref, 4 * i + 3, t) + upper
                 set_plane(s_ref, 4 * i + 3, t, total)
                 set_plane(s_ref, 4 * i, t + 1, total)
-
-
-def edge_messages(s_ref, behind_ref, ahead_ref):
-    behind_ref[...] = s_ref[0:EDGE, :]
-    ahead_ref[...] = s_ref[12 * ELEMS:15 * ELEMS, :]
 
 
 def general_sums(v_ref, s_ref, partner_any, partner_s):
@@ -333,14 +334,18 @@
         out = weak(x, lambda q: mx[q], lambda q: my[q])
         for q in range(16):
             set_plane(s_ref, q, t, out[q])
-        return carry
-
-    lax.fori_loop(0, STEPS, body, 0, unroll=2)
-
-    @pl.when(ok)
-    def _():
-        ring_sums(s_ref)
-        edge_messages(s_ref, behind_ref, ahead_ref)
+        behind = [out[0] + carry[0], out[1], out[2]]
+        ahead = [out[12] + carry[1], out[13], out[14]]
+        for j in range(3):
+            set_plane(behind_ref, j, t, behind[j])
+            set_plane(ahead_ref, j, t, ahead[j])
+            set_plane(pair_ref, j, t, jnp.where(odd == 1, behind[j], ahead[j]))
+        return (out[3], out[15])
+
+    zero = jnp.zeros((SEGS, COLS), jnp.float32)
+    tail = [pltpu.roll(v, 1, 0) for v in lax.fori_loop(0, STEPS, body, (zero, zero), unroll=4)]
+    for message, value in ((behind_ref, tail[0]), (ahead_ref, tail[1]), (pair_ref, jnp.where(odd == 1, tail[0], tail[1]))):
+        message[0:SEGS, :] = message[0:SEGS, :] + value
 
     @pl.when(jnp.logical_not(ok))
     def _():
@@ -348,13 +353,13 @@
         general_sums(v_ref, s_ref, partner_h, partner_s)
         general_messages(s_ref, behind_ref, ahead_ref, send_h, send_s)
 
-    @pl.when(odd == 1)
-    def _():
-        pair_ref[...] = behind_ref[...]
-
-    @pl.when(odd == 0)
-    def _():
-        pair_ref[...] = ahead_ref[...]
+        @pl.when(odd == 1)
+        def _():
+            pair_ref[...] = behind_ref[...]
+
+        @pl.when(odd == 0)
+        def _():
+            pair_ref[...] = ahead_ref[...]
 
 
 def edge_values(arrived, im_ref, base, t, scale):
@@ -389,7 +394,12 @@
         for q in range(16):
             im = jnp.broadcast_to(row[:, q:q + 1], (SEGS, COLS))
             set_plane(im_ref, q, t, im)
-            x.append(im * plane(s_in, q, t))
+            value = plane(s_in, q, t)
+            if q % 4 == 0:
+                value = value + preceding(s_in, q + 3, t)
+            if q % 4 == 3:
+                value = value + following(s_in, q - 3, t)
+            x.append(im * value)
         mx = [plane(mx_ref, q, t) for q in range(16)]
         for j in range(4):
             for n, (a, b) in enumerate(((0, 0), (0, 3), (3, 3))):
@@ -435,7 +445,7 @@
             return tuple(tail)
 
         zero = jnp.zeros((SEGS, COLS), jnp.float32)
-        tail = lax.fori_loop(0, STEPS, body, (zero, zero), unroll=4)
+        tail = lax.fori_loop(0, STEPS, body, (zero, zero), unroll=8)
         for out, last in zip((behind_ref, ahead_ref), tail):
             out[0:SEGS, :] = out[0:SEGS, :] + pltpu.roll(last, 1, 0)
 
@@ -459,9 +469,25 @@
         general_messages(g_ref, behind_ref, ahead_ref, send_any, send_s)
 
 
-def inner_kernel(kind, flag, w_in, g_in, forward, backward, pair_even, pair_odd, mx_ref, my_ref, im_ref, u_in, visc, recv_any, u_ref, w_ref, s_ref, recv_s):
+def leave(order_s, ok, raw, t, x):
+    elems = []
+    for s in range(SEGS):
+        y = STEPS * s + t
+        elems.append(16 * jnp.where(ok, order_s[0, 3 * y + 1] >> 4, y))
+    for half in range(2):
+        rows = flipped(x[8 * half:8 * half + 8])
+        for s in range(SEGS):
+            raw[pl.ds(pl.multiple_of(elems[s] + 8 * half, 8), 8), :] = rows[s]
+
+
+def inner_kernel(kind, flag, w_in, g_in, forward, backward, pair_even, pair_odd, mx_ref, my_ref, im_ref, u_in, visc, send_any, recv_any, u_ref, w_ref, s_ref, recv_s, order_s, sem):
+    if kind == 2:
+        load = pltpu.make_async_copy(send_any, order_s, sem)
+        load.start()
     ok = flag[0, 0] == 1
     rate = visc[...]
+    if kind == 2:
+        load.wait()
 
     @pl.when(ok)
     def _():
@@ -497,8 +523,11 @@
             x = [plane(s_ref, q, t) * plane(im_ref, q, t) for q in range(16)]
             if kind != 1:
                 x = [plane(u_in, q, t) - rate * x[q] for q in range(16)]
+            if kind == 0:
                 for q in range(16):
                     set_plane(u_ref, q, t, x[q])
+            if kind == 2:
+                leave(order_s, ok, u_ref, t, x)
             if kind != 2:
                 out = weak(x, lambda q: plane(mx_ref, q, t), lambda q: plane(my_ref, q, t))
                 for q in range(16):
@@ -522,35 +551,41 @@
             u_ref[...] = u_in[...]
 
 
-def last_kernel(flag, seen, order_s, w_in, forward, backward, pair_even, pair_odd, im_ref, u_in, visc, recv_any, out, raw, v_ref, recv_s, sem):
+def last_kernel(flag, seen, send_any, w_in, forward, backward, pair_even, pair_odd, im_ref, u_in, visc, recv_any, out,
+                raw, v_ref, order_s, recv_s, sems):
+    load = pltpu.make_async_copy(send_any, order_s, sems.at[0])
+    load.start()
     ok = flag[0, 0] == 1
     rate = visc[...]
 
-    def leave(t, x):
-        elems = []
-        for s in range(SEGS):
-            y = STEPS * s + t
-            elems.append(16 * jnp.where(ok, order_s[0, 3 * y + 1] >> 4, y))
-        for half in range(2):
-            rows = flipped(x[8 * half:8 * half + 8])
+    @pl.when(ok)
+    def _():
+        def edges(left, right, t, carry):
+            rows = flipped(edge_values(left, im_ref, 0, t, rate) + edge_values(right, im_ref, 12, t, rate))
             for s in range(SEGS):
-                raw[pl.ds(pl.multiple_of(elems[s] + 8 * half, 8), 8), :] = rows[s]
-
-    @pl.when(ok)
-    def _():
-        def body(left, right, t, carry):
-            x = [plane(u_in, q, t) for q in range(16)]
-            for base, arrived in ((0, left), (12, right)):
-                c = edge_values(arrived, im_ref, base, t, rate)
-                for j in range(4):
-                    x[base + j] = x[base + j] - c[j]
-            leave(t, x)
+                v_ref[pl.ds(pl.multiple_of((t * SEGS + s) * 8, 8), 8), :] = rows[s]
             return carry
 
         for odd, left, right in ((0, forward, pair_even), (1, pair_odd, backward)):
             @pl.when(flag[1, 0] == odd)
             def _():
-                lax.fori_loop(0, STEPS, functools.partial(body, left, right), 0, unroll=2)
+                lax.fori_loop(0, STEPS, functools.partial(edges, left, right), 0, unroll=4)
+
+    load.wait()
+
+    @pl.when(ok)
+    def _():
+        low = iota((8, COLS), 0) < 4
+
+        def body(t, carry):
+            for s in range(SEGS):
+                e = 16 * (order_s[0, 3 * (STEPS * s + t) + 1] >> 4)
+                change = tile(v_ref, (t * SEGS + s) * 8)
+                for half, mine in ((0, low), (8, jnp.logical_not(low))):
+                    raw[pl.ds(pl.multiple_of(e + half, 8), 8), :] = tile(u_in, e + half) - jnp.where(mine, change, 0.0)
+            return carry
+
+        lax.fori_loop(0, STEPS, body, 0, unroll=4)
 
     @pl.when(jnp.logical_not(ok))
     def _():
@@ -563,12 +598,12 @@
         v_ref[...] = u_in[...] - rate * (v_ref[...] * im_ref[...])
 
         def body(t, carry):
-            leave(t, [plane(v_ref, q, t) for q in range(16)])
+            leave(order_s, ok, raw, t, [plane(v_ref, q, t) for q in range(16)])
             return carry
 
         lax.fori_loop(0, STEPS, body, 0)
 
-    store = pltpu.make_async_copy(raw, out, sem)
+    store = pltpu.make_async_copy(raw, out, sems.at[1])
     store.start()
     store.wait()
 
@@ -664,16 +699,16 @@
         kind = 1 if updates else 2 if step == 2 * SUBCYCLES - 2 else 0
         u, w = call(
             functools.partial(inner_kernel, kind),
-            (flag, w, g, *arrived, *crossings, mx, my, im, u, visc, recv_rows),
-            [VM, VM, HB] + [VM] * 9 + [HB], [FIELD, FIELD], [VM] * 2,
-            [SCRATCH, RECV_S], WORK * 2, 8 * SIZE, "inner",
+            (flag, w, g, *arrived, *crossings, mx, my, im, u, visc, send_rows, recv_rows),
+            [VM, VM, HB] + [VM] * 9 + [HB] * 2, [FIELD, FIELD], [VM] * 2,
+            [SCRATCH, RECV_S, SEND_S, pltpu.SemaphoreType.DMA], WORK * 2, 8 * SIZE, "inner",
         )
     seen = call(seen_kernel, (came[1], flag), [FREE, FREE], WORD, VM, [], 0, 0, "seen")
     return call(
         last_kernel,
         (flag, seen, send_rows, w, *came, *pairs, im, u, visc, recv_rows),
-        [VM, FREE, SM] + [VM] * 8 + [HB], FIELD, HB,
-        [SCRATCH, SCRATCH, RECV_S, pltpu.SemaphoreType.DMA], WORK // 8, 4 * SIZE, "last",
+        [VM, FREE, HB] + [VM] * 8 + [HB], FIELD, HB,
+        [SCRATCH, SCRATCH, SEND_S, RECV_S, pltpu.SemaphoreType.DMA((2,))], WORK // 8, 4 * SIZE, "last",
     )
 
 

time: 56.2 us -> 55.4 us (0.986)
  waiting for transfers between devices: 18.9 us -> 17.6 us
  Pallas kernels: 23 us -> 23.6 us
    ppermute x8, waiting for transfers between devices: 18.9 us -> 17.6 us  [moved(): lax.ppermute(value, 'elem', [(i, (i + by) % size) for i in range(size)])]
    pallas_call x19, Pallas kernels: 23 us -> 23.6 us  [call(): pl.pallas_call(kernel, out_shape=shapes, in_specs=specs, out_specs=outs,...]
  transfers between devices with their start and end apart: 15 -> 15, of which waited for: 6 -> 5; matrix products, arithmetic and copies ran while one was open for 0% -> 0% of each run, Pallas kernels for 26% -> 29%
where the time goes in v5:
time: 55.4 us; the launch traced here: 55.2 us
  Pallas kernels  23.6 us (43%)
  waiting for transfers between devices  17.6 us (32%)
  starting transfers between devices  13.8 us (25%)
    pallas_call x19, Pallas kernels, call(): pl.pallas_call(kernel, out_shape=shapes, in_specs=specs, out_specs=outs,...  23.6 us
    ppermute x8, waiting for transfers between devices, moved(): lax.ppermute(value, 'elem', [(i, (i + by) % size) for i in range(size)])  17.6 us
    ppermute x8, starting transfers between devices, moved(): lax.ppermute(value, 'elem', [(i, (i + by) % size) for i in range(size)])  10 us
    ppermute x7, starting transfers between devices, crossed(): lax.ppermute(value, 'elem', [(i, i + 1 - 2 * (i % 2)) for i in range(size)])  3.79 us
  transfers between devices with their start and end apart: 15, of which 5 were waited for; matrix products, arithmetic and copies ran while one was open for 0% of the time, Pallas kernels for 29%

profile of v5, /device:TPU:0, one launch (start us, length us, event | category | flops | bytes accessed | tf_op | source)
XLA Modules:
  0.0 55.2 jit_solution(2402831058551319509)
XLA Ops:
  0.0 4.5 %first.1 = (f32[4096,128]{1,0:T(8,128)S(1)}, f32[4096,128]{1,0:T(8,128)S(1)}, f32[4096,128]{1,0:T(8,128)S(1)}, f32[4096,128]{1,0:T(8,128)S(1)}, f32[256,128]{1,0...) custom-call(f32[4096,128]{1,0:T(8,128)} %prog.1, ...), custom_call_target="tpu_custom_call" | custom-call | flops 1 | bytes 1 | tf_op jit(solution)/shard_map/first/pallas_call | solution.py:631
  4.5 0.1 collective-permute-start
  4.6 2.1 %collective-permute-start.1 = (f32[768,128]{1,0:T(8,128)S(1)}, f32[768,128]{1,0:T(8,128)S(1)}, u32[]{:S(2)}, u32[]{:S(2)}) collective-permute-start(f32[768,128]{1,0:T(8,128)S(1)} %get-tuple-element.48), channel_id=1, source_target_pairs={{0,1},{1,0},{2,3},{3,2},{4,5},{5,4},{6,7},{7,6},{8,9},{9,8},{10,11... | collective-permute-start | bytes 1179656 | tf_op jit(solution)/shard_map/ppermute | solution.py:651
  6.7 6.9 %collective-permute-start.3 = (f32[768,128]{1,0:T(8,128)S(1)}, f32[768,128]{1,0:T(8,128)S(1)}, u32[]{:S(2)}, u32[]{:S(2)}) collective-permute-start(f32[768,128]{1,0:T(8,128)S(1)} %get-tuple-element.53), channel_id=1, source_target_pairs={{0,127},{1,0},{2,1},{3,2},{4,3},{5,4},{6,5},{7,6},{8,7},{9,8},{10,... | collective-permute-start | bytes 1179656 | tf_op jit(solution)/shard_map/ppermute | solution.py:646
  13.5 3.5 %prepare.1 = (f32[4096,128]{1,0:T(8,128)S(1)}, f32[3072,128]{1,0:T(8,128)S(1)}, f32[4096,128]{1,0:T(8,128)S(1)}) custom-call(s32[8,128]{1,0:T(8,128)S(1)} %get-tuple-element.41.before.flag, f32[4096,128]{1,0:T(8,128)S(1)} %get-tuple-element.43.s_in, f32[4096,128]{1,0:T(8,128)S(1)} %get-tuple-element.44.mx_ref, f32[4096,128]{1,0:T(8,128)S(1)} %get-tuple-element.45.my_ref, ...), custom_call_target="tpu_custom_call" | custom-call | flops 1 | bytes 1 | tf_op jit(solution)/shard_map/prepare/pallas_call | solution.py:631
  17.0 1.2 %collective-permute-done.arrived.chain.forward = f32[768,128]{1,0:T(8,128)S(1)} collective-permute-done((f32[768,128]{1,0:T(8,128)S(1)}, f32[768,128]{1,0:T(8,128)S(1)}, u32[]{:S(2)}, u32[]{:S(2)}) %collective-permute-start) | collective-permute-done | bytes 393248 | tf_op jit(solution)/shard_map/ppermute | solution.py:646
  18.2 0.7 %edges.6 = (f32[768,128]{1,0:T(8,128)S(1)}, f32[4096,128]{1,0:T(8,128)}, f32[768,128]{1,0:T(8,128)S(1)}) custom-call(s32[8,128]{1,0:T(8,128)S(1)} %get-tuple-element.41.before.flag, s32[8,128]{1,0:T(8,128)S(1)} %seen.7, f32[4096,128]{1,0:T(8,128)S(1)} %get-tuple-element.47.w_ref.w_in, f32[768,128]{1,0:T(8,128)S(1)} %collective-permute-done.arrived.chain.forward, ...), custom_call_target="tpu_custom_call" | custom-call | flops 1 | bytes 1 | tf_op jit(solution)/shard_map/edges/pallas_call | solution.py:631
  18.9 0.1 collective-permute-start.2
  19.0 0.5 collective-permute-start.4
  19.5 0.1 edges.7
  19.6 0.8 %collective-permute-start.6 = (f32[768,128]{1,0:T(8,128)S(1)}, f32[768,128]{1,0:T(8,128)S(1)}, u32[]{:S(2)}, u32[]{:S(2)}) collective-permute-start(f32[768,128]{1,0:T(8,128)S(1)} %get-tuple-element.60), channel_id=1, source_target_pairs={{0,1},{1,2},{2,3},{3,4},{4,5},{5,6},{6,7},{7,8},{8,9},{9,10},{10,1... | collective-permute-start | bytes 1179656 | tf_op jit(solution)/shard_map/ppermute | solution.py:646
  20.4 0.1 collective-permute-start.7
  20.5 3.5 %inner.3 = (f32[4096,128]{1,0:T(8,128)S(1)}, f32[4096,128]{1,0:T(8,128)S(1)}) custom-call(s32[8,128]{1,0:T(8,128)S(1)} %get-tuple-element.41.before.flag, f32[4096,128]{1,0:T(8,128)S(1)} %get-tuple-element.47.w_ref.w_in, f32[4096,128]{1,0:T(8,128)} %get-tuple-element.56.g_in, f32[768,128]{1,0:T(8,128)S(1)} %collective-permute-done.arrived.chain.forward, ...), custom_call_target="tpu_custom_call" | custom-call | flops 1 | bytes 1 | tf_op jit(solution)/shard_map/inner/pallas_call | solution.py:631
  24.0 0.3 collective-permute-done.2.arrived.chain.backward
  24.3 0.1 edges.8
  24.4 0.9 %collective-permute-start.5 = (f32[768,128]{1,0:T(8,128)S(1)}, f32[768,128]{1,0:T(8,128)S(1)}, u32[]{:S(2)}, u32[]{:S(2)}) collective-permute-start(f32[768,128]{1,0:T(8,128)S(1)} %get-tuple-element.59), channel_id=1, source_target_pairs={{0,1},{1,2},{2,3},{3,4},{4,5},{5,6},{6,7},{7,8},{8,9},{9,10},{10,1... | collective-permute-start | bytes 1179656 | tf_op jit(solution)/shard_map/ppermute | solution.py:646
  25.3 0.1 collective-permute-start.8
  25.4 7.0 %collective-permute-done.6.arrived.chain.forward = f32[768,128]{1,0:T(8,128)S(1)} collective-permute-done((f32[768,128]{1,0:T(8,128)S(1)}, f32[768,128]{1,0:T(8,128)S(1)}, u32[]{:S(2)}, u32[]{:S(2)}) %collective-permute-start.6) | collective-permute-done | bytes 393248 | tf_op jit(solution)/shard_map/ppermute | solution.py:646
  32.4 0.8 %edges.9 = (f32[768,128]{1,0:T(8,128)S(1)}, f32[4096,128]{1,0:T(8,128)}, f32[768,128]{1,0:T(8,128)S(1)}) custom-call(s32[8,128]{1,0:T(8,128)S(1)} %get-tuple-element.41.before.flag, s32[8,128]{1,0:T(8,128)S(1)} %seen.11, f32[4096,128]{1,0:T(8,128)S(1)} %get-tuple-element.57.w_ref.w_in, ...), custom_call_target="tpu_custom_call", output_to_operand_aliasing={{1}: (14, {})} | custom-call | flops 1 | bytes 1 | tf_op jit(solution)/shard_map/edges/pallas_call | solution.py:631
  33.2 0.1 collective-permute-start.10
  33.3 0.5 collective-permute-start.11
  33.8 3.1 %inner.4 = (f32[4096,128]{1,0:T(8,128)S(1)}, f32[4096,128]{1,0:T(8,128)S(1)}) custom-call(s32[8,128]{1,0:T(8,128)S(1)} %get-tuple-element.41.before.flag, f32[4096,128]{1,0:T(8,128)S(1)} %get-tuple-element.57.w_ref.w_in, f32[4096,128]{1,0:T(8,128)} %get-tuple-element.64.g_in, f32[768,128]{1,0:T(8,128)S(1)} %collective-permute-done.6.arrived.chain.forward, ...), custom_call_target="tpu_custom_call" | custom-call | flops 1 | bytes 1 | tf_op jit(solution)/shard_map/inner/pallas_call | solution.py:631
  36.9 1.0 %collective-permute-done.5.arrived.chain.forward = f32[768,128]{1,0:T(8,128)S(1)} collective-permute-done((f32[768,128]{1,0:T(8,128)S(1)}, f32[768,128]{1,0:T(8,128)S(1)}, u32[]{:S(2)}, u32[]{:S(2)}) %collective-permute-start.5) | collective-permute-done | bytes 393248 | tf_op jit(solution)/shard_map/ppermute | solution.py:646
  38.0 0.7 %edges.10 = (f32[768,128]{1,0:T(8,128)S(1)}, f32[4096,128]{1,0:T(8,128)}, f32[768,128]{1,0:T(8,128)S(1)}) custom-call(s32[8,128]{1,0:T(8,128)S(1)} %get-tuple-element.41.before.flag, s32[8,128]{1,0:T(8,128)S(1)} %seen.10, f32[4096,128]{1,0:T(8,128)S(1)} %get-tuple-element.65.w_ref.w_in, f32[768,128]{1,0:T(8,128)S(1)} %collective-permute-done.5.arrived.chain.forward, ...), custom_call_target="tpu_custom_call" | custom-call | flops 1 | bytes 1 | tf_op jit(solution)/shard_map/edges/pallas_call | solution.py:631
  38.7 0.1 collective-permute-start.9
  38.8 0.1 edges.11
  38.9 1.2 %collective-permute-start.12 = (f32[768,128]{1,0:T(8,128)S(1)}, f32[768,128]{1,0:T(8,128)S(1)}, u32[]{:S(2)}, u32[]{:S(2)}) collective-permute-start(f32[768,128]{1,0:T(8,128)S(1)} %get-tuple-element.74), channel_id=1, source_target_pairs={{0,1},{1,2},{2,3},{3,4},{4,5},{5,6},{6,7},{7,8},{8,9},{9,10},{10,1... | collective-permute-start | bytes 1179656 | tf_op jit(solution)/shard_map/ppermute | solution.py:646
  40.1 0.1 collective-permute-start.13
  40.2 0.4 collective-permute-start.14
  40.6 3.4 %inner.5 = (f32[4096,128]{1,0:T(8,128)S(1)}, f32[4096,128]{1,0:T(8,128)S(1)}) custom-call(s32[8,128]{1,0:T(8,128)S(1)} %get-tuple-element.41.before.flag, f32[4096,128]{1,0:T(8,128)S(1)} %get-tuple-element.65.w_ref.w_in, f32[4096,128]{1,0:T(8,128)} %get-tuple-element.72.g_in, f32[768,128]{1,0:T(8,128)S(1)} %collective-permute-done.5.arrived.chain.forward, ...), custom_call_target="tpu_custom_call" | custom-call | flops 1 | bytes 1 | tf_op jit(solution)/shard_map/inner/pallas_call | solution.py:631
  44.1 8.1 %collective-permute-done.12.forward = f32[768,128]{1,0:T(8,128)S(1)} collective-permute-done((f32[768,128]{1,0:T(8,128)S(1)}, f32[768,128]{1,0:T(8,128)S(1)}, u32[]{:S(2)}, u32[]{:S(2)}) %collective-permute-start.12) | collective-permute-done | bytes 393248 | tf_op jit(solution)/shard_map/ppermute | solution.py:646
  52.2 3.1 %last.1 = f32[4096,128]{1,0:T(8,128)} custom-call(s32[8,128]{1,0:T(8,128)S(1)} %get-tuple-element.41.before.flag, s32[8,128]{1,0:T(8,128)S(1)} %seen.12, s32[2,768]{1,0:T(2,128)} %send_any.19, f32[4096,128]{1,0:T(8,128)S(1)} %get-tuple-element.73.w_in, f32[768,128]{1,0:T(8,128)S(1)} %collective-permute-done.12.forward, ...), custom_call_target="tpu_custom_call" | custom-call | flops 1 | bytes 1 | tf_op jit(solution)/shard_map/last/pallas_call | solution.py:631
  (21 shorter events, 0.1 us)
Async XLA Ops:
  0.0 13.5 %copy-start.1 = (f32[4096]{0:T(1024)S(1)}, f32[4096]{0:T(1024)}, u32[]{:S(2)}) copy-start(f32[4096]{0:T(1024)} %param.9) | copy-start | bytes 49156
  4.5 13.7 %collective-permute-start = (f32[768,128]{1,0:T(8,128)S(1)}, f32[768,128]{1,0:T(8,128)S(1)}, u32[]{:S(2)}, u32[]{:S(2)}) collective-permute-start(f32[768,128]{1,0:T(8,128)S(1)} %get-tuple-element.42), channel_id=1, source_target_pairs={{0,1},{1,2},{2,3},{3,4},{4,5},{5,6},{6,7},{7,8},{8,9},{9,10},{10,1... | collective-permute-start | bytes 1179656 | tf_op jit(solution)/shard_map/ppermute | solution.py:646
  4.6 13.7 %collective-permute-start.1 = (f32[768,128]{1,0:T(8,128)S(1)}, f32[768,128]{1,0:T(8,128)S(1)}, u32[]{:S(2)}, u32[]{:S(2)}) collective-permute-start(f32[768,128]{1,0:T(8,128)S(1)} %get-tuple-element.48), channel_id=1, source_target_pairs={{0,1},{1,0},{2,3},{3,2},{4,5},{5,4},{6,7},{7,6},{8,9},{9,8},{10,11... | collective-permute-start | bytes 1179656 | tf_op jit(solution)/shard_map/ppermute | solution.py:651
  6.7 12.9 %collective-permute-start.3 = (f32[768,128]{1,0:T(8,128)S(1)}, f32[768,128]{1,0:T(8,128)S(1)}, u32[]{:S(2)}, u32[]{:S(2)}) collective-permute-start(f32[768,128]{1,0:T(8,128)S(1)} %get-tuple-element.53), channel_id=1, source_target_pairs={{0,127},{1,0},{2,1},{3,2},{4,3},{5,4},{6,5},{7,6},{8,7},{9,8},{10,... | collective-permute-start | bytes 1179656 | tf_op jit(solution)/shard_map/ppermute | solution.py:646
  13.5 4.7 %copy-start = (f32[128]{0:T(128)S(1)}, f32[128]{0:T(128)}, u32[]{:S(2)}) copy-start(f32[128]{0:T(128)} %param.10) | copy-start | bytes 1540
  18.9 5.4 %collective-permute-start.2 = (f32[768,128]{1,0:T(8,128)S(1)}, f32[768,128]{1,0:T(8,128)S(1)}, u32[]{:S(2)}, u32[]{:S(2)}) collective-permute-start(f32[768,128]{1,0:T(8,128)S(1)} %get-tuple-element.52), channel_id=1, source_target_pairs={{0,127},{1,0},{2,1},{3,2},{4,3},{5,4},{6,5},{7,6},{8,7},{9,8},{10,... | collective-permute-start | bytes 1179656 | tf_op jit(solution)/shard_map/ppermute | solution.py:646
  19.0 5.3 %collective-permute-start.4 = (f32[768,128]{1,0:T(8,128)S(1)}, f32[768,128]{1,0:T(8,128)S(1)}, u32[]{:S(2)}, u32[]{:S(2)}) collective-permute-start(f32[768,128]{1,0:T(8,128)S(1)} %get-tuple-element.54.before), channel_id=1, source_target_pairs={{0,1},{1,0},{2,3},{3,2},{4,5},{5,4},{6,7},{7,6},{8,9},{9,8},{10,11... | collective-permute-start | bytes 1179656 | tf_op jit(solution)/shard_map/ppermute | solution.py:651
  19.6 12.8 %collective-permute-start.6 = (f32[768,128]{1,0:T(8,128)S(1)}, f32[768,128]{1,0:T(8,128)S(1)}, u32[]{:S(2)}, u32[]{:S(2)}) collective-permute-start(f32[768,128]{1,0:T(8,128)S(1)} %get-tuple-element.60), channel_id=1, source_target_pairs={{0,1},{1,2},{2,3},{3,4},{4,5},{5,6},{6,7},{7,8},{8,9},{9,10},{10,1... | collective-permute-start | bytes 1179656 | tf_op jit(solution)/shard_map/ppermute | solution.py:646
  20.4 12.0 %collective-permute-start.7 = (f32[768,128]{1,0:T(8,128)S(1)}, f32[768,128]{1,0:T(8,128)S(1)}, u32[]{:S(2)}, u32[]{:S(2)}) collective-permute-start(f32[768,128]{1,0:T(8,128)S(1)} %get-tuple-element.62), channel_id=1, source_target_pairs={{0,1},{1,0},{2,3},{3,2},{4,5},{5,4},{6,7},{7,6},{8,9},{9,8},{10,11... | collective-permute-start | bytes 1179656 | tf_op jit(solution)/shard_map/ppermute | solution.py:651
  24.4 13.6 %collective-permute-start.5 = (f32[768,128]{1,0:T(8,128)S(1)}, f32[768,128]{1,0:T(8,128)S(1)}, u32[]{:S(2)}, u32[]{:S(2)}) collective-permute-start(f32[768,128]{1,0:T(8,128)S(1)} %get-tuple-element.59), channel_id=1, source_target_pairs={{0,1},{1,2},{2,3},{3,4},{4,5},{5,6},{6,7},{7,8},{8,9},{9,10},{10,1... | collective-permute-start | bytes 1179656 | tf_op jit(solution)/shard_map/ppermute | solution.py:646
  25.3 12.6 %collective-permute-start.8 = (f32[768,128]{1,0:T(8,128)S(1)}, f32[768,128]{1,0:T(8,128)S(1)}, u32[]{:S(2)}, u32[]{:S(2)}) collective-permute-start(f32[768,128]{1,0:T(8,128)S(1)} %get-tuple-element.61.before), channel_id=1, source_target_pairs={{0,1},{1,0},{2,3},{3,2},{4,5},{5,4},{6,7},{7,6},{8,9},{9,8},{10,11... | collective-permute-start | bytes 1179656 | tf_op jit(solution)/shard_map/ppermute | solution.py:651
  33.2 5.6 %collective-permute-start.10 = (f32[768,128]{1,0:T(8,128)S(1)}, f32[768,128]{1,0:T(8,128)S(1)}, u32[]{:S(2)}, u32[]{:S(2)}) collective-permute-start(f32[768,128]{1,0:T(8,128)S(1)} %get-tuple-element.68), channel_id=1, source_target_pairs={{0,127},{1,0},{2,1},{3,2},{4,3},{5,4},{6,5},{7,6},{8,7},{9,8},{10,... | collective-permute-start | bytes 1179656 | tf_op jit(solution)/shard_map/ppermute | solution.py:646
  33.3 5.5 %collective-permute-start.11 = (f32[768,128]{1,0:T(8,128)S(1)}, f32[768,128]{1,0:T(8,128)S(1)}, u32[]{:S(2)}, u32[]{:S(2)}) collective-permute-start(f32[768,128]{1,0:T(8,128)S(1)} %get-tuple-element.70), channel_id=1, source_target_pairs={{0,1},{1,0},{2,3},{3,2},{4,5},{5,4},{6,7},{7,6},{8,9},{9,8},{10,11... | collective-permute-start | bytes 1179656 | tf_op jit(solution)/shard_map/ppermute | solution.py:651
  38.7 5.4 %collective-permute-start.9 = (f32[768,128]{1,0:T(8,128)S(1)}, f32[768,128]{1,0:T(8,128)S(1)}, u32[]{:S(2)}, u32[]{:S(2)}) collective-permute-start(f32[768,128]{1,0:T(8,128)S(1)} %get-tuple-element.67), channel_id=1, source_target_pairs={{0,127},{1,0},{2,1},{3,2},{4,3},{5,4},{6,5},{7,6},{8,7},{9,8},{10,... | collective-permute-start | bytes 1179656 | tf_op jit(solution)/shard_map/ppermute | solution.py:646
  38.9 13.2 %collective-permute-start.12 = (f32[768,128]{1,0:T(8,128)S(1)}, f32[768,128]{1,0:T(8,128)S(1)}, u32[]{:S(2)}, u32[]{:S(2)}) collective-permute-start(f32[768,128]{1,0:T(8,128)S(1)} %get-tuple-element.74), channel_id=1, source_target_pairs={{0,1},{1,2},{2,3},{3,4},{4,5},{5,6},{6,7},{7,8},{8,9},{9,10},{10,1... | collective-permute-start | bytes 1179656 | tf_op jit(solution)/shard_map/ppermute | solution.py:646
  40.1 12.1 %collective-permute-start.13 = (f32[768,128]{1,0:T(8,128)S(1)}, f32[768,128]{1,0:T(8,128)S(1)}, u32[]{:S(2)}, u32[]{:S(2)}) collective-permute-start(f32[768,128]{1,0:T(8,128)S(1)} %get-tuple-element.75), channel_id=1, source_target_pairs={{0,1},{1,0},{2,3},{3,2},{4,5},{5,4},{6,7},{7,6},{8,9},{9,8},{10,11... | collective-permute-start | bytes 1179656 | tf_op jit(solution)/shard_map/ppermute | solution.py:651
  40.2 12.0 %collective-permute-start.14 = (f32[768,128]{1,0:T(8,128)S(1)}, f32[768,128]{1,0:T(8,128)S(1)}, u32[]{:S(2)}, u32[]{:S(2)}) collective-permute-start(f32[768,128]{1,0:T(8,128)S(1)} %get-tuple-element.69.before), channel_id=1, source_target_pairs={{0,1},{1,0},{2,3},{3,2},{4,5},{5,4},{6,7},{7,6},{8,9},{9,8},{10,11... | collective-permute-start | bytes 1179656 | tf_op jit(solution)/shard_map/ppermute | solution.py:651

commit v6 on v5

--- a/solution.py
+++ b/solution.py
@@ -343,7 +343,7 @@
         return (out[3], out[15])
 
     zero = jnp.zeros((SEGS, COLS), jnp.float32)
-    tail = [pltpu.roll(v, 1, 0) for v in lax.fori_loop(0, STEPS, body, (zero, zero), unroll=4)]
+    tail = [pltpu.roll(v, 1, 0) for v in lax.fori_loop(0, STEPS, body, (zero, zero), unroll=8)]
     for message, value in ((behind_ref, tail[0]), (ahead_ref, tail[1]), (pair_ref, jnp.where(odd == 1, tail[0], tail[1]))):
         message[0:SEGS, :] = message[0:SEGS, :] + value
 
@@ -684,7 +684,7 @@
         chained = ()
         before = flag
         arrived, crossings = list(came), list(pairs)
-        for odd in ((0, 1) if step % 2 == 0 else (1, 0)):
+        for odd in ((1, 0) if step % 2 == 0 else (0, 1)):
             seen = call(seen_kernel, (arrived[odd], before), [FREE, FREE], WORD, VM, [], 0, 0, "seen")
             before, g, chain = call(
                 functools.partial(edge_kernel, updates, odd),
@@ -703,7 +703,7 @@
             [VM, VM, HB] + [VM] * 9 + [HB] * 2, [FIELD, FIELD], [VM] * 2,
             [SCRATCH, RECV_S, SEND_S, pltpu.SemaphoreType.DMA], WORK * 2, 8 * SIZE, "inner",
         )
-    seen = call(seen_kernel, (came[1], flag), [FREE, FREE], WORD, VM, [], 0, 0, "seen")
+    seen = call(seen_kernel, (came[0], flag), [FREE, FREE], WORD, VM, [], 0, 0, "seen")
     return call(
         last_kernel,
         (flag, seen, send_rows, w, *came, *pairs, im, u, visc, recv_rows),

time: 55.4 us -> 55.3 us (level)
  starting transfers between devices: 13.8 us -> 13.1 us
  waiting for transfers between devices: 17.6 us -> 18.2 us
    ppermute x7, starting transfers between devices: 3.79 us -> 1.27 us  [crossed(): lax.ppermute(value, 'elem', [(i, i + 1 - 2 * (i % 2)) for i in range(size)])]
    ppermute x8, starting transfers between devices: 10 us -> 11.8 us  [moved(): lax.ppermute(value, 'elem', [(i, (i + by) % size) for i in range(size)])]
    ppermute x8, waiting for transfers between devices: 17.6 us -> 18.2 us  [moved(): lax.ppermute(value, 'elem', [(i, (i + by) % size) for i in range(size)])]
  transfers between devices with their start and end apart: 15 -> 15, of which waited for: 5 -> 7; matrix products, arithmetic and copies ran while one was open for 0% -> 0% of each run, Pallas kernels for 29% -> 29%
where the time goes in v6:
time: 55.3 us; the launch traced here: 55 us
  Pallas kernels  23.5 us (42%)
  waiting for transfers between devices  18.2 us (33%)
  starting transfers between devices  13.1 us (24%)
    pallas_call x19, Pallas kernels, call(): pl.pallas_call(kernel, out_shape=shapes, in_specs=specs, out_specs=outs,...  23.5 us
    ppermute x8, waiting for transfers between devices, moved(): lax.ppermute(value, 'elem', [(i, (i + by) % size) for i in range(size)])  18.2 us
    ppermute x8, starting transfers between devices, moved(): lax.ppermute(value, 'elem', [(i, (i + by) % size) for i in range(size)])  11.8 us
    ppermute x7, starting transfers between devices, crossed(): lax.ppermute(value, 'elem', [(i, i + 1 - 2 * (i % 2)) for i in range(size)])  1.27 us
  transfers between devices with their start and end apart: 15, of which 7 were waited for; matrix products, arithmetic and copies ran while one was open for 0% of the time, Pallas kernels for 29%

profile of v6, /device:TPU:0, one launch (start us, length us, event | category | flops | bytes accessed | tf_op | source)
XLA Modules:
  0.0 55.0 jit_solution(2758324115348245343)
XLA Ops:
  0.0 4.4 %first.1 = (f32[4096,128]{1,0:T(8,128)S(1)}, f32[4096,128]{1,0:T(8,128)S(1)}, f32[4096,128]{1,0:T(8,128)S(1)}, f32[4096,128]{1,0:T(8,128)S(1)}, f32[256,128]{1,0...) custom-call(f32[4096,128]{1,0:T(8,128)} %prog.1, ...), custom_call_target="tpu_custom_call" | custom-call | flops 1 | bytes 1 | tf_op jit(solution)/shard_map/first/pallas_call | solution.py:631
  4.4 8.3 %collective-permute-start = (f32[768,128]{1,0:T(8,128)S(1)}, f32[768,128]{1,0:T(8,128)S(1)}, u32[]{:S(2)}, u32[]{:S(2)}) collective-permute-start(f32[768,128]{1,0:T(8,128)S(1)} %get-tuple-element.42), channel_id=1, source_target_pairs={{0,127},{1,0},{2,1},{3,2},{4,3},{5,4},{6,5},{7,6},{8,7},{9,8},{10,... | collective-permute-start | bytes 1179656 | tf_op jit(solution)/shard_map/ppermute | solution.py:646
  12.7 0.5 collective-permute-start.3
  13.2 3.5 %prepare.1 = (f32[4096,128]{1,0:T(8,128)S(1)}, f32[3072,128]{1,0:T(8,128)S(1)}, f32[4096,128]{1,0:T(8,128)S(1)}) custom-call(s32[8,128]{1,0:T(8,128)S(1)} %get-tuple-element.41.before.flag, f32[4096,128]{1,0:T(8,128)S(1)} %get-tuple-element.43.s_in, f32[4096,128]{1,0:T(8,128)S(1)} %get-tuple-element.44.mx_ref, f32[4096,128]{1,0:T(8,128)S(1)} %get-tuple-element.45.my_ref, ...), custom_call_target="tpu_custom_call" | custom-call | flops 1 | bytes 1 | tf_op jit(solution)/shard_map/prepare/pallas_call | solution.py:631
  16.7 1.3 %collective-permute-done.arrived.chain.backward = f32[768,128]{1,0:T(8,128)S(1)} collective-permute-done((f32[768,128]{1,0:T(8,128)S(1)}, f32[768,128]{1,0:T(8,128)S(1)}, u32[]{:S(2)}, u32[]{:S(2)}) %collective-permute-start) | collective-permute-done | bytes 393248 | tf_op jit(solution)/shard_map/ppermute | solution.py:646
  18.0 0.1 edges.6
  18.1 0.1 collective-permute-start.2
  18.2 0.1 collective-permute-start.4
  18.3 7.1 %collective-permute-done.3.arrived.chain.forward = f32[768,128]{1,0:T(8,128)S(1)} collective-permute-done((f32[768,128]{1,0:T(8,128)S(1)}, f32[768,128]{1,0:T(8,128)S(1)}, u32[]{:S(2)}, u32[]{:S(2)}) %collective-permute-start.3) | collective-permute-done | bytes 393248 | tf_op jit(solution)/shard_map/ppermute | solution.py:646
  25.3 0.7 %edges.7 = (f32[768,128]{1,0:T(8,128)S(1)}, f32[4096,128]{1,0:T(8,128)}, f32[768,128]{1,0:T(8,128)S(1)}) custom-call(s32[8,128]{1,0:T(8,128)S(1)} %get-tuple-element.41.before.flag, s32[8,128]{1,0:T(8,128)S(1)} %seen.9, f32[4096,128]{1,0:T(8,128)S(1)} %get-tuple-element.47.w_ref.w_in, ...), custom_call_target="tpu_custom_call", output_to_operand_aliasing={{1}: (14, {})} | custom-call | flops 1 | bytes 1 | tf_op jit(solution)/shard_map/edges/pallas_call | solution.py:631
  26.1 0.8 %collective-permute-start.6 = (f32[768,128]{1,0:T(8,128)S(1)}, f32[768,128]{1,0:T(8,128)S(1)}, u32[]{:S(2)}, u32[]{:S(2)}) collective-permute-start(f32[768,128]{1,0:T(8,128)S(1)} %get-tuple-element.60), channel_id=1, source_target_pairs={{0,127},{1,0},{2,1},{3,2},{4,3},{5,4},{6,5},{7,6},{8,7},{9,8},{10,... | collective-permute-start | bytes 1179656 | tf_op jit(solution)/shard_map/ppermute | solution.py:646
  26.8 3.5 %inner.3 = (f32[4096,128]{1,0:T(8,128)S(1)}, f32[4096,128]{1,0:T(8,128)S(1)}) custom-call(s32[8,128]{1,0:T(8,128)S(1)} %get-tuple-element.41.before.flag, f32[4096,128]{1,0:T(8,128)S(1)} %get-tuple-element.47.w_ref.w_in, f32[4096,128]{1,0:T(8,128)} %get-tuple-element.56.g_in, f32[768,128]{1,0:T(8,128)S(1)} %collective-permute-done.3.arrived.chain.forward, ...), custom_call_target="tpu_custom_call" | custom-call | flops 1 | bytes 1 | tf_op jit(solution)/shard_map/inner/pallas_call | solution.py:631
  30.3 1.3 %collective-permute-done.2.arrived.chain.forward = f32[768,128]{1,0:T(8,128)S(1)} collective-permute-done((f32[768,128]{1,0:T(8,128)S(1)}, f32[768,128]{1,0:T(8,128)S(1)}, u32[]{:S(2)}, u32[]{:S(2)}) %collective-permute-start.2) | collective-permute-done | bytes 393248 | tf_op jit(solution)/shard_map/ppermute | solution.py:646
  31.6 0.8 %edges.8 = (f32[768,128]{1,0:T(8,128)S(1)}, f32[4096,128]{1,0:T(8,128)}, f32[768,128]{1,0:T(8,128)S(1)}) custom-call(s32[8,128]{1,0:T(8,128)S(1)} %get-tuple-element.41.before.flag, s32[8,128]{1,0:T(8,128)S(1)} %seen.8, f32[4096,128]{1,0:T(8,128)S(1)} %get-tuple-element.57.w_ref.w_in, f32[768,128]{1,0:T(8,128)S(1)} %collective-permute-done.2.arrived.chain.forward, ...), custom_call_target="tpu_custom_call" | custom-call | flops 1 | bytes 1 | tf_op jit(solution)/shard_map/edges/pallas_call | solution.py:631
  32.4 0.1 collective-permute-start.5
  32.5 0.5 collective-permute-start.8
  33.0 0.1 edges.9
  33.1 0.9 %collective-permute-start.10 = (f32[768,128]{1,0:T(8,128)S(1)}, f32[768,128]{1,0:T(8,128)S(1)}, u32[]{:S(2)}, u32[]{:S(2)}) collective-permute-start(f32[768,128]{1,0:T(8,128)S(1)} %get-tuple-element.68), channel_id=1, source_target_pairs={{0,1},{1,2},{2,3},{3,4},{4,5},{5,6},{6,7},{7,8},{8,9},{9,10},{10,1... | collective-permute-start | bytes 1179656 | tf_op jit(solution)/shard_map/ppermute | solution.py:646
  33.9 0.1 collective-permute-start.11
  34.0 3.1 %inner.4 = (f32[4096,128]{1,0:T(8,128)S(1)}, f32[4096,128]{1,0:T(8,128)S(1)}) custom-call(s32[8,128]{1,0:T(8,128)S(1)} %get-tuple-element.41.before.flag, f32[4096,128]{1,0:T(8,128)S(1)} %get-tuple-element.57.w_ref.w_in, f32[4096,128]{1,0:T(8,128)} %get-tuple-element.64.g_in, f32[768,128]{1,0:T(8,128)S(1)} %collective-permute-done.2.arrived.chain.forward, ...), custom_call_target="tpu_custom_call" | custom-call | flops 1 | bytes 1 | tf_op jit(solution)/shard_map/inner/pallas_call | solution.py:631
  37.2 0.6 %collective-permute-done.5.arrived.chain.backward = f32[768,128]{1,0:T(8,128)S(1)} collective-permute-done((f32[768,128]{1,0:T(8,128)S(1)}, f32[768,128]{1,0:T(8,128)S(1)}, u32[]{:S(2)}, u32[]{:S(2)}) %collective-permute-start.5) | collective-permute-done | bytes 393248 | tf_op jit(solution)/shard_map/ppermute | solution.py:646
  37.8 0.1 edges.10
  37.9 1.2 %collective-permute-start.9 = (f32[768,128]{1,0:T(8,128)S(1)}, f32[768,128]{1,0:T(8,128)S(1)}, u32[]{:S(2)}, u32[]{:S(2)}) collective-permute-start(f32[768,128]{1,0:T(8,128)S(1)} %get-tuple-element.67), channel_id=1, source_target_pairs={{0,1},{1,2},{2,3},{3,4},{4,5},{5,6},{6,7},{7,8},{8,9},{9,10},{10,1... | collective-permute-start | bytes 1179656 | tf_op jit(solution)/shard_map/ppermute | solution.py:646
  39.0 6.7 %collective-permute-done.10.arrived.chain.forward = f32[768,128]{1,0:T(8,128)S(1)} collective-permute-done((f32[768,128]{1,0:T(8,128)S(1)}, f32[768,128]{1,0:T(8,128)S(1)}, u32[]{:S(2)}, u32[]{:S(2)}) %collective-permute-start.10) | collective-permute-done | bytes 393248 | tf_op jit(solution)/shard_map/ppermute | solution.py:646
  45.8 0.7 %edges.11 = (f32[768,128]{1,0:T(8,128)S(1)}, f32[4096,128]{1,0:T(8,128)}, f32[768,128]{1,0:T(8,128)S(1)}) custom-call(s32[8,128]{1,0:T(8,128)S(1)} %get-tuple-element.41.before.flag, s32[8,128]{1,0:T(8,128)S(1)} %seen.13, f32[4096,128]{1,0:T(8,128)S(1)} %get-tuple-element.65.w_ref.w_in, ...), custom_call_target="tpu_custom_call", output_to_operand_aliasing={{1}: (14, {})} | custom-call | flops 1 | bytes 1 | tf_op jit(solution)/shard_map/edges/pallas_call | solution.py:631
  46.5 0.1 collective-permute-start.12
  46.6 0.5 collective-permute-start.14
  47.1 0.1 collective-permute-start.13
  47.2 3.4 %inner.5 = (f32[4096,128]{1,0:T(8,128)S(1)}, f32[4096,128]{1,0:T(8,128)S(1)}) custom-call(s32[8,128]{1,0:T(8,128)S(1)} %get-tuple-element.41.before.flag, f32[4096,128]{1,0:T(8,128)S(1)} %get-tuple-element.65.w_ref.w_in, f32[4096,128]{1,0:T(8,128)} %get-tuple-element.72.g_in, f32[768,128]{1,0:T(8,128)S(1)} %collective-permute-done.10.arrived.chain.forward, ...), custom_call_target="tpu_custom_call" | custom-call | flops 1 | bytes 1 | tf_op jit(solution)/shard_map/inner/pallas_call | solution.py:631
  50.6 0.8 %collective-permute-done.9.arrived.forward = f32[768,128]{1,0:T(8,128)S(1)} collective-permute-done((f32[768,128]{1,0:T(8,128)S(1)}, f32[768,128]{1,0:T(8,128)S(1)}, u32[]{:S(2)}, u32[]{:S(2)}) %collective-permute-start.9) | collective-permute-done | bytes 393248 | tf_op jit(solution)/shard_map/ppermute | solution.py:646
  51.3 0.5 collective-permute-done.12.backward
  51.9 3.1 %last.1 = f32[4096,128]{1,0:T(8,128)} custom-call(s32[8,128]{1,0:T(8,128)S(1)} %get-tuple-element.41.before.flag, s32[8,128]{1,0:T(8,128)S(1)} %seen.12, s32[2,768]{1,0:T(2,128)} %send_any.19, f32[4096,128]{1,0:T(8,128)S(1)} %get-tuple-element.73.w_in, f32[768,128]{1,0:T(8,128)S(1)} %collective-permute-done.9.arrived.forward, ...), custom_call_target="tpu_custom_call" | custom-call | flops 1 | bytes 1 | tf_op jit(solution)/shard_map/last/pallas_call | solution.py:631
  (21 shorter events, 0.0 us)
Async XLA Ops:
  0.0 13.2 %copy-start.1 = (f32[4096]{0:T(1024)S(1)}, f32[4096]{0:T(1024)}, u32[]{:S(2)}) copy-start(f32[4096]{0:T(1024)} %param.9) | copy-start | bytes 49156
  4.4 13.6 %collective-permute-start = (f32[768,128]{1,0:T(8,128)S(1)}, f32[768,128]{1,0:T(8,128)S(1)}, u32[]{:S(2)}, u32[]{:S(2)}) collective-permute-start(f32[768,128]{1,0:T(8,128)S(1)} %get-tuple-element.42), channel_id=1, source_target_pairs={{0,127},{1,0},{2,1},{3,2},{4,3},{5,4},{6,5},{7,6},{8,7},{9,8},{10,... | collective-permute-start | bytes 1179656 | tf_op jit(solution)/shard_map/ppermute | solution.py:646
  12.7 5.3 %collective-permute-start.1 = (f32[768,128]{1,0:T(8,128)S(1)}, f32[768,128]{1,0:T(8,128)S(1)}, u32[]{:S(2)}, u32[]{:S(2)}) collective-permute-start(f32[768,128]{1,0:T(8,128)S(1)} %get-tuple-element.48), channel_id=1, source_target_pairs={{0,1},{1,0},{2,3},{3,2},{4,5},{5,4},{6,7},{7,6},{8,9},{9,8},{10,11... | collective-permute-start | bytes 1179656 | tf_op jit(solution)/shard_map/ppermute | solution.py:651
  12.7 12.6 %collective-permute-start.3 = (f32[768,128]{1,0:T(8,128)S(1)}, f32[768,128]{1,0:T(8,128)S(1)}, u32[]{:S(2)}, u32[]{:S(2)}) collective-permute-start(f32[768,128]{1,0:T(8,128)S(1)} %get-tuple-element.53), channel_id=1, source_target_pairs={{0,1},{1,2},{2,3},{3,4},{4,5},{5,6},{6,7},{7,8},{8,9},{9,10},{10,1... | collective-permute-start | bytes 1179656 | tf_op jit(solution)/shard_map/ppermute | solution.py:646
  13.2 4.8 %copy-start = (f32[128]{0:T(128)S(1)}, f32[128]{0:T(128)}, u32[]{:S(2)}) copy-start(f32[128]{0:T(128)} %param.10) | copy-start | bytes 1540
  18.1 13.5 %collective-permute-start.2 = (f32[768,128]{1,0:T(8,128)S(1)}, f32[768,128]{1,0:T(8,128)S(1)}, u32[]{:S(2)}, u32[]{:S(2)}) collective-permute-start(f32[768,128]{1,0:T(8,128)S(1)} %get-tuple-element.52), channel_id=1, source_target_pairs={{0,1},{1,2},{2,3},{3,4},{4,5},{5,6},{6,7},{7,8},{8,9},{9,10},{10,1... | collective-permute-start | bytes 1179656 | tf_op jit(solution)/shard_map/ppermute | solution.py:646
  18.2 13.4 %collective-permute-start.4 = (f32[768,128]{1,0:T(8,128)S(1)}, f32[768,128]{1,0:T(8,128)S(1)}, u32[]{:S(2)}, u32[]{:S(2)}) collective-permute-start(f32[768,128]{1,0:T(8,128)S(1)} %get-tuple-element.54.before), channel_id=1, source_target_pairs={{0,1},{1,0},{2,3},{3,2},{4,5},{5,4},{6,7},{7,6},{8,9},{9,8},{10,11... | collective-permute-start | bytes 1179656 | tf_op jit(solution)/shard_map/ppermute | solution.py:651
  26.1 6.9 %collective-permute-start.6 = (f32[768,128]{1,0:T(8,128)S(1)}, f32[768,128]{1,0:T(8,128)S(1)}, u32[]{:S(2)}, u32[]{:S(2)}) collective-permute-start(f32[768,128]{1,0:T(8,128)S(1)} %get-tuple-element.60), channel_id=1, source_target_pairs={{0,127},{1,0},{2,1},{3,2},{4,3},{5,4},{6,5},{7,6},{8,7},{9,8},{10,... | collective-permute-start | bytes 1179656 | tf_op jit(solution)/shard_map/ppermute | solution.py:646
  26.8 6.2 %collective-permute-start.7 = (f32[768,128]{1,0:T(8,128)S(1)}, f32[768,128]{1,0:T(8,128)S(1)}, u32[]{:S(2)}, u32[]{:S(2)}) collective-permute-start(f32[768,128]{1,0:T(8,128)S(1)} %get-tuple-element.62), channel_id=1, source_target_pairs={{0,1},{1,0},{2,3},{3,2},{4,5},{5,4},{6,7},{7,6},{8,9},{9,8},{10,11... | collective-permute-start | bytes 1179656 | tf_op jit(solution)/shard_map/ppermute | solution.py:651
  32.4 5.4 %collective-permute-start.5 = (f32[768,128]{1,0:T(8,128)S(1)}, f32[768,128]{1,0:T(8,128)S(1)}, u32[]{:S(2)}, u32[]{:S(2)}) collective-permute-start(f32[768,128]{1,0:T(8,128)S(1)} %get-tuple-element.59), channel_id=1, source_target_pairs={{0,127},{1,0},{2,1},{3,2},{4,3},{5,4},{6,5},{7,6},{8,7},{9,8},{10,... | collective-permute-start | bytes 1179656 | tf_op jit(solution)/shard_map/ppermute | solution.py:646
  32.5 5.3 %collective-permute-start.8 = (f32[768,128]{1,0:T(8,128)S(1)}, f32[768,128]{1,0:T(8,128)S(1)}, u32[]{:S(2)}, u32[]{:S(2)}) collective-permute-start(f32[768,128]{1,0:T(8,128)S(1)} %get-tuple-element.61.before), channel_id=1, source_target_pairs={{0,1},{1,0},{2,3},{3,2},{4,5},{5,4},{6,7},{7,6},{8,9},{9,8},{10,11... | collective-permute-start | bytes 1179656 | tf_op jit(solution)/shard_map/ppermute | solution.py:651
  33.1 12.7 %collective-permute-start.10 = (f32[768,128]{1,0:T(8,128)S(1)}, f32[768,128]{1,0:T(8,128)S(1)}, u32[]{:S(2)}, u32[]{:S(2)}) collective-permute-start(f32[768,128]{1,0:T(8,128)S(1)} %get-tuple-element.68), channel_id=1, source_target_pairs={{0,1},{1,2},{2,3},{3,4},{4,5},{5,6},{6,7},{7,8},{8,9},{9,10},{10,1... | collective-permute-start | bytes 1179656 | tf_op jit(solution)/shard_map/ppermute | solution.py:646
  33.9 11.8 %collective-permute-start.11 = (f32[768,128]{1,0:T(8,128)S(1)}, f32[768,128]{1,0:T(8,128)S(1)}, u32[]{:S(2)}, u32[]{:S(2)}) collective-permute-start(f32[768,128]{1,0:T(8,128)S(1)} %get-tuple-element.70), channel_id=1, source_target_pairs={{0,1},{1,0},{2,3},{3,2},{4,5},{5,4},{6,7},{7,6},{8,9},{9,8},{10,11... | collective-permute-start | bytes 1179656 | tf_op jit(solution)/shard_map/ppermute | solution.py:651
  37.9 13.5 %collective-permute-start.9 = (f32[768,128]{1,0:T(8,128)S(1)}, f32[768,128]{1,0:T(8,128)S(1)}, u32[]{:S(2)}, u32[]{:S(2)}) collective-permute-start(f32[768,128]{1,0:T(8,128)S(1)} %get-tuple-element.67), channel_id=1, source_target_pairs={{0,1},{1,2},{2,3},{3,4},{4,5},{5,6},{6,7},{7,8},{8,9},{9,10},{10,1... | collective-permute-start | bytes 1179656 | tf_op jit(solution)/shard_map/ppermute | solution.py:646
  46.5 5.4 %collective-permute-start.12 = (f32[768,128]{1,0:T(8,128)S(1)}, f32[768,128]{1,0:T(8,128)S(1)}, u32[]{:S(2)}, u32[]{:S(2)}) collective-permute-start(f32[768,128]{1,0:T(8,128)S(1)} %get-tuple-element.74), channel_id=1, source_target_pairs={{0,127},{1,0},{2,1},{3,2},{4,3},{5,4},{6,5},{7,6},{8,7},{9,8},{10,... | collective-permute-start | bytes 1179656 | tf_op jit(solution)/shard_map/ppermute | solution.py:646
  46.6 5.3 %collective-permute-start.14 = (f32[768,128]{1,0:T(8,128)S(1)}, f32[768,128]{1,0:T(8,128)S(1)}, u32[]{:S(2)}, u32[]{:S(2)}) collective-permute-start(f32[768,128]{1,0:T(8,128)S(1)} %get-tuple-element.75), channel_id=1, source_target_pairs={{0,1},{1,0},{2,3},{3,2},{4,5},{5,4},{6,7},{7,6},{8,9},{9,8},{10,11... | collective-permute-start | bytes 1179656 | tf_op jit(solution)/shard_map/ppermute | solution.py:651
  47.1 4.8 %collective-permute-start.13 = (f32[768,128]{1,0:T(8,128)S(1)}, f32[768,128]{1,0:T(8,128)S(1)}, u32[]{:S(2)}, u32[]{:S(2)}) collective-permute-start(f32[768,128]{1,0:T(8,128)S(1)} %get-tuple-element.69.before), channel_id=1, source_target_pairs={{0,1},{1,0},{2,3},{3,2},{4,5},{5,4},{6,7},{7,6},{8,9},{9,8},{10,11... | collective-permute-start | bytes 1179656 | tf_op jit(solution)/shard_map/ppermute | solution.py:651

commit v7 on v6

--- a/solution.py
+++ b/solution.py
@@ -445,7 +445,7 @@
             return tuple(tail)
 
         zero = jnp.zeros((SEGS, COLS), jnp.float32)
-        tail = lax.fori_loop(0, STEPS, body, (zero, zero), unroll=8)
+        tail = lax.fori_loop(0, STEPS, body, (zero, zero), unroll=16)
         for out, last in zip((behind_ref, ahead_ref), tail):
             out[0:SEGS, :] = out[0:SEGS, :] + pltpu.roll(last, 1, 0)
 
@@ -569,7 +569,7 @@
         for odd, left, right in ((0, forward, pair_even), (1, pair_odd, backward)):
             @pl.when(flag[1, 0] == odd)
             def _():
-                lax.fori_loop(0, STEPS, functools.partial(edges, left, right), 0, unroll=4)
+                lax.fori_loop(0, STEPS, functools.partial(edges, left, right), 0, unroll=8)
 
     load.wait()
 
@@ -585,7 +585,7 @@
                     raw[pl.ds(pl.multiple_of(e + half, 8), 8), :] = tile(u_in, e + half) - jnp.where(mine, change, 0.0)
             return carry
 
-        lax.fori_loop(0, STEPS, body, 0, unroll=4)
+        lax.fori_loop(0, STEPS, body, 0, unroll=8)
 
     @pl.when(jnp.logical_not(ok))
     def _():

time: 55.3 us -> 55.6 us (level)
  no operation moved by 1% of the time
where the time goes in v7:
time: 55.6 us; the launch traced here: 55.3 us
  Pallas kernels  23.7 us (43%)
  waiting for transfers between devices  18.2 us (33%)
  starting transfers between devices  13.1 us (24%)
    pallas_call x19, Pallas kernels, call(): pl.pallas_call(kernel, out_shape=shapes, in_specs=specs, out_specs=outs,...  23.7 us
    ppermute x8, waiting for transfers between devices, moved(): lax.ppermute(value, 'elem', [(i, (i + by) % size) for i in range(size)])  18.2 us
    ppermute x8, starting transfers between devices, moved(): lax.ppermute(value, 'elem', [(i, (i + by) % size) for i in range(size)])  11.8 us
    ppermute x7, starting transfers between devices, crossed(): lax.ppermute(value, 'elem', [(i, i + 1 - 2 * (i % 2)) for i in range(size)])  1.27 us
  transfers between devices with their start and end apart: 15, of which 7 were waited for; matrix products, arithmetic and copies ran while one was open for 0% of the time, Pallas kernels for 29%

profile of v7, /device:TPU:0, one launch (start us, length us, event | category | flops | bytes accessed | tf_op | source)
XLA Modules:
  0.0 55.3 jit_solution(1592090514455231581)
XLA Ops:
  0.0 4.4 %first.1 = (f32[4096,128]{1,0:T(8,128)S(1)}, f32[4096,128]{1,0:T(8,128)S(1)}, f32[4096,128]{1,0:T(8,128)S(1)}, f32[4096,128]{1,0:T(8,128)S(1)}, f32[256,128]{1,0...) custom-call(f32[4096,128]{1,0:T(8,128)} %prog.1, ...), custom_call_target="tpu_custom_call" | custom-call | flops 1 | bytes 1 | tf_op jit(solution)/shard_map/first/pallas_call | solution.py:631
  4.4 8.3 %collective-permute-start = (f32[768,128]{1,0:T(8,128)S(1)}, f32[768,128]{1,0:T(8,128)S(1)}, u32[]{:S(2)}, u32[]{:S(2)}) collective-permute-start(f32[768,128]{1,0:T(8,128)S(1)} %get-tuple-element.42), channel_id=1, source_target_pairs={{0,127},{1,0},{2,1},{3,2},{4,3},{5,4},{6,5},{7,6},{8,7},{9,8},{10,... | collective-permute-start | bytes 1179656 | tf_op jit(solution)/shard_map/ppermute | solution.py:646
  12.7 0.5 collective-permute-start.3
  13.2 3.5 %prepare.1 = (f32[4096,128]{1,0:T(8,128)S(1)}, f32[3072,128]{1,0:T(8,128)S(1)}, f32[4096,128]{1,0:T(8,128)S(1)}) custom-call(s32[8,128]{1,0:T(8,128)S(1)} %get-tuple-element.41.before.flag, f32[4096,128]{1,0:T(8,128)S(1)} %get-tuple-element.43.s_in, f32[4096,128]{1,0:T(8,128)S(1)} %get-tuple-element.44.mx_ref, f32[4096,128]{1,0:T(8,128)S(1)} %get-tuple-element.45.my_ref, ...), custom_call_target="tpu_custom_call" | custom-call | flops 1 | bytes 1 | tf_op jit(solution)/shard_map/prepare/pallas_call | solution.py:631
  16.7 1.3 %collective-permute-done.arrived.chain.backward = f32[768,128]{1,0:T(8,128)S(1)} collective-permute-done((f32[768,128]{1,0:T(8,128)S(1)}, f32[768,128]{1,0:T(8,128)S(1)}, u32[]{:S(2)}, u32[]{:S(2)}) %collective-permute-start) | collective-permute-done | bytes 393248 | tf_op jit(solution)/shard_map/ppermute | solution.py:646
  18.0 0.1 edges.6
  18.1 0.1 collective-permute-start.2
  18.2 0.1 collective-permute-start.4
  18.3 7.1 %collective-permute-done.3.arrived.chain.forward = f32[768,128]{1,0:T(8,128)S(1)} collective-permute-done((f32[768,128]{1,0:T(8,128)S(1)}, f32[768,128]{1,0:T(8,128)S(1)}, u32[]{:S(2)}, u32[]{:S(2)}) %collective-permute-start.3) | collective-permute-done | bytes 393248 | tf_op jit(solution)/shard_map/ppermute | solution.py:646
  25.3 0.7 %edges.7 = (f32[768,128]{1,0:T(8,128)S(1)}, f32[4096,128]{1,0:T(8,128)}, f32[768,128]{1,0:T(8,128)S(1)}) custom-call(s32[8,128]{1,0:T(8,128)S(1)} %get-tuple-element.41.before.flag, s32[8,128]{1,0:T(8,128)S(1)} %seen.9, f32[4096,128]{1,0:T(8,128)S(1)} %get-tuple-element.47.w_ref.w_in, ...), custom_call_target="tpu_custom_call", output_to_operand_aliasing={{1}: (14, {})} | custom-call | flops 1 | bytes 1 | tf_op jit(solution)/shard_map/edges/pallas_call | solution.py:631
  26.0 0.8 %collective-permute-start.6 = (f32[768,128]{1,0:T(8,128)S(1)}, f32[768,128]{1,0:T(8,128)S(1)}, u32[]{:S(2)}, u32[]{:S(2)}) collective-permute-start(f32[768,128]{1,0:T(8,128)S(1)} %get-tuple-element.60), channel_id=1, source_target_pairs={{0,127},{1,0},{2,1},{3,2},{4,3},{5,4},{6,5},{7,6},{8,7},{9,8},{10,... | collective-permute-start | bytes 1179656 | tf_op jit(solution)/shard_map/ppermute | solution.py:646
  26.8 3.5 %inner.3 = (f32[4096,128]{1,0:T(8,128)S(1)}, f32[4096,128]{1,0:T(8,128)S(1)}) custom-call(s32[8,128]{1,0:T(8,128)S(1)} %get-tuple-element.41.before.flag, f32[4096,128]{1,0:T(8,128)S(1)} %get-tuple-element.47.w_ref.w_in, f32[4096,128]{1,0:T(8,128)} %get-tuple-element.56.g_in, f32[768,128]{1,0:T(8,128)S(1)} %collective-permute-done.3.arrived.chain.forward, ...), custom_call_target="tpu_custom_call" | custom-call | flops 1 | bytes 1 | tf_op jit(solution)/shard_map/inner/pallas_call | solution.py:631
  30.3 1.3 %collective-permute-done.2.arrived.chain.forward = f32[768,128]{1,0:T(8,128)S(1)} collective-permute-done((f32[768,128]{1,0:T(8,128)S(1)}, f32[768,128]{1,0:T(8,128)S(1)}, u32[]{:S(2)}, u32[]{:S(2)}) %collective-permute-start.2) | collective-permute-done | bytes 393248 | tf_op jit(solution)/shard_map/ppermute | solution.py:646
  31.6 0.8 %edges.8 = (f32[768,128]{1,0:T(8,128)S(1)}, f32[4096,128]{1,0:T(8,128)}, f32[768,128]{1,0:T(8,128)S(1)}) custom-call(s32[8,128]{1,0:T(8,128)S(1)} %get-tuple-element.41.before.flag, s32[8,128]{1,0:T(8,128)S(1)} %seen.8, f32[4096,128]{1,0:T(8,128)S(1)} %get-tuple-element.57.w_ref.w_in, f32[768,128]{1,0:T(8,128)S(1)} %collective-permute-done.2.arrived.chain.forward, ...), custom_call_target="tpu_custom_call" | custom-call | flops 1 | bytes 1 | tf_op jit(solution)/shard_map/edges/pallas_call | solution.py:631
  32.3 0.1 collective-permute-start.5
  32.4 0.5 collective-permute-start.8
  32.9 0.1 edges.9
  33.0 0.9 %collective-permute-start.10 = (f32[768,128]{1,0:T(8,128)S(1)}, f32[768,128]{1,0:T(8,128)S(1)}, u32[]{:S(2)}, u32[]{:S(2)}) collective-permute-start(f32[768,128]{1,0:T(8,128)S(1)} %get-tuple-element.68), channel_id=1, source_target_pairs={{0,1},{1,2},{2,3},{3,4},{4,5},{5,6},{6,7},{7,8},{8,9},{9,10},{10,1... | collective-permute-start | bytes 1179656 | tf_op jit(solution)/shard_map/ppermute | solution.py:646
  33.9 0.1 collective-permute-start.11
  34.0 3.1 %inner.4 = (f32[4096,128]{1,0:T(8,128)S(1)}, f32[4096,128]{1,0:T(8,128)S(1)}) custom-call(s32[8,128]{1,0:T(8,128)S(1)} %get-tuple-element.41.before.flag, f32[4096,128]{1,0:T(8,128)S(1)} %get-tuple-element.57.w_ref.w_in, f32[4096,128]{1,0:T(8,128)} %get-tuple-element.64.g_in, f32[768,128]{1,0:T(8,128)S(1)} %collective-permute-done.2.arrived.chain.forward, ...), custom_call_target="tpu_custom_call" | custom-call | flops 1 | bytes 1 | tf_op jit(solution)/shard_map/inner/pallas_call | solution.py:631
  37.1 0.6 %collective-permute-done.5.arrived.chain.backward = f32[768,128]{1,0:T(8,128)S(1)} collective-permute-done((f32[768,128]{1,0:T(8,128)S(1)}, f32[768,128]{1,0:T(8,128)S(1)}, u32[]{:S(2)}, u32[]{:S(2)}) %collective-permute-start.5) | collective-permute-done | bytes 393248 | tf_op jit(solution)/shard_map/ppermute | solution.py:646
  37.7 0.1 edges.10
  37.8 1.2 %collective-permute-start.9 = (f32[768,128]{1,0:T(8,128)S(1)}, f32[768,128]{1,0:T(8,128)S(1)}, u32[]{:S(2)}, u32[]{:S(2)}) collective-permute-start(f32[768,128]{1,0:T(8,128)S(1)} %get-tuple-element.67), channel_id=1, source_target_pairs={{0,1},{1,2},{2,3},{3,4},{4,5},{5,6},{6,7},{7,8},{8,9},{9,10},{10,1... | collective-permute-start | bytes 1179656 | tf_op jit(solution)/shard_map/ppermute | solution.py:646
  39.0 6.7 %collective-permute-done.10.arrived.chain.forward = f32[768,128]{1,0:T(8,128)S(1)} collective-permute-done((f32[768,128]{1,0:T(8,128)S(1)}, f32[768,128]{1,0:T(8,128)S(1)}, u32[]{:S(2)}, u32[]{:S(2)}) %collective-permute-start.10) | collective-permute-done | bytes 393248 | tf_op jit(solution)/shard_map/ppermute | solution.py:646
  45.7 0.9 %edges.11 = (f32[768,128]{1,0:T(8,128)S(1)}, f32[4096,128]{1,0:T(8,128)}, f32[768,128]{1,0:T(8,128)S(1)}) custom-call(s32[8,128]{1,0:T(8,128)S(1)} %get-tuple-element.41.before.flag, s32[8,128]{1,0:T(8,128)S(1)} %seen.13, f32[4096,128]{1,0:T(8,128)S(1)} %get-tuple-element.65.w_ref.w_in, ...), custom_call_target="tpu_custom_call", output_to_operand_aliasing={{1}: (14, {})} | custom-call | flops 1 | bytes 1 | tf_op jit(solution)/shard_map/edges/pallas_call | solution.py:631
  46.6 0.1 collective-permute-start.12
  46.7 0.5 collective-permute-start.14
  47.2 0.1 collective-permute-start.13
  47.3 3.4 %inner.5 = (f32[4096,128]{1,0:T(8,128)S(1)}, f32[4096,128]{1,0:T(8,128)S(1)}) custom-call(s32[8,128]{1,0:T(8,128)S(1)} %get-tuple-element.41.before.flag, f32[4096,128]{1,0:T(8,128)S(1)} %get-tuple-element.65.w_ref.w_in, f32[4096,128]{1,0:T(8,128)} %get-tuple-element.72.g_in, f32[768,128]{1,0:T(8,128)S(1)} %collective-permute-done.10.arrived.chain.forward, ...), custom_call_target="tpu_custom_call" | custom-call | flops 1 | bytes 1 | tf_op jit(solution)/shard_map/inner/pallas_call | solution.py:631
  50.7 0.6 %collective-permute-done.9.arrived.forward = f32[768,128]{1,0:T(8,128)S(1)} collective-permute-done((f32[768,128]{1,0:T(8,128)S(1)}, f32[768,128]{1,0:T(8,128)S(1)}, u32[]{:S(2)}, u32[]{:S(2)}) %collective-permute-start.9) | collective-permute-done | bytes 393248 | tf_op jit(solution)/shard_map/ppermute | solution.py:646
  51.3 0.7 %collective-permute-done.12.backward = f32[768,128]{1,0:T(8,128)S(1)} collective-permute-done((f32[768,128]{1,0:T(8,128)S(1)}, f32[768,128]{1,0:T(8,128)S(1)}, u32[]{:S(2)}, u32[]{:S(2)}) %collective-permute-start.12) | collective-permute-done | bytes 393248 | tf_op jit(solution)/shard_map/ppermute | solution.py:646
  52.0 3.1 %last.1 = f32[4096,128]{1,0:T(8,128)} custom-call(s32[8,128]{1,0:T(8,128)S(1)} %get-tuple-element.41.before.flag, s32[8,128]{1,0:T(8,128)S(1)} %seen.12, s32[2,768]{1,0:T(2,128)} %send_any.19, f32[4096,128]{1,0:T(8,128)S(1)} %get-tuple-element.73.w_in, f32[768,128]{1,0:T(8,128)S(1)} %collective-permute-done.9.arrived.forward, ...), custom_call_target="tpu_custom_call" | custom-call | flops 1 | bytes 1 | tf_op jit(solution)/shard_map/last/pallas_call | solution.py:631
  (21 shorter events, 0.0 us)
Async XLA Ops:
  0.0 13.2 %copy-start.1 = (f32[4096]{0:T(1024)S(1)}, f32[4096]{0:T(1024)}, u32[]{:S(2)}) copy-start(f32[4096]{0:T(1024)} %param.9) | copy-start | bytes 49156
  4.4 13.6 %collective-permute-start = (f32[768,128]{1,0:T(8,128)S(1)}, f32[768,128]{1,0:T(8,128)S(1)}, u32[]{:S(2)}, u32[]{:S(2)}) collective-permute-start(f32[768,128]{1,0:T(8,128)S(1)} %get-tuple-element.42), channel_id=1, source_target_pairs={{0,127},{1,0},{2,1},{3,2},{4,3},{5,4},{6,5},{7,6},{8,7},{9,8},{10,... | collective-permute-start | bytes 1179656 | tf_op jit(solution)/shard_map/ppermute | solution.py:646
  12.7 5.3 %collective-permute-start.1 = (f32[768,128]{1,0:T(8,128)S(1)}, f32[768,128]{1,0:T(8,128)S(1)}, u32[]{:S(2)}, u32[]{:S(2)}) collective-permute-start(f32[768,128]{1,0:T(8,128)S(1)} %get-tuple-element.48), channel_id=1, source_target_pairs={{0,1},{1,0},{2,3},{3,2},{4,5},{5,4},{6,7},{7,6},{8,9},{9,8},{10,11... | collective-permute-start | bytes 1179656 | tf_op jit(solution)/shard_map/ppermute | solution.py:651
  12.7 12.6 %collective-permute-start.3 = (f32[768,128]{1,0:T(8,128)S(1)}, f32[768,128]{1,0:T(8,128)S(1)}, u32[]{:S(2)}, u32[]{:S(2)}) collective-permute-start(f32[768,128]{1,0:T(8,128)S(1)} %get-tuple-element.53), channel_id=1, source_target_pairs={{0,1},{1,2},{2,3},{3,4},{4,5},{5,6},{6,7},{7,8},{8,9},{9,10},{10,1... | collective-permute-start | bytes 1179656 | tf_op jit(solution)/shard_map/ppermute | solution.py:646
  13.2 4.8 %copy-start = (f32[128]{0:T(128)S(1)}, f32[128]{0:T(128)}, u32[]{:S(2)}) copy-start(f32[128]{0:T(128)} %param.10) | copy-start | bytes 1540
  18.1 13.5 %collective-permute-start.2 = (f32[768,128]{1,0:T(8,128)S(1)}, f32[768,128]{1,0:T(8,128)S(1)}, u32[]{:S(2)}, u32[]{:S(2)}) collective-permute-start(f32[768,128]{1,0:T(8,128)S(1)} %get-tuple-element.52), channel_id=1, source_target_pairs={{0,1},{1,2},{2,3},{3,4},{4,5},{5,6},{6,7},{7,8},{8,9},{9,10},{10,1... | collective-permute-start | bytes 1179656 | tf_op jit(solution)/shard_map/ppermute | solution.py:646
  18.2 13.4 %collective-permute-start.4 = (f32[768,128]{1,0:T(8,128)S(1)}, f32[768,128]{1,0:T(8,128)S(1)}, u32[]{:S(2)}, u32[]{:S(2)}) collective-permute-start(f32[768,128]{1,0:T(8,128)S(1)} %get-tuple-element.54.before), channel_id=1, source_target_pairs={{0,1},{1,0},{2,3},{3,2},{4,5},{5,4},{6,7},{7,6},{8,9},{9,8},{10,11... | collective-permute-start | bytes 1179656 | tf_op jit(solution)/shard_map/ppermute | solution.py:651
  26.0 6.9 %collective-permute-start.6 = (f32[768,128]{1,0:T(8,128)S(1)}, f32[768,128]{1,0:T(8,128)S(1)}, u32[]{:S(2)}, u32[]{:S(2)}) collective-permute-start(f32[768,128]{1,0:T(8,128)S(1)} %get-tuple-element.60), channel_id=1, source_target_pairs={{0,127},{1,0},{2,1},{3,2},{4,3},{5,4},{6,5},{7,6},{8,7},{9,8},{10,... | collective-permute-start | bytes 1179656 | tf_op jit(solution)/shard_map/ppermute | solution.py:646
  26.8 6.1 %collective-permute-start.7 = (f32[768,128]{1,0:T(8,128)S(1)}, f32[768,128]{1,0:T(8,128)S(1)}, u32[]{:S(2)}, u32[]{:S(2)}) collective-permute-start(f32[768,128]{1,0:T(8,128)S(1)} %get-tuple-element.62), channel_id=1, source_target_pairs={{0,1},{1,0},{2,3},{3,2},{4,5},{5,4},{6,7},{7,6},{8,9},{9,8},{10,11... | collective-permute-start | bytes 1179656 | tf_op jit(solution)/shard_map/ppermute | solution.py:651
  32.3 5.4 %collective-permute-start.5 = (f32[768,128]{1,0:T(8,128)S(1)}, f32[768,128]{1,0:T(8,128)S(1)}, u32[]{:S(2)}, u32[]{:S(2)}) collective-permute-start(f32[768,128]{1,0:T(8,128)S(1)} %get-tuple-element.59), channel_id=1, source_target_pairs={{0,127},{1,0},{2,1},{3,2},{4,3},{5,4},{6,5},{7,6},{8,7},{9,8},{10,... | collective-permute-start | bytes 1179656 | tf_op jit(solution)/shard_map/ppermute | solution.py:646
  32.4 5.3 %collective-permute-start.8 = (f32[768,128]{1,0:T(8,128)S(1)}, f32[768,128]{1,0:T(8,128)S(1)}, u32[]{:S(2)}, u32[]{:S(2)}) collective-permute-start(f32[768,128]{1,0:T(8,128)S(1)} %get-tuple-element.61.before), channel_id=1, source_target_pairs={{0,1},{1,0},{2,3},{3,2},{4,5},{5,4},{6,7},{7,6},{8,9},{9,8},{10,11... | collective-permute-start | bytes 1179656 | tf_op jit(solution)/shard_map/ppermute | solution.py:651
  33.0 12.7 %collective-permute-start.10 = (f32[768,128]{1,0:T(8,128)S(1)}, f32[768,128]{1,0:T(8,128)S(1)}, u32[]{:S(2)}, u32[]{:S(2)}) collective-permute-start(f32[768,128]{1,0:T(8,128)S(1)} %get-tuple-element.68), channel_id=1, source_target_pairs={{0,1},{1,2},{2,3},{3,4},{4,5},{5,6},{6,7},{7,8},{8,9},{9,10},{10,1... | collective-permute-start | bytes 1179656 | tf_op jit(solution)/shard_map/ppermute | solution.py:646
  33.9 11.9 %collective-permute-start.11 = (f32[768,128]{1,0:T(8,128)S(1)}, f32[768,128]{1,0:T(8,128)S(1)}, u32[]{:S(2)}, u32[]{:S(2)}) collective-permute-start(f32[768,128]{1,0:T(8,128)S(1)} %get-tuple-element.70), channel_id=1, source_target_pairs={{0,1},{1,0},{2,3},{3,2},{4,5},{5,4},{6,7},{7,6},{8,9},{9,8},{10,11... | collective-permute-start | bytes 1179656 | tf_op jit(solution)/shard_map/ppermute | solution.py:651
  37.8 13.5 %collective-permute-start.9 = (f32[768,128]{1,0:T(8,128)S(1)}, f32[768,128]{1,0:T(8,128)S(1)}, u32[]{:S(2)}, u32[]{:S(2)}) collective-permute-start(f32[768,128]{1,0:T(8,128)S(1)} %get-tuple-element.67), channel_id=1, source_target_pairs={{0,1},{1,2},{2,3},{3,4},{4,5},{5,6},{6,7},{7,8},{8,9},{9,10},{10,1... | collective-permute-start | bytes 1179656 | tf_op jit(solution)/shard_map/ppermute | solution.py:646
  46.6 5.4 %collective-permute-start.12 = (f32[768,128]{1,0:T(8,128)S(1)}, f32[768,128]{1,0:T(8,128)S(1)}, u32[]{:S(2)}, u32[]{:S(2)}) collective-permute-start(f32[768,128]{1,0:T(8,128)S(1)} %get-tuple-element.74), channel_id=1, source_target_pairs={{0,127},{1,0},{2,1},{3,2},{4,3},{5,4},{6,5},{7,6},{8,7},{9,8},{10,... | collective-permute-start | bytes 1179656 | tf_op jit(solution)/shard_map/ppermute | solution.py:646
  46.7 5.3 %collective-permute-start.14 = (f32[768,128]{1,0:T(8,128)S(1)}, f32[768,128]{1,0:T(8,128)S(1)}, u32[]{:S(2)}, u32[]{:S(2)}) collective-permute-start(f32[768,128]{1,0:T(8,128)S(1)} %get-tuple-element.75), channel_id=1, source_target_pairs={{0,1},{1,0},{2,3},{3,2},{4,5},{5,4},{6,7},{7,6},{8,9},{9,8},{10,11... | collective-permute-start | bytes 1179656 | tf_op jit(solution)/shard_map/ppermute | solution.py:651
  47.2 4.8 %collective-permute-start.13 = (f32[768,128]{1,0:T(8,128)S(1)}, f32[768,128]{1,0:T(8,128)S(1)}, u32[]{:S(2)}, u32[]{:S(2)}) collective-permute-start(f32[768,128]{1,0:T(8,128)S(1)} %get-tuple-element.69.before), channel_id=1, source_target_pairs={{0,1},{1,0},{2,3},{3,2},{4,5},{5,4},{6,7},{7,6},{8,9},{9,8},{10,11... | collective-permute-start | bytes 1179656 | tf_op jit(solution)/shard_map/ppermute | solution.py:651
